TPU v7x, 32 devices: a whole 2x2x4 slice. The times are simulated.
32 devices in a mesh: ctx: 16 (over z, y, x), fsdp: 2 (over core).
Axes of the slice: x: 2, y: 2, z: 4, core: 2. Of those that a mesh axis runs over, the one named last changes fastest.
Arguments:
- tokens: bfloat16 [2, 2048, 4096], P('fsdp', 'ctx'), may hold values from -6 to 6
- queries: bfloat16 [2, 2048, 512], P('fsdp', 'ctx'), may hold values from -6 to 6
- flags: int32 [2, 2048], P('fsdp', 'ctx'), may hold values from 0 to 1, as said below
- w_key: bfloat16 [4096, 512], P(('ctx', 'fsdp')), may hold values from -0.09375 to 0.09375
- w_value: bfloat16 [4096, 512], P(('ctx', 'fsdp')), may hold values from -0.09375 to 0.09375
- norm_gain: float32 [512], replicated, may hold values from 0.25 to 1.75
Outputs:
- attended: bfloat16 [2, 2048, 512], P('fsdp', 'ctx')
Inputs may be any that keep to these rules, and one draw needn't show every extreme that they name: `flags`: in each sequence a document starts at token 0 and at every token k * 1024 + 1024 // 2; other tokens start one at random, never before token 1536 and never at the first token of a block. No document is longer than 1024 tokens.
All inputs are finite; a program needn't handle non-finite values.
Results may differ from a plain program's by a relative error of at most 0.0053.
Values may be sent and summed in bfloat16 or wider, within the bound.
No kernel may reach another device: no remote copies, remote signals or barrier semaphores. Data moves between devices by JAX's collectives and lax.ppermute only.
A program may use at most 64 MiB of HBM per device.

v0:
```python
import jax
import jax.numpy as jnp
from jax import lax
from jax.sharding import PartitionSpec as P

HEAD = 128


def entering(array, axis, join, neutral):
    place = lax.axis_index(axis)
    gathered = jax.tree.map(
        lambda a, kind: lax.all_gather(a.astype(kind), axis), array, (jnp.bfloat16, jnp.bfloat16)
    )
    state = jax.tree.map(lambda a, e: jnp.zeros_like(a) + jnp.asarray(e, a.dtype), array, neutral)

    def one(lap, state):
        return join(
            state,
            jax.tree.map(
                lambda a, own: lax.dynamic_index_in_dim(a, lap, 0, False).astype(own.dtype),
                gathered,
                array,
            ),
        )

    return lax.fori_loop(0, place, one, state)


def feature(u):
    return jax.nn.elu(u) + 1.0


def combine(earlier, later):
    keep = 1.0 - later[0][0]
    return (jnp.maximum(earlier[0], later[0]), later[1] + keep * earlier[1])


def on_device(tokens, queries, flags, w_key, w_value, norm_gain):
    rows = tokens[0]
    count = rows.shape[0]
    width = w_key.shape[1]
    heads = width // HEAD
    full_panels = (
        lax.all_gather(w_key, ("ctx", "fsdp"), axis=0, tiled=True),
        lax.all_gather(w_value, ("ctx", "fsdp"), axis=0, tiled=True),
    )
    proj_key = jnp.dot(rows, full_panels[0], preferred_element_type=jnp.float32)
    proj_value = jnp.dot(rows, full_panels[1], preferred_element_type=jnp.float32)
    key = feature(proj_key).astype(jnp.bfloat16).reshape(count, heads, HEAD)
    value = proj_value.astype(jnp.bfloat16).reshape(count, heads, HEAD)
    query = feature(queries[0].astype(jnp.float32)).astype(jnp.bfloat16).reshape(count, heads, HEAD)
    seg = jnp.cumsum(flags[0])
    last = seg[count - 1]
    reset = (last > 0).astype(jnp.float32).reshape(1)
    tail = (seg == last).astype(jnp.bfloat16)
    local_state = jnp.einsum(
        "the,thf->hef", key * tail[:, None, None], value, preferred_element_type=jnp.float32
    )
    identity = (jnp.zeros((1,), jnp.float32), jnp.zeros_like(local_state))
    carried = entering((reset, local_state), "ctx", combine, identity)
    carried_b = carried[1].astype(jnp.bfloat16)
    places = jnp.arange(count, dtype=jnp.int32)
    allowed = (places[None, :] <= places[:, None]) & (seg[None, :] == seg[:, None])
    scores = jnp.einsum("the,she->hts", query, key, preferred_element_type=jnp.float32)
    scores = jnp.where(allowed[None, :, :], scores, 0.0).astype(jnp.bfloat16)
    inside = jnp.einsum("hts,shf->thf", scores, value, preferred_element_type=jnp.float32)
    first = (seg == 0).astype(jnp.float32)
    carried_term = (
        jnp.einsum("the,hef->thf", query, carried_b, preferred_element_type=jnp.float32)
        * first[:, None, None]
    )
    mixed = carried_term + inside
    scale = lax.rsqrt(jnp.mean(mixed * mixed, axis=-1, keepdims=True) + 1e-06)
    attended = (mixed * scale * norm_gain.reshape(heads, HEAD)).astype(jnp.bfloat16)
    return attended.reshape(1, count, width)


def solution(mesh):
    in_specs = (
        P("fsdp", "ctx", None),
        P("fsdp", "ctx", None),
        P("fsdp", "ctx"),
        P(("ctx", "fsdp"), None),
        P(("ctx", "fsdp"), None),
        P(),
    )
    out_specs = P("fsdp", "ctx", None)
    return jax.shard_map(
        on_device, mesh=mesh, in_specs=in_specs, out_specs=out_specs, check_vma=False
    )
```

profile of v0, /device:TPU:30, one launch (start us, length us, event | category | flops | bytes accessed | tf_op | source)
XLA Modules:
  0.0 239.8 jit_solution(15691701118312775918)
XLA Ops:
  6.5 0.0 all-gather.5.cloned.1.call-start
  6.5 0.7 all-gather.5.cloned.1.call-update
  7.3 0.0 all-gather.7.cloned.1.call-start
  7.3 0.7 all-gather.7.cloned.1.call-update
  8.0 0.0 all-gather.9.cloned.1.call-start
  8.1 0.8 copy.25
  8.8 0.2 broadcast_in_dim.30
  9.0 0.6 slice.5
  9.6 0.1 reduce
  9.7 0.7 compare_convert_fusion.1
  10.4 60.5 %all-gather.5.cloned.1.call-done = bf16[4096,512]{1,0:T(8,128)(2,1)} async-done(((bf16[128,512]{1,0:T(8,128)(2,1)}), bf16[4096,512]{1,0:T(8,128)(2,1)}) %all-gather.5.cloned.1.call-update) | async-done | bytes 4194320 | tf_op jit(solution)/shard_map/all_gather | solution.py:44
  70.8 0.0 copy-done
  70.8 3.0 %fusion.11 = bf16[128,512]{1,0:T(8,128)(2,1)S(1)} fusion(bf16[4096,512]{1,0:T(8,128)(2,1)} %all-gather.5.cloned.1.call-done, bf16[1,128,4096]{2,1,0:T(8,128)(2,1)S(1)} %copy-done), kind=kOutput, calls=%fused_computation.18 | convolution fusion | flops 537198592 | bytes 5373952 | tf_op jit(solution)/shard_map/dot_general | solution.py:47
  73.8 0.0 copy-start.3
  73.8 0.0 copy-start.1
  73.9 0.1 copy.36
  74.0 60.3 %all-gather.7.cloned.1.call-done = bf16[4096,512]{1,0:T(8,128)(2,1)} async-done(((bf16[128,512]{1,0:T(8,128)(2,1)}), bf16[4096,512]{1,0:T(8,128)(2,1)}) %all-gather.7.cloned.1.call-update) | async-done | bytes 4194320 | tf_op jit(solution)/shard_map/all_gather | solution.py:45
  134.3 2.9 %convolution_convert_fusion = bf16[128,512]{1,0:T(8,128)(2,1)S(1)} fusion(bf16[4096,512]{1,0:T(8,128)(2,1)} %all-gather.7.cloned.1.call-done, bf16[1,128,4096]{2,1,0:T(8,128)(2,1)S(1)} %copy-done), kind=kOutput, calls=%fused_computation.7 | convolution fusion | flops 536936448 | bytes 5373952 | tf_op jit(solution)/shard_map/dot_general | solution.py:48
  137.2 0.0 copy-start.2
  137.2 0.1 copy.37
  137.4 0.9 convolution_convert_fusion.1
  138.2 0.0 all-gather.9.cloned.1.call-update
  139.0 0.6 dynamic-slice
  139.5 0.7 dynamic-update-slice
  140.2 36.5 %all-reduce = bf16[16]{0:T(256)(128)(2,1)S(1)} all-reduce(bf16[16]{0:T(256)(128)(2,1)S(1)} %dynamic-update-slice), channel_id=1, replica_groups=mesh['ctx'=16,'fsdp'=2] {'ctx'}, use_global_device_ids=true, to_apply=%add | all-reduce | flops 16 | bytes 64
  176.7 0.0 copy-done.1
  176.7 0.1 reshape.107
  176.8 0.1 fusion.22
  176.8 21.1 %all-gather.9.cloned.1.call-done = bf16[64,128,128]{2,1,0:T(8,128)(2,1)} async-done(((bf16[4,128,128]{2,1,0:T(8,128)(2,1)}), bf16[64,128,128]{2,1,0:T(8,128)(2,1)}) %all-gather.9.cloned.1.call-update) | async-done | bytes 2097168 | tf_op jit(solution)/shard_map/all_gather | solution.py:12
  197.9 33.8 %while.12 = (s32[]{:T(128)}, f32[4,128,128]{2,1,0:T(8,128)S(1)}, s32[]{:T(128)}, bf16[16,4,128,128]{3,2,1,0:T(8,128)(2,1)}, bf16[16,1]{0,1:T(2,128)(2,1)S(1)}, /*index=5*/s32[]{:T(128)}, s32[]{:T(128)}, s32[]{:T(128)}) while((s32[]{:T(128)}, f32[4,128,128]{2,1,0:T(8,128)S(1)}, s32[]{:T(128)}, bf16[16,4,128,128]{3,2,1,0:T(8,128)(2,1)}, ...), condition=%wide.region_2.3_spmd, body=%wide.region_1.2_spmd.sunk | while | flops 196614 | bytes 655505 | solution.py:26
  198.0 0.6 fusion.36
  198.6 1.6 convert_add_fusion.2
  200.2 0.6 fusion.36
  200.8 1.6 convert_add_fusion.2
  202.5 0.6 fusion.36
  203.1 1.6 convert_add_fusion.2
  204.7 0.6 fusion.36
  205.3 1.6 convert_add_fusion.2
  207.0 0.6 fusion.36
  207.6 1.6 convert_add_fusion.2
  209.2 0.6 fusion.36
  209.8 1.6 convert_add_fusion.2
  211.5 0.6 fusion.36
  212.1 1.6 convert_add_fusion.2
  213.7 0.6 fusion.36
  214.3 1.6 convert_add_fusion.2
  216.0 0.6 fusion.36
  216.6 1.6 convert_add_fusion.2
  218.2 0.6 fusion.36
  218.8 1.6 convert_add_fusion.2
  220.5 0.6 fusion.36
  221.1 1.6 convert_add_fusion.2
  222.7 0.6 fusion.36
  223.3 1.6 convert_add_fusion.2
  225.0 0.6 fusion.36
  225.6 1.6 convert_add_fusion.2
  227.2 0.6 fusion.36
  227.8 1.6 convert_add_fusion.2
  229.5 0.6 fusion.36
  230.1 1.6 convert_add_fusion.2
  231.7 0.3 convolution_multiply_fusion
  232.0 0.4 multiply_reduce_fusion
  232.4 0.1 multiply_convert_fusion
  232.5 0.8 copy.34
  (6 shorter events, 0.0 us)
Async XLA Ops:
  6.5 64.3 %copy-start = (bf16[1,128,4096]{2,1,0:T(8,128)(2,1)S(1)}, bf16[1,128,4096]{2,1,0:T(8,128)(2,1)}, u32[]{:S(2)}) copy-start(bf16[1,128,4096]{2,1,0:T(8,128)(2,1)} %param.8) | copy-start | bytes 3145732
  6.5 64.3 %all-gather.5.cloned.1.call-start = ((), (), s32[]{:S(2)}) async-start(), calls=%async_computation | async-start | bytes 4325376 | tf_op jit(solution)/shard_map/all_gather | solution.py:44
  7.3 127.1 %all-gather.7.cloned.1.call-start = ((), (), s32[]{:S(2)}) async-start(), calls=%async_computation.1 | async-start | bytes 4325376 | tf_op jit(solution)/shard_map/all_gather | solution.py:45
  8.0 189.9 %all-gather.9.cloned.1.call-start = ((), (), s32[]{:S(2)}) async-start(), calls=%async_computation.2 | async-start | bytes 2228224 | tf_op jit(solution)/shard_map/all_gather | solution.py:12
  73.8 65.1 %copy-start.3 = (u32[32]{0:T(128)S(1)}, u32[32]{0:T(128)}, u32[]{:S(2)}) copy-start(u32[32]{0:T(128)} %constant.54) | copy-start | bytes 388
  73.8 102.8 %copy-start.1 = (bf16[1,128,512]{2,1,0:T(8,128)(2,1)S(1)}, bf16[1,128,512]{2,1,0:T(8,128)(2,1)}, u32[]{:S(2)}) copy-start(bf16[1,128,512]{2,1,0:T(8,128)(2,1)} %param.9) | copy-start | bytes 393220
  137.2 95.2 %copy-start.2 = (f32[512]{0:T(512)S(1)}, f32[512]{0:T(512)}, u32[]{:S(2)}) copy-start(f32[512]{0:T(512)} %param.13) | copy-start | bytes 6148
Sparse Core Ops, SparseCore 0:
  10.2 60.5 all-gather.4
  73.7 60.5 all-gather.6
  138.4 59.5 all-gather.8
where the time goes:
time: 240 us
  waiting for transfers between devices  143 us (60%)
  blocking collectives  36.5 us (15%)
  other arithmetic  34.6 us (14%)
  between operations  13.9 us (6%)
  matrix products  7.42 us (3%)
  local copies, waits for them, and re-layouts  3.73 us (2%)
    all_gather x1, waiting for transfers between devices, on_device(): lax.all_gather(w_key, ('ctx', 'fsdp'), axis=0, tiled=True)  60.5 us
    all_gather x1, waiting for transfers between devices, on_device(): lax.all_gather(w_value, ('ctx', 'fsdp'), axis=0, tiled=True)  60.3 us
    unnamed x1, blocking collectives  36.5 us
    add x15, other arithmetic, combine(): return (jnp.maximum(earlier[0], later[0]), later[1] + keep * earlier[1])  24.7 us
    all_gather x1, waiting for transfers between devices, entering(): lax.all_gather(a.astype(kind), axis)  21.1 us
    sub x15, other arithmetic, combine(): keep = 1.0 - later[0][0]  8.79 us
  transfers between devices with their start and end apart: 3, of which 3 were waited for; matrix products, arithmetic and copies ran while one was open for 3% of the time, Pallas kernels for 0%

commit v1 on v0

v1 whole, which is shorter than its diff:
```python
import functools

import jax
import jax.numpy as jnp
from jax import lax
from jax.experimental import pallas as pl
from jax.experimental.pallas import tpu as pltpu
from jax.sharding import PartitionSpec as P

HEAD = 128
BF, F32 = jnp.bfloat16, jnp.float32
DOC_BLOCKS = {16: 8, 64: 16}


def phi(u):
    return jnp.where(u > 0, u + 1.0, jnp.exp(jnp.minimum(u, 0.0)))


def aligned(index, size):
    return pl.ds(pl.multiple_of(index * size, size), size)


def inner_outer(heads):
    me = lax.axis_index("ctx")
    return lax.rem(me, heads), lax.div(me, heads)


def pack_kernel(heads, tok_ref, query_ref, flag_ref, *out_refs):
    inner, _ = inner_outer(heads)
    count, depth = tok_ref.shape
    outer = depth // (heads * 2 * HEAD)
    marks = jnp.broadcast_to(flag_ref[...].astype(F32), (count, count)).astype(BF)
    for k, out in enumerate(out_refs):
        to = jnp.bitwise_xor(inner, k)
        for o in range(outer):
            out[:, o * 256 : (o + 1) * 256] = tok_ref[:, aligned(o * heads + to, 256)]
        cols = outer * 256
        out[:, cols : cols + HEAD] = phi(query_ref[:, aligned(to, HEAD)].astype(F32)).astype(BF)
        out[:, cols + HEAD :] = marks


def pack(tokens, queries, flags, heads, fsdp, rows):
    count, depth = tokens.shape
    share = fsdp * rows
    if share == 2 * HEAD:
        wide = depth // heads + 2 * HEAD
        return pl.pallas_call(
            functools.partial(pack_kernel, heads),
            out_shape=[jax.ShapeDtypeStruct((count, wide), BF)] * heads,
            name="pack",
        )(tokens, queries, flags)
    inner, _ = inner_outer(heads)
    by_inner = tokens.reshape(count, -1, heads, share).transpose(2, 0, 1, 3).reshape(heads, count, -1)
    query = phi(queries.astype(F32)).astype(BF).reshape(count, heads, HEAD).transpose(1, 0, 2)
    marks = jnp.broadcast_to(flags.astype(BF), (count, count))
    out = []
    for k in range(heads):
        to = jnp.bitwise_xor(inner, k)
        parts = [lax.dynamic_index_in_dim(a, to, 0, False) for a in (by_inner, query)]
        out.append(jnp.concatenate(parts + [marks], axis=1))
    return out


def product_kernel(heads, split, *refs):
    x_refs, w_refs = refs[:heads], refs[heads : -heads - 1]
    out_refs, tok = refs[-heads - 1 : -1], refs[-1]
    inner, outer = inner_outer(heads)
    count = x_refs[0].shape[0]
    for k, x in enumerate(x_refs):
        rows = aligned(jnp.bitwise_xor(inner, k), count)
        if split:
            core = lax.axis_index("fsdp")
            for i in range(len(w_refs)):
                at = jnp.bitwise_xor(outer, i // 2) * 2 + jnp.bitwise_xor(core, i % 2)
                tok[rows, i * HEAD : (i + 1) * HEAD] = x[:, aligned(at, HEAD)]
        else:
            tok[rows, :] = x[:, : tok.shape[1]]
    for k, out in list(enumerate(out_refs))[1:] + [(0, out_refs[0])]:
        cols = aligned(jnp.bitwise_xor(inner, k), 2 * HEAD)
        w = jnp.concatenate([w[:, cols] for w in w_refs], axis=0)
        out[...] = jnp.dot(tok[...], w, preferred_element_type=F32).astype(out.dtype)


def product(xs, ws, heads, split):
    count = xs[0].shape[0]
    depth = sum(w.shape[0] for w in ws)
    shape = (heads * count, 2 * HEAD)
    return pl.pallas_call(
        functools.partial(product_kernel, heads, split),
        out_shape=[jax.ShapeDtypeStruct(shape, F32)] + [jax.ShapeDtypeStruct(shape, BF)] * (heads - 1),
        scratch_shapes=[pltpu.VMEM((heads * count, depth), BF)],
        compiler_params=pltpu.CompilerParams(vmem_limit_bytes=40 * 2**20),
        name="product",
    )(*xs, *ws)


def inside_kernel(heads, *refs):
    parts, extras = refs[:heads], refs[heads : 2 * heads]
    state_ref, keep_ref, first_ref, inside_ref, query, marks = refs[2 * heads :]
    inner, _ = inner_outer(heads)
    count = extras[0].shape[0]
    total = heads * count
    for k, extra in enumerate(extras):
        at = jnp.bitwise_xor(inner, k)
        query[aligned(at, count), :] = extra[:, :HEAD]
        marks[:, aligned(at, count)] = extra[:, HEAD:]
    proj = parts[0][...]
    for part in parts[1:]:
        proj = proj + part[...].astype(F32)
    key = phi(proj[:, :HEAD]).astype(BF)
    value = proj[:, HEAD:].astype(BF)
    early = lax.broadcasted_iota(jnp.int32, (total, total), 0)
    late = lax.broadcasted_iota(jnp.int32, (total, total), 1)
    upto = jnp.where(early <= late, 1.0, 0.0).astype(BF)
    seg = jnp.dot(marks[...], upto, preferred_element_type=F32)
    seg_col = seg.T
    last = jnp.broadcast_to(seg_col[total - 1 :, :], (total, HEAD))
    tail = jnp.where(seg_col == last, value.astype(F32), 0.0).astype(BF)
    state_ref[...] = lax.dot_general(key, tail, (((0,), (0,)), ((), ())), preferred_element_type=F32)
    keep_ref[...] = jnp.where(last[:HEAD, :] == 0.0, 1.0, 0.0)
    first_ref[...] = jnp.where(seg_col == 0.0, query[...].astype(F32), 0.0).astype(BF)
    for i in range(heads):
        rows, width = slice(i * count, (i + 1) * count), (i + 1) * count
        scores = lax.dot_general(
            query[rows, :], key[:width, :], (((1,), (1,)), ((), ())), preferred_element_type=F32
        )
        own = jnp.concatenate([seg_col[rows, :]] * (i + 1), axis=1)
        allowed = (own == seg[:, :width]) & (late[:count, :width] <= early[rows, :width])
        scores = jnp.where(allowed, scores, 0.0).astype(BF)
        inside_ref[rows, :] = jnp.dot(scores, value[:width, :], preferred_element_type=F32)


def inside(parts, packed, heads):
    count, wide = packed[0].shape
    total = heads * count
    whole = pl.BlockSpec((total, 2 * HEAD), lambda i: (0, 0))
    extra = pl.BlockSpec((count, 2 * HEAD), lambda i: (0, wide // (2 * HEAD) - 1))
    square = jax.ShapeDtypeStruct((HEAD, HEAD), F32)
    return pl.pallas_call(
        functools.partial(inside_kernel, heads),
        grid=(1,),
        in_specs=[whole] * heads + [extra] * heads,
        out_shape=[
            square,
            square,
            jax.ShapeDtypeStruct((total, HEAD), BF),
            jax.ShapeDtypeStruct((total, HEAD), F32),
        ],
        out_specs=[
            pl.BlockSpec((HEAD, HEAD), lambda i: (0, 0)),
            pl.BlockSpec((HEAD, HEAD), lambda i: (0, 0)),
            pl.BlockSpec((total, HEAD), lambda i: (0, 0)),
            pl.BlockSpec((total, HEAD), lambda i: (0, 0)),
        ],
        scratch_shapes=[pltpu.VMEM((total, HEAD), BF), pltpu.VMEM((count, total), BF)],
        compiler_params=pltpu.CompilerParams(vmem_limit_bytes=40 * 2**20),
        name="inside",
    )(*parts, *packed)


def finish_kernel(heads, carried_ref, first_ref, inside_ref, gain_ref, *refs):
    out_refs, done = refs[:-1], refs[-1]
    inner, _ = inner_outer(heads)
    count = out_refs[0].shape[0]
    mixed = inside_ref[...] + jnp.dot(first_ref[...], carried_ref[...], preferred_element_type=F32)
    scale = lax.rsqrt(jnp.mean(mixed * mixed, axis=-1, keepdims=True) + 1e-06)
    done[...] = (mixed * scale * gain_ref[:, aligned(inner, HEAD)]).astype(BF)
    for k, out in enumerate(out_refs):
        out[...] = done[aligned(jnp.bitwise_xor(inner, k), count), :]


def finish(carried, first, within, gain, heads):
    total = first.shape[0]
    return pl.pallas_call(
        functools.partial(finish_kernel, heads),
        out_shape=[jax.ShapeDtypeStruct((total // heads, HEAD), BF)] * heads,
        scratch_shapes=[pltpu.VMEM((total, HEAD), BF)],
        name="finish",
    )(carried, first, within, gain)


def join_kernel(heads, *refs):
    inner, _ = inner_outer(heads)
    for k, part in enumerate(refs[:-1]):
        refs[-1][:, aligned(jnp.bitwise_xor(inner, k), HEAD)] = part[...]


def join(parts, heads):
    count = parts[0].shape[0]
    return pl.pallas_call(
        functools.partial(join_kernel, heads),
        out_shape=jax.ShapeDtypeStruct((count, heads * HEAD), BF),
        name="join",
    )(*parts)


def on_device(n_ctx, fsdp, tokens, queries, flags, w_key, w_value, norm_gain):
    rows, width = w_key.shape
    heads = width // HEAD
    outer = n_ctx // heads

    def swap(a, mask):
        return lax.ppermute(a, "ctx", [(i, i ^ mask) for i in range(n_ctx)])

    by_head = [w.reshape(rows, heads, HEAD) for w in (w_key, w_value)]
    weights = jnp.concatenate(by_head, axis=2).reshape(rows, 2 * width)
    packed = pack(tokens[0], queries[0], flags, heads, fsdp, rows)
    split = outer == 4 and fsdp == 2 and rows == HEAD
    if split:
        far = swap(weights, 3 * heads)
        near = swap(weights, heads)
        received = [packed[0]] + [swap(packed[k], k) for k in range(1, heads)]
        pieces = [weights, near, swap(far, heads), far]
        panels = []
        for piece in pieces:
            panels += [piece, lax.ppermute(piece, "fsdp", [(0, 1), (1, 0)])]
    else:
        received = [packed[0]] + [swap(packed[k], k) for k in range(1, heads)]
        groups = [[o * heads + q for o in range(outer)] for q in range(heads)]
        chip = lax.all_gather(weights, "fsdp", axis=0, tiled=True)
        panels = [lax.all_gather(chip, "ctx", axis=0, tiled=True, axis_index_groups=groups)]
    partial = product(received, panels, heads, split)
    parts = [partial[0]] + [swap(partial[k], k) for k in range(1, heads)]
    state, keep, first, within = inside(parts, received, heads)

    doc = DOC_BLOCKS.get(n_ctx, 2 * n_ctx)
    starts = [b for b in range(n_ctx) if b % doc == doc // 2]
    pairs = [
        (b, b + heads)
        for b in range(n_ctx - heads)
        if (b // heads + 1) * heads not in starts
    ]
    rounds = max(1, min(doc // heads, outer) - 1)
    carried = lax.ppermute(state.astype(BF), "ctx", pairs)
    for _ in range(rounds - 1):
        carried = lax.ppermute((state + keep * carried.astype(F32)).astype(BF), "ctx", pairs)
    done = finish(carried, first, within, norm_gain.reshape(1, width), heads)
    mine = [done[0]] + [swap(done[k], k) for k in range(1, heads)]
    return join(mine, heads)[None]


def solution(mesh):
    n_ctx, fsdp = mesh.shape["ctx"], mesh.shape["fsdp"]
    in_specs = (
        P("fsdp", "ctx", None),
        P("fsdp", "ctx", None),
        P("fsdp", "ctx"),
        P(("ctx", "fsdp"), None),
        P(("ctx", "fsdp"), None),
        P(),
    )
    return jax.shard_map(
        functools.partial(on_device, n_ctx, fsdp),
        mesh=mesh,
        in_specs=in_specs,
        out_specs=P("fsdp", "ctx", None),
        check_vma=False,
    )
```

time: 240 us -> 67.5 us (0.28)
  the two profiles are of different devices: /device:TPU:30 before, /device:TPU:16 now
where the time goes in v1:
time: 67.5 us; the launch traced here: 67.2 us
  waiting for transfers between devices  38.6 us (57%)
  starting transfers between devices  15.1 us (22%)
  Pallas kernels  8.61 us (13%)
  local copies, waits for them, and re-layouts  4.6 us (7%)
    ppermute x12, waiting for transfers between devices, swap(): return lax.ppermute(a, 'ctx', [(i, i ^ mask) for i in range(n_ctx)])  34.1 us
    ppermute x12, starting transfers between devices, swap(): return lax.ppermute(a, 'ctx', [(i, i ^ mask) for i in range(n_ctx)])  13.4 us
    ppermute x1, waiting for transfers between devices, on_device(): carried = lax.ppermute(state.astype(BF), 'ctx', pairs)  4.51 us
    unnamed x17, local copies, waits for them, and re-layouts  3.59 us
    pallas_call x1, Pallas kernels, pack(): pl.pallas_call(functools.partial(pack_kernel, heads), out_shape=[jax.Shap...  2.56 us
    pallas_call x1, Pallas kernels, finish(): pl.pallas_call(functools.partial(finish_kernel, heads), out_shape=[jax.Sh...  2 us
    pallas_call x1, Pallas kernels, product(): pl.pallas_call(functools.partial(product_kernel, heads, split), out_shape...  1.51 us
    pallas_call x1, Pallas kernels, join(): pl.pallas_call(functools.partial(join_kernel, heads), out_shape=jax.Shape...  1.49 us
  transfers between devices with their start and end apart: 17, of which 10 were waited for; matrix products, arithmetic and copies ran while one was open for 0% of the time, Pallas kernels for 4%

profile of v1, /device:TPU:16, one launch (start us, length us, event | category | flops | bytes accessed | tf_op | source)
XLA Modules:
  0.0 67.2 jit_solution(9626602516600835283)
XLA Ops:
  0.0 0.0 copy-start.3
  0.0 1.0 %reshape.12 = bf16[128,4,128]{2,1,0:T(4,128)(2,1)S(1)} reshape(bf16[128,512]{1,0:T(8,128)(2,1)} %param.9) | data formatting | bytes 262144 | tf_op jit(solution)/shard_map/reshape | solution.py:205
  1.0 0.0 copy-done.3
  1.0 0.1 pad_maximum_fusion
  1.2 0.5 collective-permute-start.6
  1.7 1.2 %collective-permute-start.4 = (bf16[128,1024]{1,0:T(8,128)(2,1)S(1)}, bf16[128,1024]{1,0:T(8,128)(2,1)S(1)}, u32[]{:S(2)}, u32[]{:S(2)}) collective-permute-start(bf16[128,1024]{1,0:T(8,128)(2,1)S(1)} %bitcast.7), channel_id=1, source_target_pairs={{0,8},{2,10},{4,12},{6,14},{8,0},{10,2},{12,4},{14,6},{16,24},{18,... | collective-permute-start | bytes 786440 | tf_op jit(solution)/shard_map/ppermute | solution.py:203
  2.9 2.6 %pack.1 = (bf16[128,1280]{1,0:T(8,128)(2,1)}, bf16[128,1280]{1,0:T(8,128)(2,1)}, bf16[128,1280]{1,0:T(8,128)(2,1)}, bf16[128,1280]{1,0:T(8,128)(2,1)}) custom-call(bf16[128,4096]{1,0:T(8,128)(2,1)} %bitcast.10, bf16[128,512]{1,0:T(8,128)(2,1)} %bitcast.12, s32[1,128]{1,0:T(1,128)} %flag_ref.1), custom_call_target="tpu_custom_call" | custom-call | tf_op jit(solution)/shard_map/pack/pallas_call | solution.py:47
  5.5 1.6 %collective-permute-start = (bf16[128,1280]{1,0:T(8,128)(2,1)}, bf16[128,1280]{1,0:T(8,128)(2,1)S(1)}, u32[]{:S(2)}, u32[]{:S(2)}) collective-permute-start(bf16[128,1280]{1,0:T(8,128)(2,1)} %get-tuple-element.21), channel_id=1, source_target_pairs={{0,2},{2,0},{4,6},{6,4},{8,10},{10,8},{12,14},{14,12},{16,18},{18,... | collective-permute-start | bytes 983048 | tf_op jit(solution)/shard_map/ppermute | solution.py:203
  7.1 0.0 collective-permute-start.3
  7.1 7.8 %collective-permute-done.6.refs_10_ = bf16[128,1024]{1,0:T(8,128)(2,1)S(1)} collective-permute-done((bf16[128,1024]{1,0:T(8,128)(2,1)S(1)}, bf16[128,1024]{1,0:T(8,128)(2,1)S(1)}, u32[]{:S(2)}, u32[]{:S(2)}) %collective-permute-start.6) | collective-permute-done | bytes 262176 | tf_op jit(solution)/shard_map/ppermute | solution.py:203
  14.9 0.0 collective-permute-start.7
  14.9 1.5 %collective-permute-start.1 = (bf16[128,1280]{1,0:T(8,128)(2,1)}, bf16[128,1280]{1,0:T(8,128)(2,1)S(1)}, u32[]{:S(2)}, u32[]{:S(2)}) collective-permute-start(bf16[128,1280]{1,0:T(8,128)(2,1)} %get-tuple-element.22), channel_id=1, source_target_pairs={{0,4},{2,6},{4,0},{6,2},{8,12},{10,14},{12,8},{14,10},{16,20},{18,... | collective-permute-start | bytes 983048 | tf_op jit(solution)/shard_map/ppermute | solution.py:203
  16.5 0.0 collective-permute-done.4.refs_6_
  16.5 1.4 %collective-permute-start.2 = (bf16[128,1280]{1,0:T(8,128)(2,1)}, bf16[128,1280]{1,0:T(8,128)(2,1)S(1)}, u32[]{:S(2)}, u32[]{:S(2)}) collective-permute-start(bf16[128,1280]{1,0:T(8,128)(2,1)} %get-tuple-element.23), channel_id=1, source_target_pairs={{0,6},{2,4},{4,2},{6,0},{8,14},{10,12},{12,10},{14,8},{16,22},{18,... | collective-permute-start | bytes 983048 | tf_op jit(solution)/shard_map/ppermute | solution.py:203
  17.9 0.0 collective-permute-done.3.refs_5_
  17.9 0.0 collective-permute-start.9
  17.9 0.0 collective-permute-done.refs_1_.refs_5_
  17.9 0.5 collective-permute-start.5
  18.4 3.7 %collective-permute-done.7.refs_8_ = bf16[128,1024]{1,0:T(8,128)(2,1)S(1)} collective-permute-done((bf16[128,1024]{1,0:T(8,128)(2,1)S(1)}, bf16[128,1024]{1,0:T(8,128)(2,1)S(1)}, u32[]{:S(2)}, u32[]{:S(2)}) %collective-permute-start.7) | collective-permute-done | bytes 262176 | tf_op jit(solution)/shard_map/ppermute | solution.py:203
  22.1 0.0 collective-permute-start.8
  22.1 8.6 %collective-permute-done.1.refs_2_.refs_6_ = bf16[128,1280]{1,0:T(8,128)(2,1)S(1)} collective-permute-done((bf16[128,1280]{1,0:T(8,128)(2,1)}, bf16[128,1280]{1,0:T(8,128)(2,1)S(1)}, u32[]{:S(2)}, u32[]{:S(2)}) %collective-permute-start.1) | collective-permute-done | bytes 327712 | tf_op jit(solution)/shard_map/ppermute | solution.py:203
  30.8 0.0 collective-permute-done.2.refs_3_.refs_7_
  30.8 0.0 collective-permute-done.9.refs_11_
  30.8 0.0 collective-permute-done.5.refs_7_
  30.8 0.0 collective-permute-done.8.refs_9_
  30.8 0.0 copy-start
  30.8 1.0 %copy-done = bf16[128,1280]{1,0:T(8,128)(2,1)S(1)} copy-done((bf16[128,1280]{1,0:T(8,128)(2,1)S(1)}, bf16[128,1280]{1,0:T(8,128)(2,1)}, u32[]{:S(2)}) %copy-start) | copy-done | bytes 327704
  31.8 1.5 %product.1 = (f32[512,256]{1,0:T(8,128)S(1)}, bf16[512,256]{1,0:T(8,128)(2,1)S(1)}, bf16[512,256]{1,0:T(8,128)(2,1)S(1)}, bf16[512,256]{1,0:T(8,128)(2,1)S(1)}) custom-call(bf16[128,1280]{1,0:T(8,128)(2,1)S(1)} %copy-done, bf16[128,1280]{1,0:T(8,128)(2,1)S(1)} %collective-permute-done.refs_1_.refs_5_, ...), custom_call_target="tpu_custom_call" | custom-call | tf_op jit(solution)/shard_map/product/pallas_call | solution.py:88
  33.3 1.5 %collective-permute-start.10 = (bf16[512,256]{1,0:T(8,128)(2,1)S(1)}, bf16[512,256]{1,0:T(8,128)(2,1)S(1)}, u32[]{:S(2)}, u32[]{:S(2)}) collective-permute-start(bf16[512,256]{1,0:T(8,128)(2,1)S(1)} %get-tuple-element.25), channel_id=1, source_target_pairs={{0,2},{2,0},{4,6},{6,4},{8,10},{10,8},{12,14},{14,12},{16,18},{18,... | collective-permute-start | bytes 786440 | tf_op jit(solution)/shard_map/ppermute | solution.py:203
  34.8 1.5 %collective-permute-start.11 = (bf16[512,256]{1,0:T(8,128)(2,1)S(1)}, bf16[512,256]{1,0:T(8,128)(2,1)S(1)}, u32[]{:S(2)}, u32[]{:S(2)}) collective-permute-start(bf16[512,256]{1,0:T(8,128)(2,1)S(1)} %get-tuple-element.26), channel_id=1, source_target_pairs={{0,4},{2,6},{4,0},{6,2},{8,12},{10,14},{12,8},{14,10},{16,20},{18,... | collective-permute-start | bytes 786440 | tf_op jit(solution)/shard_map/ppermute | solution.py:203
  36.3 0.5 collective-permute-start.12
  36.8 5.7 %collective-permute-done.10.refs_1_ = bf16[512,256]{1,0:T(8,128)(2,1)S(1)} collective-permute-done((bf16[512,256]{1,0:T(8,128)(2,1)S(1)}, bf16[512,256]{1,0:T(8,128)(2,1)S(1)}, u32[]{:S(2)}, u32[]{:S(2)}) %collective-permute-start.10) | collective-permute-done | bytes 262176 | tf_op jit(solution)/shard_map/ppermute | solution.py:203
  42.5 3.7 %collective-permute-done.11.refs_2_ = bf16[512,256]{1,0:T(8,128)(2,1)S(1)} collective-permute-done((bf16[512,256]{1,0:T(8,128)(2,1)S(1)}, bf16[512,256]{1,0:T(8,128)(2,1)S(1)}, u32[]{:S(2)}, u32[]{:S(2)}) %collective-permute-start.11) | collective-permute-done | bytes 262176 | tf_op jit(solution)/shard_map/ppermute | solution.py:203
  46.2 0.7 %collective-permute-done.12.refs_3_ = bf16[512,256]{1,0:T(8,128)(2,1)S(1)} collective-permute-done((bf16[512,256]{1,0:T(8,128)(2,1)S(1)}, bf16[512,256]{1,0:T(8,128)(2,1)S(1)}, u32[]{:S(2)}, u32[]{:S(2)}) %collective-permute-start.12) | collective-permute-done | bytes 262176 | tf_op jit(solution)/shard_map/ppermute | solution.py:203
  47.0 1.1 %inside.1 = (f32[128,128]{1,0:T(8,128)S(1)}, f32[128,128]{1,0:T(8,128)}, bf16[512,128]{1,0:T(8,128)(2,1)S(1)}, f32[512,128]{1,0:T(8,128)S(1)}) custom-call(f32[512,256]{1,0:T(8,128)S(1)} %get-tuple-element.24.refs_0_, bf16[512,256]{1,0:T(8,128)(2,1)S(1)} %collective-permute-done.10.refs_1_, bf16[512,256]{1,0:T(8,128)(2,1)S(1)} %collective-permute-done.11.refs_2_, ...), custom_call_target="tpu_custom_call" | custom-call | tf_op jit(solution)/shard_map/inside/pallas_call | solution.py:139
  48.0 0.0 copy-start.1
  48.0 0.7 %copy-done.1 = f32[512,128]{1,0:T(8,128)} copy-done((f32[512,128]{1,0:T(8,128)}, f32[512,128]{1,0:T(8,128)S(1)}, u32[]{:S(2)}) %copy-start.1) | copy-done | bytes 262168
  48.7 0.0 copy-start.2
  48.7 0.7 copy-done.2
  49.4 1.3 %collective-permute-start.13 = (bf16[128,128]{1,0:T(8,128)(2,1)S(1)}, bf16[128,128]{1,0:T(8,128)(2,1)S(1)}, u32[]{:S(2)}, u32[]{:S(2)}) collective-permute-start(bf16[128,128]{1,0:T(8,128)(2,1)S(1)} %convert_element_type.3), channel_id=1, source_target_pairs={{8,16},{10,18},{12,20},{14,22},{9,17},{11,19},{13,21},{15,23}} | collective-permute-start | bytes 98312 | tf_op jit(solution)/shard_map/ppermute | solution.py:234
  50.7 4.5 %collective-permute-done.13.carried_ref = bf16[128,128]{1,0:T(8,128)(2,1)S(1)} collective-permute-done((bf16[128,128]{1,0:T(8,128)(2,1)S(1)}, bf16[128,128]{1,0:T(8,128)(2,1)S(1)}, u32[]{:S(2)}, u32[]{:S(2)}) %collective-permute-start.13) | collective-permute-done | bytes 32800 | tf_op jit(solution)/shard_map/ppermute | solution.py:234
  55.2 0.0 copy-start.7
  55.2 0.6 copy-done.7
  55.8 2.0 %finish.1 = (bf16[128,128]{1,0:T(8,128)(2,1)}, bf16[128,128]{1,0:T(8,128)(2,1)}, bf16[128,128]{1,0:T(8,128)(2,1)}, bf16[128,128]{1,0:T(8,128)(2,1)}) custom-call(bf16[128,128]{1,0:T(8,128)(2,1)} %copy-done.7, bf16[512,128]{1,0:T(8,128)(2,1)} %copy-done.2, f32[512,128]{1,0:T(8,128)} %copy-done.1, f32[1,512]{1,0:T(1,128)} %bitcast.13), custom_call_target="tpu_custom_call" | custom-call | tf_op jit(solution)/shard_map/finish/pallas_call | solution.py:174
  57.8 1.5 %collective-permute-start.14 = (bf16[128,128]{1,0:T(8,128)(2,1)}, bf16[128,128]{1,0:T(8,128)(2,1)S(1)}, u32[]{:S(2)}, u32[]{:S(2)}) collective-permute-start(bf16[128,128]{1,0:T(8,128)(2,1)} %get-tuple-element.32), channel_id=1, source_target_pairs={{0,2},{2,0},{4,6},{6,4},{8,10},{10,8},{12,14},{14,12},{16,18},{18,... | collective-permute-start | bytes 98312 | tf_op jit(solution)/shard_map/ppermute | solution.py:203
  59.3 0.8 %collective-permute-start.15 = (bf16[128,128]{1,0:T(8,128)(2,1)}, bf16[128,128]{1,0:T(8,128)(2,1)S(1)}, u32[]{:S(2)}, u32[]{:S(2)}) collective-permute-start(bf16[128,128]{1,0:T(8,128)(2,1)} %get-tuple-element.33), channel_id=1, source_target_pairs={{0,4},{2,6},{4,0},{6,2},{8,12},{10,14},{12,8},{14,10},{16,20},{18,... | collective-permute-start | bytes 98312 | tf_op jit(solution)/shard_map/ppermute | solution.py:203
  60.1 1.2 %collective-permute-start.16 = (bf16[128,128]{1,0:T(8,128)(2,1)}, bf16[128,128]{1,0:T(8,128)(2,1)S(1)}, u32[]{:S(2)}, u32[]{:S(2)}) collective-permute-start(bf16[128,128]{1,0:T(8,128)(2,1)} %get-tuple-element.34), channel_id=1, source_target_pairs={{0,6},{2,4},{4,2},{6,0},{8,14},{10,12},{12,10},{14,8},{16,22},{18,... | collective-permute-start | bytes 98312 | tf_op jit(solution)/shard_map/ppermute | solution.py:203
  61.3 0.6 collective-permute-done.14.refs_1_
  61.9 0.0 copy-start.4
  61.9 1.5 %collective-permute-done.15.refs_2_ = bf16[128,128]{1,0:T(8,128)(2,1)S(1)} collective-permute-done((bf16[128,128]{1,0:T(8,128)(2,1)}, bf16[128,128]{1,0:T(8,128)(2,1)S(1)}, u32[]{:S(2)}, u32[]{:S(2)}) %collective-permute-start.15) | collective-permute-done | bytes 32800 | tf_op jit(solution)/shard_map/ppermute | solution.py:203
  63.4 0.0 copy-start.5
  63.4 1.7 %collective-permute-done.16.refs_3_ = bf16[128,128]{1,0:T(8,128)(2,1)S(1)} collective-permute-done((bf16[128,128]{1,0:T(8,128)(2,1)}, bf16[128,128]{1,0:T(8,128)(2,1)S(1)}, u32[]{:S(2)}, u32[]{:S(2)}) %collective-permute-start.16) | collective-permute-done | bytes 32800 | tf_op jit(solution)/shard_map/ppermute | solution.py:203
  65.1 0.0 copy-start.6
  65.1 0.0 copy-done.4
  65.1 0.0 copy-done.5
  65.1 0.6 copy-done.6
  65.7 1.5 %join.1 = bf16[128,512]{1,0:T(8,128)(2,1)} custom-call(bf16[128,128]{1,0:T(8,128)(2,1)} %get-tuple-element.31.refs_0_, bf16[128,128]{1,0:T(8,128)(2,1)} %copy-done.4, bf16[128,128]{1,0:T(8,128)(2,1)} %copy-done.5, bf16[128,128]{1,0:T(8,128)(2,1)} %copy-done.6), custom_call_target="tpu_custom_call" | custom-call | tf_op jit(solution)/shard_map/join/pallas_call | solution.py:190
  (3 shorter events, 0.1 us)
Async XLA Ops:
  0.0 1.0 %copy-start.3 = (bf16[128,512]{1,0:T(8,128)(2,1)S(1)}, bf16[128,512]{1,0:T(8,128)(2,1)}, u32[]{:S(2)}) copy-start(bf16[128,512]{1,0:T(8,128)(2,1)} %param.10) | copy-start | bytes 393220
  1.2 13.7 %collective-permute-start.6 = (bf16[128,1024]{1,0:T(8,128)(2,1)S(1)}, bf16[128,1024]{1,0:T(8,128)(2,1)S(1)}, u32[]{:S(2)}, u32[]{:S(2)}) collective-permute-start(bf16[128,1024]{1,0:T(8,128)(2,1)S(1)} %bitcast.6), channel_id=1, source_target_pairs={{0,24},{2,26},{4,28},{6,30},{8,16},{10,18},{12,20},{14,22},{16,8},... | collective-permute-start | bytes 786440 | tf_op jit(solution)/shard_map/ppermute | solution.py:203
  1.7 14.7 %collective-permute-start.4 = (bf16[128,1024]{1,0:T(8,128)(2,1)S(1)}, bf16[128,1024]{1,0:T(8,128)(2,1)S(1)}, u32[]{:S(2)}, u32[]{:S(2)}) collective-permute-start(bf16[128,1024]{1,0:T(8,128)(2,1)S(1)} %bitcast.7), channel_id=1, source_target_pairs={{0,8},{2,10},{4,12},{6,14},{8,0},{10,2},{12,4},{14,6},{16,24},{18,... | collective-permute-start | bytes 786440 | tf_op jit(solution)/shard_map/ppermute | solution.py:203
  5.5 12.4 %collective-permute-start = (bf16[128,1280]{1,0:T(8,128)(2,1)}, bf16[128,1280]{1,0:T(8,128)(2,1)S(1)}, u32[]{:S(2)}, u32[]{:S(2)}) collective-permute-start(bf16[128,1280]{1,0:T(8,128)(2,1)} %get-tuple-element.21), channel_id=1, source_target_pairs={{0,2},{2,0},{4,6},{6,4},{8,10},{10,8},{12,14},{14,12},{16,18},{18,... | collective-permute-start | bytes 983048 | tf_op jit(solution)/shard_map/ppermute | solution.py:203
  7.1 10.8 %collective-permute-start.3 = (bf16[128,1024]{1,0:T(8,128)(2,1)S(1)}, bf16[128,1024]{1,0:T(8,128)(2,1)S(1)}, u32[]{:S(2)}, u32[]{:S(2)}) collective-permute-start(bf16[128,1024]{1,0:T(8,128)(2,1)S(1)} %bitcast.8), channel_id=1, source_target_pairs={{0,1},{1,0},{2,3},{3,2},{4,5},{5,4},{6,7},{7,6},{8,9},{9,8},{10,11... | collective-permute-start | bytes 786440 | tf_op jit(solution)/shard_map/ppermute | solution.py:216
  14.9 7.2 %collective-permute-start.7 = (bf16[128,1024]{1,0:T(8,128)(2,1)S(1)}, bf16[128,1024]{1,0:T(8,128)(2,1)S(1)}, u32[]{:S(2)}, u32[]{:S(2)}) collective-permute-start(bf16[128,1024]{1,0:T(8,128)(2,1)S(1)} %collective-permute-done.6.refs_10_), channel_id=1, source_target_pairs={{0,8},{2,10},{4,12},{6,14},{8,0},{10,2},{12,4},{14,6},{16,24},{18,... | collective-permute-start | bytes 786440 | tf_op jit(solution)/shard_map/ppermute | solution.py:203
  14.9 15.8 %collective-permute-start.1 = (bf16[128,1280]{1,0:T(8,128)(2,1)}, bf16[128,1280]{1,0:T(8,128)(2,1)S(1)}, u32[]{:S(2)}, u32[]{:S(2)}) collective-permute-start(bf16[128,1280]{1,0:T(8,128)(2,1)} %get-tuple-element.22), channel_id=1, source_target_pairs={{0,4},{2,6},{4,0},{6,2},{8,12},{10,14},{12,8},{14,10},{16,20},{18,... | collective-permute-start | bytes 983048 | tf_op jit(solution)/shard_map/ppermute | solution.py:203
  16.5 14.3 %collective-permute-start.2 = (bf16[128,1280]{1,0:T(8,128)(2,1)}, bf16[128,1280]{1,0:T(8,128)(2,1)S(1)}, u32[]{:S(2)}, u32[]{:S(2)}) collective-permute-start(bf16[128,1280]{1,0:T(8,128)(2,1)} %get-tuple-element.23), channel_id=1, source_target_pairs={{0,6},{2,4},{4,2},{6,0},{8,14},{10,12},{12,10},{14,8},{16,22},{18,... | collective-permute-start | bytes 983048 | tf_op jit(solution)/shard_map/ppermute | solution.py:203
  17.9 12.9 %collective-permute-start.9 = (bf16[128,1024]{1,0:T(8,128)(2,1)S(1)}, bf16[128,1024]{1,0:T(8,128)(2,1)S(1)}, u32[]{:S(2)}, u32[]{:S(2)}) collective-permute-start(bf16[128,1024]{1,0:T(8,128)(2,1)S(1)} %collective-permute-done.6.refs_10_), channel_id=1, source_target_pairs={{0,1},{1,0},{2,3},{3,2},{4,5},{5,4},{6,7},{7,6},{8,9},{9,8},{10,11... | collective-permute-start | bytes 786440 | tf_op jit(solution)/shard_map/ppermute | solution.py:216
  17.9 12.9 %collective-permute-start.5 = (bf16[128,1024]{1,0:T(8,128)(2,1)S(1)}, bf16[128,1024]{1,0:T(8,128)(2,1)S(1)}, u32[]{:S(2)}, u32[]{:S(2)}) collective-permute-start(bf16[128,1024]{1,0:T(8,128)(2,1)S(1)} %collective-permute-done.4.refs_6_), channel_id=1, source_target_pairs={{0,1},{1,0},{2,3},{3,2},{4,5},{5,4},{6,7},{7,6},{8,9},{9,8},{10,11... | collective-permute-start | bytes 786440 | tf_op jit(solution)/shard_map/ppermute | solution.py:216
  22.1 8.7 %collective-permute-start.8 = (bf16[128,1024]{1,0:T(8,128)(2,1)S(1)}, bf16[128,1024]{1,0:T(8,128)(2,1)S(1)}, u32[]{:S(2)}, u32[]{:S(2)}) collective-permute-start(bf16[128,1024]{1,0:T(8,128)(2,1)S(1)} %collective-permute-done.7.refs_8_), channel_id=1, source_target_pairs={{0,1},{1,0},{2,3},{3,2},{4,5},{5,4},{6,7},{7,6},{8,9},{9,8},{10,11... | collective-permute-start | bytes 786440 | tf_op jit(solution)/shard_map/ppermute | solution.py:216
  30.8 1.0 %copy-start = (bf16[128,1280]{1,0:T(8,128)(2,1)S(1)}, bf16[128,1280]{1,0:T(8,128)(2,1)}, u32[]{:S(2)}) copy-start(bf16[128,1280]{1,0:T(8,128)(2,1)} %get-tuple-element.20.refs_0_.refs_4_) | copy-start | bytes 983044
  33.3 9.2 %collective-permute-start.10 = (bf16[512,256]{1,0:T(8,128)(2,1)S(1)}, bf16[512,256]{1,0:T(8,128)(2,1)S(1)}, u32[]{:S(2)}, u32[]{:S(2)}) collective-permute-start(bf16[512,256]{1,0:T(8,128)(2,1)S(1)} %get-tuple-element.25), channel_id=1, source_target_pairs={{0,2},{2,0},{4,6},{6,4},{8,10},{10,8},{12,14},{14,12},{16,18},{18,... | collective-permute-start | bytes 786440 | tf_op jit(solution)/shard_map/ppermute | solution.py:203
  34.8 11.4 %collective-permute-start.11 = (bf16[512,256]{1,0:T(8,128)(2,1)S(1)}, bf16[512,256]{1,0:T(8,128)(2,1)S(1)}, u32[]{:S(2)}, u32[]{:S(2)}) collective-permute-start(bf16[512,256]{1,0:T(8,128)(2,1)S(1)} %get-tuple-element.26), channel_id=1, source_target_pairs={{0,4},{2,6},{4,0},{6,2},{8,12},{10,14},{12,8},{14,10},{16,20},{18,... | collective-permute-start | bytes 786440 | tf_op jit(solution)/shard_map/ppermute | solution.py:203
  36.3 10.6 %collective-permute-start.12 = (bf16[512,256]{1,0:T(8,128)(2,1)S(1)}, bf16[512,256]{1,0:T(8,128)(2,1)S(1)}, u32[]{:S(2)}, u32[]{:S(2)}) collective-permute-start(bf16[512,256]{1,0:T(8,128)(2,1)S(1)} %get-tuple-element.27), channel_id=1, source_target_pairs={{0,6},{2,4},{4,2},{6,0},{8,14},{10,12},{12,10},{14,8},{16,22},{18,... | collective-permute-start | bytes 786440 | tf_op jit(solution)/shard_map/ppermute | solution.py:203
  48.0 0.7 %copy-start.1 = (f32[512,128]{1,0:T(8,128)}, f32[512,128]{1,0:T(8,128)S(1)}, u32[]{:S(2)}) copy-start(f32[512,128]{1,0:T(8,128)S(1)} %get-tuple-element.30.inside_ref) | copy-start | bytes 786436
  48.7 0.7 copy-start.2
  49.4 5.8 %collective-permute-start.13 = (bf16[128,128]{1,0:T(8,128)(2,1)S(1)}, bf16[128,128]{1,0:T(8,128)(2,1)S(1)}, u32[]{:S(2)}, u32[]{:S(2)}) collective-permute-start(bf16[128,128]{1,0:T(8,128)(2,1)S(1)} %convert_element_type.3), channel_id=1, source_target_pairs={{8,16},{10,18},{12,20},{14,22},{9,17},{11,19},{13,21},{15,23}} | collective-permute-start | bytes 98312 | tf_op jit(solution)/shard_map/ppermute | solution.py:234
  55.2 0.6 copy-start.7
  57.8 4.1 %collective-permute-start.14 = (bf16[128,128]{1,0:T(8,128)(2,1)}, bf16[128,128]{1,0:T(8,128)(2,1)S(1)}, u32[]{:S(2)}, u32[]{:S(2)}) collective-permute-start(bf16[128,128]{1,0:T(8,128)(2,1)} %get-tuple-element.32), channel_id=1, source_target_pairs={{0,2},{2,0},{4,6},{6,4},{8,10},{10,8},{12,14},{14,12},{16,18},{18,... | collective-permute-start | bytes 98312 | tf_op jit(solution)/shard_map/ppermute | solution.py:203
  59.3 4.1 %collective-permute-start.15 = (bf16[128,128]{1,0:T(8,128)(2,1)}, bf16[128,128]{1,0:T(8,128)(2,1)S(1)}, u32[]{:S(2)}, u32[]{:S(2)}) collective-permute-start(bf16[128,128]{1,0:T(8,128)(2,1)} %get-tuple-element.33), channel_id=1, source_target_pairs={{0,4},{2,6},{4,0},{6,2},{8,12},{10,14},{12,8},{14,10},{16,20},{18,... | collective-permute-start | bytes 98312 | tf_op jit(solution)/shard_map/ppermute | solution.py:203
  60.1 5.0 %collective-permute-start.16 = (bf16[128,128]{1,0:T(8,128)(2,1)}, bf16[128,128]{1,0:T(8,128)(2,1)S(1)}, u32[]{:S(2)}, u32[]{:S(2)}) collective-permute-start(bf16[128,128]{1,0:T(8,128)(2,1)} %get-tuple-element.34), channel_id=1, source_target_pairs={{0,6},{2,4},{4,2},{6,0},{8,14},{10,12},{12,10},{14,8},{16,22},{18,... | collective-permute-start | bytes 98312 | tf_op jit(solution)/shard_map/ppermute | solution.py:203
  61.9 3.2 %copy-start.4 = (bf16[128,128]{1,0:T(8,128)(2,1)}, bf16[128,128]{1,0:T(8,128)(2,1)S(1)}, u32[]{:S(2)}) copy-start(bf16[128,128]{1,0:T(8,128)(2,1)S(1)} %collective-permute-done.14.refs_1_) | copy-start | bytes 98308
  63.4 1.7 %copy-start.5 = (bf16[128,128]{1,0:T(8,128)(2,1)}, bf16[128,128]{1,0:T(8,128)(2,1)S(1)}, u32[]{:S(2)}) copy-start(bf16[128,128]{1,0:T(8,128)(2,1)S(1)} %collective-permute-done.15.refs_2_) | copy-start | bytes 98308
  65.1 0.6 copy-start.6

commit v2 on v1

v2 whole, which is shorter than its diff:
```python
import functools

import jax
import jax.numpy as jnp
from jax import lax
from jax.experimental import pallas as pl
from jax.experimental.pallas import tpu as pltpu
from jax.sharding import PartitionSpec as P

HEAD = 128
BF, F32 = jnp.bfloat16, jnp.float32
DOC_BLOCKS = {16: 8, 64: 16}
MARKS = 16


def phi(u):
    return jnp.where(u > 0, u + 1.0, jnp.exp(jnp.minimum(u, 0.0)))


def aligned(index, size):
    return pl.ds(pl.multiple_of(index * size, size), size)


def inner_outer(heads):
    me = lax.axis_index("ctx")
    return lax.rem(me, heads), lax.div(me, heads)


def limit(mib):
    return pltpu.CompilerParams(vmem_limit_bytes=mib * 2**20)


def pack_kernel(heads, tok_ref, query_ref, flag_ref, key_ref, value_ref, *refs):
    weight_ref, out_refs = refs[0], refs[1 : 1 + heads]
    query, flag, extra, in_sems, tok_sems, out_sems = refs[1 + heads :]
    inner, _ = inner_outer(heads)
    count, depth = tok_ref.shape
    rows = key_ref.shape[0]
    squares = depth // (heads * HEAD)
    loads = [
        pltpu.make_async_copy(query_ref, query, in_sems.at[0]),
        pltpu.make_async_copy(flag_ref, flag, in_sems.at[1]),
    ]
    copies = [
        pltpu.make_async_copy(key_ref, weight_ref.at[:rows, :], in_sems.at[2]),
        pltpu.make_async_copy(value_ref, weight_ref.at[rows:, :], in_sems.at[3]),
    ]
    for k in list(range(1, heads)) + [0]:
        to = jnp.bitwise_xor(inner, k)
        for i in range(squares):
            at = ((i // 2) * heads + to) * 2 + i % 2
            copies.append(
                pltpu.make_async_copy(
                    tok_ref.at[:, aligned(at, HEAD)],
                    out_refs[k].at[i * count : (i + 1) * count, :],
                    tok_sems.at[k, i],
                )
            )
    for copy in loads + copies:
        copy.start()
    for copy in loads:
        copy.wait()
    marks = jnp.broadcast_to(flag[...].astype(F32), (MARKS, count)).astype(BF)
    for k, out in enumerate(out_refs):
        own = query[:, aligned(jnp.bitwise_xor(inner, k), HEAD)].astype(F32)
        extra[k, :count, :] = phi(own).astype(BF)
        extra[k, count:, :] = marks
        copy = pltpu.make_async_copy(extra.at[k], out.at[squares * count :, :], out_sems.at[k])
        copy.start()
        copies.append(copy)
    for copy in copies:
        copy.wait()


def pack(tokens, queries, flags, w_key, w_value, heads, fsdp):
    count, depth = tokens.shape
    rows, width = w_key.shape
    share, squares = fsdp * rows, depth // (heads * HEAD)
    if share == 2 * HEAD:
        shape = ((squares + 1) * count + MARKS, HEAD)
        hbm = pl.BlockSpec(memory_space=pl.ANY)
        weights, *packed = pl.pallas_call(
            functools.partial(pack_kernel, heads),
            in_specs=[hbm] * 5,
            out_specs=[hbm] * (1 + heads),
            out_shape=[jax.ShapeDtypeStruct((2 * rows, width), BF)]
            + [jax.ShapeDtypeStruct(shape, BF)] * heads,
            scratch_shapes=[
                pltpu.VMEM((count, width), BF),
                pltpu.VMEM((1, count), jnp.int32),
                pltpu.VMEM((heads, count + MARKS, HEAD), BF),
                pltpu.SemaphoreType.DMA((4,)),
                pltpu.SemaphoreType.DMA((heads, squares)),
                pltpu.SemaphoreType.DMA((heads,)),
            ],
            compiler_params=limit(60),
            name="pack",
        )(tokens, queries, flags, w_key, w_value)
        return weights, packed
    inner, _ = inner_outer(heads)
    by_inner = tokens.reshape(count, -1, heads, share).transpose(2, 0, 1, 3)
    by_inner = by_inner.reshape(heads, count, squares, HEAD).transpose(0, 2, 1, 3).reshape(heads, -1, HEAD)
    query = phi(queries.astype(F32)).astype(BF).reshape(count, heads, HEAD).transpose(1, 0, 2)
    marks = jnp.broadcast_to(flags.astype(BF), (MARKS, count))
    out = []
    for k in range(heads):
        to = jnp.bitwise_xor(inner, k)
        parts = [lax.dynamic_index_in_dim(a, to, 0, False) for a in (by_inner, query)]
        out.append(jnp.concatenate(parts + [marks], axis=0))
    return jnp.concatenate([w_key, w_value], axis=0), out


def product_kernel(heads, count, split, places, *refs):
    x_refs, w_refs = refs[:heads], refs[heads : -heads - 1]
    out_refs, tok = refs[-heads - 1 : -1], refs[-1]
    inner, outer = inner_outer(heads)
    squares = tok.shape[1] // HEAD
    half = tok.shape[1] // len(places)
    for k, x in enumerate(x_refs):
        rows = aligned(jnp.bitwise_xor(inner, k), count)
        for i in range(squares):
            at = i
            if split:
                core = lax.axis_index("fsdp")
                at = jnp.bitwise_xor(outer, i // 2) * 2 + jnp.bitwise_xor(core, i % 2)
            tok[rows, i * HEAD : (i + 1) * HEAD] = x[aligned(at, count), :]
    for k in list(range(1, heads)) + [0]:
        cols = aligned(jnp.bitwise_xor(inner, k), HEAD)
        key = jnp.concatenate([w_refs[j][at : at + half, cols] for j, at in places], axis=0)
        value = jnp.concatenate([w_refs[j][at + half : at + 2 * half, cols] for j, at in places], axis=0)
        w = jnp.concatenate([key, value], axis=1)
        out = out_refs[k]
        out[...] = jnp.dot(tok[...], w, preferred_element_type=F32).astype(out.dtype)


def product(xs, ws, heads, count, split, places):
    depth = sum(w.shape[0] for w in ws) // 2
    shape = (heads * count, 2 * HEAD)
    return pl.pallas_call(
        functools.partial(product_kernel, heads, count, split, places),
        out_shape=[jax.ShapeDtypeStruct(shape, F32)] + [jax.ShapeDtypeStruct(shape, BF)] * (heads - 1),
        scratch_shapes=[pltpu.VMEM((heads * count, depth), BF)],
        compiler_params=limit(24),
        name="product",
    )(*xs, *ws)


def inside_kernel(heads, *refs):
    parts, queries, flags = refs[:heads], refs[heads : 2 * heads], refs[2 * heads : 3 * heads]
    state_ref, keep_ref, first_ref = refs[3 * heads : 3 * heads + 3]
    within_refs = refs[3 * heads + 3 : -3]
    query, marks, within = refs[-3:]
    inner, _ = inner_outer(heads)
    count = queries[0].shape[0]
    total = heads * count
    for k in range(heads):
        at = jnp.bitwise_xor(inner, k)
        query[aligned(at, count), :] = queries[k][...]
        marks[:, aligned(at, count)] = flags[k][...]
    proj = parts[0][...]
    for part in parts[1:]:
        proj = proj + part[...].astype(F32)
    key = phi(proj[:, :HEAD]).astype(BF)
    value = proj[:, HEAD:].astype(BF)
    early = lax.broadcasted_iota(jnp.int32, (total, total), 0)
    late = lax.broadcasted_iota(jnp.int32, (total, total), 1)
    upto = jnp.where(early <= late, 1.0, 0.0).astype(BF)
    seg = jnp.dot(marks[...], upto, preferred_element_type=F32)[:1, :]
    seg = jnp.broadcast_to(seg, (HEAD, total))
    seg_col = seg.T
    last = jnp.broadcast_to(seg_col[total - 1 :, :], (total, HEAD))
    tail = jnp.where(seg_col == last, value.astype(F32), 0.0).astype(BF)
    state = lax.dot_general(key, tail, (((0,), (0,)), ((), ())), preferred_element_type=F32)
    state_ref[...] = state.astype(state_ref.dtype)
    keep_ref[...] = jnp.where(last[:HEAD, :] == 0.0, 1.0, 0.0)
    within[...] = jnp.where(seg_col == 0.0, 1.0, 0.0)
    first_ref[...] = within[aligned(inner, count), :].astype(BF)
    for i in range(heads):
        rows, width = slice(i * count, (i + 1) * count), (i + 1) * count
        scores = lax.dot_general(
            query[rows, :], key[:width, :], (((1,), (1,)), ((), ())), preferred_element_type=F32
        )
        own = jnp.concatenate([seg_col[rows, :]] * (i + 1), axis=1)
        allowed = (own == seg[:, :width]) & (late[:count, :width] <= early[rows, :width])
        scores = jnp.where(allowed, scores, 0.0).astype(BF)
        within[rows, :] = jnp.dot(scores, value[:width, :], preferred_element_type=F32)
    for k, out in enumerate(within_refs):
        out[...] = within[aligned(jnp.bitwise_xor(inner, k), count), :].astype(out.dtype)


def inside(parts, packed, heads, count, kind):
    total = heads * count
    squares = (packed[0].shape[0] - MARKS) // count - 1

    def at(rows, cols, place=0):
        return pl.BlockSpec((rows, cols), lambda i: (place, 0))

    def shape(rows, cols, dtype):
        return jax.ShapeDtypeStruct((rows, cols), dtype)

    return pl.pallas_call(
        functools.partial(inside_kernel, heads),
        grid=(1,),
        in_specs=[at(total, 2 * HEAD)] * heads
        + [at(count, HEAD, squares)] * heads
        + [at(MARKS, HEAD, (squares + 1) * count // MARKS)] * heads,
        out_shape=[shape(HEAD, HEAD, kind), shape(HEAD, HEAD, F32), shape(count, HEAD, BF)]
        + [shape(count, HEAD, F32)]
        + [shape(count, HEAD, BF)] * (heads - 1),
        out_specs=[at(HEAD, HEAD)] * 2 + [at(count, HEAD)] * (heads + 1),
        scratch_shapes=[
            pltpu.VMEM((total, HEAD), BF),
            pltpu.VMEM((MARKS, total), BF),
            pltpu.VMEM((total, HEAD), F32),
        ],
        compiler_params=limit(24),
        name="inside",
    )(*parts, *packed, *packed)


def finish_kernel(heads, *refs):
    carried, within, queries = refs[:heads], refs[heads : 2 * heads], refs[2 * heads : 3 * heads]
    first_ref, gain_ref, out_ref = refs[3 * heads :]
    inner, _ = inner_outer(heads)
    for k in range(heads):
        cols = aligned(jnp.bitwise_xor(inner, k), HEAD)
        query = queries[k][...] * first_ref[...]
        mixed = within[k][...].astype(F32) + jnp.dot(query, carried[k][...], preferred_element_type=F32)
        scale = lax.rsqrt(jnp.mean(mixed * mixed, axis=-1, keepdims=True) + 1e-06)
        out_ref[:, cols] = (mixed * scale * gain_ref[:, cols]).astype(BF)


def finish(carried, within, packed, first, gain, heads):
    count = first.shape[0]
    squares = (packed[0].shape[0] - MARKS) // count - 1

    def at(rows, cols, place=0):
        return pl.BlockSpec((rows, cols), lambda i: (place, 0))

    return pl.pallas_call(
        functools.partial(finish_kernel, heads),
        grid=(1,),
        in_specs=[at(HEAD, HEAD)] * heads
        + [at(count, HEAD)] * heads
        + [at(count, HEAD, squares)] * heads
        + [at(count, HEAD), at(1, heads * HEAD)],
        out_shape=jax.ShapeDtypeStruct((count, heads * HEAD), BF),
        out_specs=at(count, heads * HEAD),
        compiler_params=limit(8),
        name="finish",
    )(*carried, *within, *packed, first, gain)


def on_device(n_ctx, fsdp, tokens, queries, flags, w_key, w_value, norm_gain):
    count = tokens.shape[1]
    rows, width = w_key.shape
    heads = width // HEAD
    outer = n_ctx // heads

    def swap(a, mask):
        return lax.ppermute(a, "ctx", [(i, i ^ mask) for i in range(n_ctx)])

    split = outer == 4 and fsdp == 2 and rows == HEAD
    weights, packed = pack(tokens[0], queries[0], flags, w_key, w_value, heads, fsdp)
    if split:
        far = swap(weights, 3 * heads)
        near = swap(weights, heads)
    received = [packed[0]] + [swap(packed[k], k) for k in range(1, heads)]
    if split:
        far, near, *received = lax.optimization_barrier((far, near, *received))
        last = swap(far, heads)
        early = jnp.concatenate([weights, near, far], axis=0)
        early, last_other = [lax.ppermute(w, "fsdp", [(0, 1), (1, 0)]) for w in (early, last)]
        panels = [weights, near, last, far, early, last_other]
        places = [(0, 0), (4, 0), (1, 0), (4, 2 * rows), (2, 0), (5, 0), (3, 0), (4, 4 * rows)]
    else:
        groups = [[o * heads + q for o in range(outer)] for q in range(heads)]
        chip = [lax.all_gather(w, "fsdp", axis=0, tiled=True) for w in (w_key, w_value)]
        panels = [lax.all_gather(w, "ctx", axis=0, tiled=True, axis_index_groups=groups) for w in chip]
        panels, places = [jnp.concatenate(panels, axis=0)], [(0, 0)]
    partial = product(received, panels, heads, count, split, places)
    parts = [partial[0]] + [swap(partial[k], k) for k in range(1, heads)]

    doc = DOC_BLOCKS.get(n_ctx, 2 * n_ctx)
    starts = [b for b in range(n_ctx) if b % doc == doc // 2]
    pairs = [
        (b, b + heads)
        for b in range(n_ctx - heads)
        if (b // heads + 1) * heads not in starts
    ]
    rounds = max(1, min(doc // heads, outer) - 1)
    state, keep, first, *within = inside(parts, received, heads, count, BF if rounds == 1 else F32)
    leaving = state
    for _ in range(rounds - 1):
        carried = lax.ppermute(leaving.astype(BF), "ctx", pairs)
        leaving = state + keep * carried.astype(F32)
    leaving = leaving.astype(BF)
    carried = [lax.ppermute(leaving, "ctx", [(a, b ^ k) for a, b in pairs]) for k in range(heads)]
    within = [within[0]] + [swap(within[k], k) for k in range(1, heads)]
    return finish(carried, within, packed, first, norm_gain.reshape(1, width), heads)[None]


def solution(mesh):
    n_ctx, fsdp = mesh.shape["ctx"], mesh.shape["fsdp"]
    in_specs = (
        P("fsdp", "ctx", None),
        P("fsdp", "ctx", None),
        P("fsdp", "ctx"),
        P(("ctx", "fsdp"), None),
        P(("ctx", "fsdp"), None),
        P(),
    )
    return jax.shard_map(
        functools.partial(on_device, n_ctx, fsdp),
        mesh=mesh,
        in_specs=in_specs,
        out_specs=P("fsdp", "ctx", None),
        check_vma=False,
    )
```

time: 67.5 us -> 104 us (1.54)
  Pallas kernels: 8.61 us -> 44.9 us
  local copies, waits for them, and re-layouts: 4.6 us -> 0.03 us
  starting transfers between devices: 15.1 us -> 17.9 us
  waiting for transfers between devices: 38.6 us -> 39.7 us
    pallas_call x4 -> x3, Pallas kernels: 7.56 us -> 43.7 us  [the longest x1 41.2 us: pack(): pl.pallas_call(functools.partial(pack_kernel, heads), in_specs=[hbm] * 5,...]
    unnamed x17 -> x12, local copies, waits for them, and re-layouts: 3.59 us -> 0.03 us
    ppermute x5 -> x6, starting transfers between devices: 1.79 us -> 5.22 us  [the longest x4 5.15 us: on_device(): lax.ppermute(leaving, 'ctx', [(a, b ^ k) for a, b in pairs])]
    ppermute x5 -> x6, waiting for transfers between devices: 4.52 us -> 5.87 us  [the longest x4 4.34 us: on_device(): lax.ppermute(leaving, 'ctx', [(a, b ^ k) for a, b in pairs])]
  transfers between devices with their start and end apart: 17 -> 18, of which waited for: 10 -> 10; matrix products, arithmetic and copies ran while one was open for 0% -> 0% of each run, Pallas kernels for 4% -> 0%
where the time goes in v2:
time: 104 us
  Pallas kernels  44.9 us (43%)
  waiting for transfers between devices  39.7 us (38%)
  starting transfers between devices  17.9 us (17%)
    pallas_call x1, Pallas kernels, pack(): pl.pallas_call(functools.partial(pack_kernel, heads), in_specs=[hbm] * 5,...  41.2 us
    ppermute x12, waiting for transfers between devices, swap(): return lax.ppermute(a, 'ctx', [(i, i ^ mask) for i in range(n_ctx)])  33.8 us
    ppermute x12, starting transfers between devices, swap(): return lax.ppermute(a, 'ctx', [(i, i ^ mask) for i in range(n_ctx)])  12.7 us
    ppermute x4, starting transfers between devices, on_device(): lax.ppermute(leaving, 'ctx', [(a, b ^ k) for a, b in pairs])  5.15 us
    ppermute x4, waiting for transfers between devices, on_device(): lax.ppermute(leaving, 'ctx', [(a, b ^ k) for a, b in pairs])  4.34 us
  transfers between devices with their start and end apart: 18, of which 10 were waited for; matrix products, arithmetic and copies ran while one was open for 0% of the time, Pallas kernels for 0%

profile of v2, /device:TPU:16, one launch (start us, length us, event | category | flops | bytes accessed | tf_op | source)
XLA Modules:
  0.0 103.7 jit_solution(6884167560084365564)
XLA Ops:
  0.0 41.2 %pack.1 = (bf16[256,512]{1,0:T(8,128)(2,1)}, bf16[1168,128]{1,0:T(8,128)(2,1)}, bf16[1168,128]{1,0:T(8,128)(2,1)}, bf16[1168,128]{1,0:T(8,128)(2,1)}, bf16[1168,128]{1,0:T(8,128)(2,1)}) custom-call(bf16[128,4096]{1,0:T(8,128)(2,1)} %bitcast.5, bf16[128,512]{1,0:T(8,128)(2,1)} %bitcast.6, s32[1,128]{1,0:T(1,128)} %flag_ref.1, bf16[128,512]{1,0:T(8,128)(2,1)} %key_ref.1, ...), custom_call_target="tpu_custom_call" | custom-call | tf_op jit(solution)/shard_map/pack/pallas_call | solution.py:82
  41.2 0.0 copy-start
  41.2 0.0 copy-start.1
  41.2 1.6 %collective-permute-start.2 = (bf16[1168,128]{1,0:T(8,128)(2,1)}, bf16[1168,128]{1,0:T(8,128)(2,1)S(1)}, u32[]{:S(2)}, u32[]{:S(2)}) collective-permute-start(bf16[1168,128]{1,0:T(8,128)(2,1)} %get-tuple-element.28.refs_9_), channel_id=1, source_target_pairs={{0,2},{2,0},{4,6},{6,4},{8,10},{10,8},{12,14},{14,12},{16,18},{18,... | collective-permute-start | bytes 897032 | tf_op jit(solution)/shard_map/ppermute | solution.py:261
  42.8 1.5 %collective-permute-start.3 = (bf16[1168,128]{1,0:T(8,128)(2,1)}, bf16[1168,128]{1,0:T(8,128)(2,1)S(1)}, u32[]{:S(2)}, u32[]{:S(2)}) collective-permute-start(bf16[1168,128]{1,0:T(8,128)(2,1)} %get-tuple-element.29.refs_10_), channel_id=1, source_target_pairs={{0,4},{2,6},{4,0},{6,2},{8,12},{10,14},{12,8},{14,10},{16,20},{18,... | collective-permute-start | bytes 897032 | tf_op jit(solution)/shard_map/ppermute | solution.py:261
  44.3 0.5 collective-permute-start.4
  44.8 1.6 %collective-permute-start.1 = (bf16[256,512]{1,0:T(8,128)(2,1)}, bf16[256,512]{1,0:T(8,128)(2,1)S(1)}, u32[]{:S(2)}, u32[]{:S(2)}) collective-permute-start(bf16[256,512]{1,0:T(8,128)(2,1)} %get-tuple-element.26.refs_4_), channel_id=1, source_target_pairs={{0,8},{2,10},{4,12},{6,14},{8,0},{10,2},{12,4},{14,6},{16,24},{18,... | collective-permute-start | bytes 786440 | tf_op jit(solution)/shard_map/ppermute | solution.py:261
  46.3 0.0 collective-permute-start
  46.3 7.9 %collective-permute-done.1.refs_5_ = bf16[256,512]{1,0:T(8,128)(2,1)S(1)} collective-permute-done((bf16[256,512]{1,0:T(8,128)(2,1)}, bf16[256,512]{1,0:T(8,128)(2,1)S(1)}, u32[]{:S(2)}, u32[]{:S(2)}) %collective-permute-start.1) | collective-permute-done | bytes 262176 | tf_op jit(solution)/shard_map/ppermute | solution.py:261
  54.2 4.9 %collective-permute-done.refs_7_ = bf16[256,512]{1,0:T(8,128)(2,1)S(1)} collective-permute-done((bf16[256,512]{1,0:T(8,128)(2,1)}, bf16[256,512]{1,0:T(8,128)(2,1)S(1)}, u32[]{:S(2)}, u32[]{:S(2)}) %collective-permute-start) | collective-permute-done | bytes 262176 | tf_op jit(solution)/shard_map/ppermute | solution.py:261
  59.1 0.0 collective-permute-done.2.refs_1_.refs_5_.refs_9_
  59.1 0.0 collective-permute-done.3.refs_2_.refs_6_.refs_10_
  59.1 0.0 collective-permute-done.4.refs_3_.refs_7_.refs_11_
  59.1 1.0 pad_maximum_fusion
  60.1 0.1 collective-permute-start.6
  60.2 0.5 collective-permute-start.5
  60.7 8.2 %collective-permute-done.5.refs_6_ = bf16[256,512]{1,0:T(8,128)(2,1)S(1)} collective-permute-done((bf16[256,512]{1,0:T(8,128)(2,1)S(1)}, bf16[256,512]{1,0:T(8,128)(2,1)S(1)}, u32[]{:S(2)}, u32[]{:S(2)}) %collective-permute-start.5) | collective-permute-done | bytes 262176 | tf_op jit(solution)/shard_map/ppermute | solution.py:261
  68.9 0.0 collective-permute-start.7
  68.9 1.5 %collective-permute-done.7.refs_9_ = bf16[256,512]{1,0:T(8,128)(2,1)S(1)} collective-permute-done((bf16[256,512]{1,0:T(8,128)(2,1)S(1)}, bf16[256,512]{1,0:T(8,128)(2,1)S(1)}, u32[]{:S(2)}, u32[]{:S(2)}) %collective-permute-start.7) | collective-permute-done | bytes 262176 | tf_op jit(solution)/shard_map/ppermute | solution.py:273
  70.4 0.0 collective-permute-done.6.refs_8_
  70.4 0.0 copy-done
  70.4 0.0 copy-done.1
  70.5 1.5 %product.1 = (f32[512,256]{1,0:T(8,128)S(1)}, bf16[512,256]{1,0:T(8,128)(2,1)S(1)}, bf16[512,256]{1,0:T(8,128)(2,1)S(1)}, bf16[512,256]{1,0:T(8,128)(2,1)S(1)}) custom-call(bf16[1168,128]{1,0:T(8,128)(2,1)S(1)} %copy-done, bf16[1168,128]{1,0:T(8,128)(2,1)S(1)} %collective-permute-done.2.refs_1_.refs_5_.refs_9_, ...), custom_call_target="tpu_custom_call" | custom-call | tf_op jit(solution)/shard_map/product/pallas_call | solution.py:139
  72.0 1.6 %collective-permute-start.8 = (bf16[512,256]{1,0:T(8,128)(2,1)S(1)}, bf16[512,256]{1,0:T(8,128)(2,1)S(1)}, u32[]{:S(2)}, u32[]{:S(2)}) collective-permute-start(bf16[512,256]{1,0:T(8,128)(2,1)S(1)} %get-tuple-element.38), channel_id=1, source_target_pairs={{0,2},{2,0},{4,6},{6,4},{8,10},{10,8},{12,14},{14,12},{16,18},{18,... | collective-permute-start | bytes 786440 | tf_op jit(solution)/shard_map/ppermute | solution.py:261
  73.6 1.5 %collective-permute-start.9 = (bf16[512,256]{1,0:T(8,128)(2,1)S(1)}, bf16[512,256]{1,0:T(8,128)(2,1)S(1)}, u32[]{:S(2)}, u32[]{:S(2)}) collective-permute-start(bf16[512,256]{1,0:T(8,128)(2,1)S(1)} %get-tuple-element.39), channel_id=1, source_target_pairs={{0,4},{2,6},{4,0},{6,2},{8,12},{10,14},{12,8},{14,10},{16,20},{18,... | collective-permute-start | bytes 786440 | tf_op jit(solution)/shard_map/ppermute | solution.py:261
  75.1 0.5 collective-permute-start.10
  75.6 5.7 %collective-permute-done.8.refs_1_ = bf16[512,256]{1,0:T(8,128)(2,1)S(1)} collective-permute-done((bf16[512,256]{1,0:T(8,128)(2,1)S(1)}, bf16[512,256]{1,0:T(8,128)(2,1)S(1)}, u32[]{:S(2)}, u32[]{:S(2)}) %collective-permute-start.8) | collective-permute-done | bytes 262176 | tf_op jit(solution)/shard_map/ppermute | solution.py:261
  81.2 6.0 %collective-permute-done.9.refs_2_ = bf16[512,256]{1,0:T(8,128)(2,1)S(1)} collective-permute-done((bf16[512,256]{1,0:T(8,128)(2,1)S(1)}, bf16[512,256]{1,0:T(8,128)(2,1)S(1)}, u32[]{:S(2)}, u32[]{:S(2)}) %collective-permute-start.9) | collective-permute-done | bytes 262176 | tf_op jit(solution)/shard_map/ppermute | solution.py:261
  87.2 0.0 collective-permute-done.10.refs_3_
  87.2 0.0 copy-start.2
  87.2 0.0 copy-start.3
  87.2 0.0 copy-start.4
  87.2 0.0 copy-start.5
  87.3 1.2 %inside.1 = (bf16[128,128]{1,0:T(8,128)(2,1)S(1)}, f32[128,128]{1,0:T(8,128)}, bf16[128,128]{1,0:T(8,128)(2,1)S(1)}, f32[128,128]{1,0:T(8,128)S(1)}, bf16[128,12...) custom-call(f32[512,256]{1,0:T(8,128)S(1)} %get-tuple-element.37.refs_0_, ...), custom_call_target="tpu_custom_call" | custom-call | tf_op jit(solution)/shard_map/inside/pallas_call | solution.py:201
  88.5 1.2 %collective-permute-start.15 = (bf16[128,128]{1,0:T(8,128)(2,1)S(1)}, bf16[128,128]{1,0:T(8,128)(2,1)S(1)}, u32[]{:S(2)}, u32[]{:S(2)}) collective-permute-start(bf16[128,128]{1,0:T(8,128)(2,1)S(1)} %get-tuple-element.43), channel_id=1, source_target_pairs={{0,2},{2,0},{4,6},{6,4},{8,10},{10,8},{12,14},{14,12},{16,18},{18,... | collective-permute-start | bytes 98312 | tf_op jit(solution)/shard_map/ppermute | solution.py:261
  89.7 0.8 collective-permute-start.16
  90.5 1.3 %collective-permute-start.14 = (bf16[128,128]{1,0:T(8,128)(2,1)S(1)}, bf16[128,128]{1,0:T(8,128)(2,1)S(1)}, u32[]{:S(2)}, u32[]{:S(2)}) collective-permute-start(bf16[128,128]{1,0:T(8,128)(2,1)S(1)} %get-tuple-element.41), channel_id=1, source_target_pairs={{8,22},{10,20},{12,18},{14,16},{9,23},{11,21},{13,19},{15,17}} | collective-permute-start | bytes 98312 | tf_op jit(solution)/shard_map/ppermute | solution.py:298
  91.8 1.3 %collective-permute-start.13 = (bf16[128,128]{1,0:T(8,128)(2,1)S(1)}, bf16[128,128]{1,0:T(8,128)(2,1)S(1)}, u32[]{:S(2)}, u32[]{:S(2)}) collective-permute-start(bf16[128,128]{1,0:T(8,128)(2,1)S(1)} %get-tuple-element.41), channel_id=1, source_target_pairs={{8,20},{10,22},{12,16},{14,18},{9,21},{11,23},{13,17},{15,19}} | collective-permute-start | bytes 98312 | tf_op jit(solution)/shard_map/ppermute | solution.py:298
  93.1 1.5 %collective-permute-start.17 = (bf16[128,128]{1,0:T(8,128)(2,1)S(1)}, bf16[128,128]{1,0:T(8,128)(2,1)S(1)}, u32[]{:S(2)}, u32[]{:S(2)}) collective-permute-start(bf16[128,128]{1,0:T(8,128)(2,1)S(1)} %get-tuple-element.45), channel_id=1, source_target_pairs={{0,6},{2,4},{4,2},{6,0},{8,14},{10,12},{12,10},{14,8},{16,22},{18,... | collective-permute-start | bytes 98312 | tf_op jit(solution)/shard_map/ppermute | solution.py:261
  94.6 0.0 collective-permute-done.15.refs_5_
  94.6 1.3 %collective-permute-start.12 = (bf16[128,128]{1,0:T(8,128)(2,1)S(1)}, bf16[128,128]{1,0:T(8,128)(2,1)S(1)}, u32[]{:S(2)}, u32[]{:S(2)}) collective-permute-start(bf16[128,128]{1,0:T(8,128)(2,1)S(1)} %get-tuple-element.41), channel_id=1, source_target_pairs={{8,18},{10,16},{12,22},{14,20},{9,19},{11,17},{13,23},{15,21}} | collective-permute-start | bytes 98312 | tf_op jit(solution)/shard_map/ppermute | solution.py:298
  95.9 0.0 collective-permute-done.16.refs_6_
  95.9 1.3 %collective-permute-start.11 = (bf16[128,128]{1,0:T(8,128)(2,1)S(1)}, bf16[128,128]{1,0:T(8,128)(2,1)S(1)}, u32[]{:S(2)}, u32[]{:S(2)}) collective-permute-start(bf16[128,128]{1,0:T(8,128)(2,1)S(1)} %get-tuple-element.41), channel_id=1, source_target_pairs={{8,16},{10,18},{12,20},{14,22},{9,17},{11,19},{13,21},{15,23}} | collective-permute-start | bytes 98312 | tf_op jit(solution)/shard_map/ppermute | solution.py:298
  97.2 1.1 %collective-permute-done.17.refs_7_ = bf16[128,128]{1,0:T(8,128)(2,1)S(1)} collective-permute-done((bf16[128,128]{1,0:T(8,128)(2,1)S(1)}, bf16[128,128]{1,0:T(8,128)(2,1)S(1)}, u32[]{:S(2)}, u32[]{:S(2)}) %collective-permute-start.17) | collective-permute-done | bytes 32800 | tf_op jit(solution)/shard_map/ppermute | solution.py:261
  98.3 0.0 collective-permute-done.14.refs_3_
  98.3 1.4 %collective-permute-done.13.refs_2_ = bf16[128,128]{1,0:T(8,128)(2,1)S(1)} collective-permute-done((bf16[128,128]{1,0:T(8,128)(2,1)S(1)}, bf16[128,128]{1,0:T(8,128)(2,1)S(1)}, u32[]{:S(2)}, u32[]{:S(2)}) %collective-permute-start.13) | collective-permute-done | bytes 32800 | tf_op jit(solution)/shard_map/ppermute | solution.py:298
  99.8 2.5 %collective-permute-done.12.refs_1_ = bf16[128,128]{1,0:T(8,128)(2,1)S(1)} collective-permute-done((bf16[128,128]{1,0:T(8,128)(2,1)S(1)}, bf16[128,128]{1,0:T(8,128)(2,1)S(1)}, u32[]{:S(2)}, u32[]{:S(2)}) %collective-permute-start.12) | collective-permute-done | bytes 32800 | tf_op jit(solution)/shard_map/ppermute | solution.py:298
  102.3 0.4 collective-permute-done.11.refs_0_
  102.7 0.0 copy-done.2
  102.7 0.0 copy-done.3
  102.7 0.0 copy-done.4
  102.7 0.0 copy-done.5
  102.7 1.0 finish.1
Async XLA Ops:
  41.2 29.3 %copy-start = (bf16[1168,128]{1,0:T(8,128)(2,1)S(1)}, bf16[1168,128]{1,0:T(8,128)(2,1)}, u32[]{:S(2)}) copy-start(bf16[1168,128]{1,0:T(8,128)(2,1)} %get-tuple-element.31.refs_0_.refs_4_.refs_8_) | copy-start | bytes 897028
  41.2 29.3 %copy-start.1 = (bf16[256,512]{1,0:T(8,128)(2,1)S(1)}, bf16[256,512]{1,0:T(8,128)(2,1)}, u32[]{:S(2)}) copy-start(bf16[256,512]{1,0:T(8,128)(2,1)} %get-tuple-element.26.refs_4_) | copy-start | bytes 786436
  41.2 17.9 %collective-permute-start.2 = (bf16[1168,128]{1,0:T(8,128)(2,1)}, bf16[1168,128]{1,0:T(8,128)(2,1)S(1)}, u32[]{:S(2)}, u32[]{:S(2)}) collective-permute-start(bf16[1168,128]{1,0:T(8,128)(2,1)} %get-tuple-element.28.refs_9_), channel_id=1, source_target_pairs={{0,2},{2,0},{4,6},{6,4},{8,10},{10,8},{12,14},{14,12},{16,18},{18,... | collective-permute-start | bytes 897032 | tf_op jit(solution)/shard_map/ppermute | solution.py:261
  42.8 16.3 %collective-permute-start.3 = (bf16[1168,128]{1,0:T(8,128)(2,1)}, bf16[1168,128]{1,0:T(8,128)(2,1)S(1)}, u32[]{:S(2)}, u32[]{:S(2)}) collective-permute-start(bf16[1168,128]{1,0:T(8,128)(2,1)} %get-tuple-element.29.refs_10_), channel_id=1, source_target_pairs={{0,4},{2,6},{4,0},{6,2},{8,12},{10,14},{12,8},{14,10},{16,20},{18,... | collective-permute-start | bytes 897032 | tf_op jit(solution)/shard_map/ppermute | solution.py:261
  44.3 14.8 %collective-permute-start.4 = (bf16[1168,128]{1,0:T(8,128)(2,1)}, bf16[1168,128]{1,0:T(8,128)(2,1)S(1)}, u32[]{:S(2)}, u32[]{:S(2)}) collective-permute-start(bf16[1168,128]{1,0:T(8,128)(2,1)} %get-tuple-element.30.refs_11_), channel_id=1, source_target_pairs={{0,6},{2,4},{4,2},{6,0},{8,14},{10,12},{12,10},{14,8},{16,22},{18,... | collective-permute-start | bytes 897032 | tf_op jit(solution)/shard_map/ppermute | solution.py:261
  44.8 9.5 %collective-permute-start.1 = (bf16[256,512]{1,0:T(8,128)(2,1)}, bf16[256,512]{1,0:T(8,128)(2,1)S(1)}, u32[]{:S(2)}, u32[]{:S(2)}) collective-permute-start(bf16[256,512]{1,0:T(8,128)(2,1)} %get-tuple-element.26.refs_4_), channel_id=1, source_target_pairs={{0,8},{2,10},{4,12},{6,14},{8,0},{10,2},{12,4},{14,6},{16,24},{18,... | collective-permute-start | bytes 786440 | tf_op jit(solution)/shard_map/ppermute | solution.py:261
  46.3 12.8 %collective-permute-start = (bf16[256,512]{1,0:T(8,128)(2,1)}, bf16[256,512]{1,0:T(8,128)(2,1)S(1)}, u32[]{:S(2)}, u32[]{:S(2)}) collective-permute-start(bf16[256,512]{1,0:T(8,128)(2,1)} %get-tuple-element.26.refs_4_), channel_id=1, source_target_pairs={{0,24},{2,26},{4,28},{6,30},{8,16},{10,18},{12,20},{14,22},{16,8},... | collective-permute-start | bytes 786440 | tf_op jit(solution)/shard_map/ppermute | solution.py:261
  60.1 10.3 %collective-permute-start.6 = (bf16[768,512]{1,0:T(8,128)(2,1)S(1)}, bf16[768,512]{1,0:T(8,128)(2,1)S(1)}, u32[]{:S(2)}, u32[]{:S(2)}) collective-permute-start(bf16[768,512]{1,0:T(8,128)(2,1)S(1)} %pad_maximum_fusion), channel_id=1, source_target_pairs={{0,1},{1,0},{2,3},{3,2},{4,5},{5,4},{6,7},{7,6},{8,9},{9,8},{10,11... | collective-permute-start | bytes 2359304 | tf_op jit(solution)/shard_map/ppermute | solution.py:273
  60.2 8.7 %collective-permute-start.5 = (bf16[256,512]{1,0:T(8,128)(2,1)S(1)}, bf16[256,512]{1,0:T(8,128)(2,1)S(1)}, u32[]{:S(2)}, u32[]{:S(2)}) collective-permute-start(bf16[256,512]{1,0:T(8,128)(2,1)S(1)} %collective-permute-done.refs_7_), channel_id=1, source_target_pairs={{0,8},{2,10},{4,12},{6,14},{8,0},{10,2},{12,4},{14,6},{16,24},{18,... | collective-permute-start | bytes 786440 | tf_op jit(solution)/shard_map/ppermute | solution.py:261
  68.9 1.5 %collective-permute-start.7 = (bf16[256,512]{1,0:T(8,128)(2,1)S(1)}, bf16[256,512]{1,0:T(8,128)(2,1)S(1)}, u32[]{:S(2)}, u32[]{:S(2)}) collective-permute-start(bf16[256,512]{1,0:T(8,128)(2,1)S(1)} %collective-permute-done.5.refs_6_), channel_id=1, source_target_pairs={{0,1},{1,0},{2,3},{3,2},{4,5},{5,4},{6,7},{7,6},{8,9},{9,8},{10,11... | collective-permute-start | bytes 786440 | tf_op jit(solution)/shard_map/ppermute | solution.py:273
  72.0 9.2 %collective-permute-start.8 = (bf16[512,256]{1,0:T(8,128)(2,1)S(1)}, bf16[512,256]{1,0:T(8,128)(2,1)S(1)}, u32[]{:S(2)}, u32[]{:S(2)}) collective-permute-start(bf16[512,256]{1,0:T(8,128)(2,1)S(1)} %get-tuple-element.38), channel_id=1, source_target_pairs={{0,2},{2,0},{4,6},{6,4},{8,10},{10,8},{12,14},{14,12},{16,18},{18,... | collective-permute-start | bytes 786440 | tf_op jit(solution)/shard_map/ppermute | solution.py:261
  73.6 13.7 %collective-permute-start.9 = (bf16[512,256]{1,0:T(8,128)(2,1)S(1)}, bf16[512,256]{1,0:T(8,128)(2,1)S(1)}, u32[]{:S(2)}, u32[]{:S(2)}) collective-permute-start(bf16[512,256]{1,0:T(8,128)(2,1)S(1)} %get-tuple-element.39), channel_id=1, source_target_pairs={{0,4},{2,6},{4,0},{6,2},{8,12},{10,14},{12,8},{14,10},{16,20},{18,... | collective-permute-start | bytes 786440 | tf_op jit(solution)/shard_map/ppermute | solution.py:261
  75.1 12.2 %collective-permute-start.10 = (bf16[512,256]{1,0:T(8,128)(2,1)S(1)}, bf16[512,256]{1,0:T(8,128)(2,1)S(1)}, u32[]{:S(2)}, u32[]{:S(2)}) collective-permute-start(bf16[512,256]{1,0:T(8,128)(2,1)S(1)} %get-tuple-element.40), channel_id=1, source_target_pairs={{0,6},{2,4},{4,2},{6,0},{8,14},{10,12},{12,10},{14,8},{16,22},{18,... | collective-permute-start | bytes 786440 | tf_op jit(solution)/shard_map/ppermute | solution.py:261
  87.2 15.4 %copy-start.2 = (bf16[1168,128]{1,0:T(8,128)(2,1)S(1)}, bf16[1168,128]{1,0:T(8,128)(2,1)}, u32[]{:S(2)}) copy-start(bf16[1168,128]{1,0:T(8,128)(2,1)} %get-tuple-element.28.refs_9_) | copy-start | bytes 897028
  87.2 15.4 %copy-start.3 = (bf16[1168,128]{1,0:T(8,128)(2,1)S(1)}, bf16[1168,128]{1,0:T(8,128)(2,1)}, u32[]{:S(2)}) copy-start(bf16[1168,128]{1,0:T(8,128)(2,1)} %get-tuple-element.29.refs_10_) | copy-start | bytes 897028
  87.2 15.4 %copy-start.4 = (bf16[1168,128]{1,0:T(8,128)(2,1)S(1)}, bf16[1168,128]{1,0:T(8,128)(2,1)}, u32[]{:S(2)}) copy-start(bf16[1168,128]{1,0:T(8,128)(2,1)} %get-tuple-element.30.refs_11_) | copy-start | bytes 897028
  87.2 15.4 %copy-start.5 = (f32[512]{0:T(512)S(1)}, f32[512]{0:T(512)}, u32[]{:S(2)}) copy-start(f32[512]{0:T(512)} %param.11) | copy-start | bytes 6148
  88.5 6.1 %collective-permute-start.15 = (bf16[128,128]{1,0:T(8,128)(2,1)S(1)}, bf16[128,128]{1,0:T(8,128)(2,1)S(1)}, u32[]{:S(2)}, u32[]{:S(2)}) collective-permute-start(bf16[128,128]{1,0:T(8,128)(2,1)S(1)} %get-tuple-element.43), channel_id=1, source_target_pairs={{0,2},{2,0},{4,6},{6,4},{8,10},{10,8},{12,14},{14,12},{16,18},{18,... | collective-permute-start | bytes 98312 | tf_op jit(solution)/shard_map/ppermute | solution.py:261
  89.7 6.2 %collective-permute-start.16 = (bf16[128,128]{1,0:T(8,128)(2,1)S(1)}, bf16[128,128]{1,0:T(8,128)(2,1)S(1)}, u32[]{:S(2)}, u32[]{:S(2)}) collective-permute-start(bf16[128,128]{1,0:T(8,128)(2,1)S(1)} %get-tuple-element.44), channel_id=1, source_target_pairs={{0,4},{2,6},{4,0},{6,2},{8,12},{10,14},{12,8},{14,10},{16,20},{18,... | collective-permute-start | bytes 98312 | tf_op jit(solution)/shard_map/ppermute | solution.py:261
  90.5 7.8 %collective-permute-start.14 = (bf16[128,128]{1,0:T(8,128)(2,1)S(1)}, bf16[128,128]{1,0:T(8,128)(2,1)S(1)}, u32[]{:S(2)}, u32[]{:S(2)}) collective-permute-start(bf16[128,128]{1,0:T(8,128)(2,1)S(1)} %get-tuple-element.41), channel_id=1, source_target_pairs={{8,22},{10,20},{12,18},{14,16},{9,23},{11,21},{13,19},{15,17}} | collective-permute-start | bytes 98312 | tf_op jit(solution)/shard_map/ppermute | solution.py:298
  91.8 8.0 %collective-permute-start.13 = (bf16[128,128]{1,0:T(8,128)(2,1)S(1)}, bf16[128,128]{1,0:T(8,128)(2,1)S(1)}, u32[]{:S(2)}, u32[]{:S(2)}) collective-permute-start(bf16[128,128]{1,0:T(8,128)(2,1)S(1)} %get-tuple-element.41), channel_id=1, source_target_pairs={{8,20},{10,22},{12,16},{14,18},{9,21},{11,23},{13,17},{15,19}} | collective-permute-start | bytes 98312 | tf_op jit(solution)/shard_map/ppermute | solution.py:298
  93.1 5.2 %collective-permute-start.17 = (bf16[128,128]{1,0:T(8,128)(2,1)S(1)}, bf16[128,128]{1,0:T(8,128)(2,1)S(1)}, u32[]{:S(2)}, u32[]{:S(2)}) collective-permute-start(bf16[128,128]{1,0:T(8,128)(2,1)S(1)} %get-tuple-element.45), channel_id=1, source_target_pairs={{0,6},{2,4},{4,2},{6,0},{8,14},{10,12},{12,10},{14,8},{16,22},{18,... | collective-permute-start | bytes 98312 | tf_op jit(solution)/shard_map/ppermute | solution.py:261
  94.6 7.6 %collective-permute-start.12 = (bf16[128,128]{1,0:T(8,128)(2,1)S(1)}, bf16[128,128]{1,0:T(8,128)(2,1)S(1)}, u32[]{:S(2)}, u32[]{:S(2)}) collective-permute-start(bf16[128,128]{1,0:T(8,128)(2,1)S(1)} %get-tuple-element.41), channel_id=1, source_target_pairs={{8,18},{10,16},{12,22},{14,20},{9,19},{11,17},{13,23},{15,21}} | collective-permute-start | bytes 98312 | tf_op jit(solution)/shard_map/ppermute | solution.py:298
  95.9 6.8 %collective-permute-start.11 = (bf16[128,128]{1,0:T(8,128)(2,1)S(1)}, bf16[128,128]{1,0:T(8,128)(2,1)S(1)}, u32[]{:S(2)}, u32[]{:S(2)}) collective-permute-start(bf16[128,128]{1,0:T(8,128)(2,1)S(1)} %get-tuple-element.41), channel_id=1, source_target_pairs={{8,16},{10,18},{12,20},{14,22},{9,17},{11,19},{13,21},{15,23}} | collective-permute-start | bytes 98312 | tf_op jit(solution)/shard_map/ppermute | solution.py:298

commit v3 on v1

v3 whole, which is shorter than its diff:
```python
import functools

import jax
import jax.numpy as jnp
from jax import lax
from jax.experimental import pallas as pl
from jax.experimental.pallas import tpu as pltpu
from jax.sharding import PartitionSpec as P

HEAD = 128
BF, F32 = jnp.bfloat16, jnp.float32
DOC_BLOCKS = {16: 8, 64: 16}
MARKS = 16


def phi(u):
    return jnp.where(u > 0, u + 1.0, jnp.exp(jnp.minimum(u, 0.0)))


def aligned(index, size):
    return pl.ds(pl.multiple_of(index * size, size), size)


def inner_outer(heads):
    me = lax.axis_index("ctx")
    return lax.rem(me, heads), lax.div(me, heads)


def limit(mib):
    return pltpu.CompilerParams(vmem_limit_bytes=mib * 2**20)


def pack_kernel(heads, tok_ref, query_ref, flag_ref, *refs):
    out_refs, sems = refs[:heads], refs[heads]
    inner, _ = inner_outer(heads)
    count, depth = tok_ref.shape
    squares = depth // (heads * HEAD)
    copies = []
    for k in list(range(1, heads)) + [0]:
        to = jnp.bitwise_xor(inner, k)
        for i in range(squares):
            at = ((i // 2) * heads + to) * 2 + i % 2
            copy = pltpu.make_async_copy(
                tok_ref.at[:, aligned(at, HEAD)],
                out_refs[k].at[i * count : (i + 1) * count, :],
                sems.at[k, i],
            )
            copy.start()
            copies.append(copy)
    marks = jnp.broadcast_to(flag_ref[...].astype(F32), (MARKS, count)).astype(BF)
    for k, out in enumerate(out_refs):
        own = query_ref[:, aligned(jnp.bitwise_xor(inner, k), HEAD)].astype(F32)
        out[squares * count : (squares + 1) * count, :] = phi(own).astype(BF)
        out[(squares + 1) * count :, :] = marks
    for copy in copies:
        copy.wait()


def pack(tokens, queries, flags, heads, share):
    count, depth = tokens.shape
    squares = depth // (heads * HEAD)
    if share == 2 * HEAD:
        shape = ((squares + 1) * count + MARKS, HEAD)
        vmem = pl.BlockSpec(memory_space=pltpu.VMEM)
        return pl.pallas_call(
            functools.partial(pack_kernel, heads),
            in_specs=[pl.BlockSpec(memory_space=pl.ANY), vmem, vmem],
            out_specs=[vmem] * heads,
            out_shape=[jax.ShapeDtypeStruct(shape, BF)] * heads,
            scratch_shapes=[pltpu.SemaphoreType.DMA((heads, squares))],
            compiler_params=limit(60),
            name="pack",
        )(tokens, queries, flags)
    inner, _ = inner_outer(heads)
    by_inner = tokens.reshape(count, -1, heads, share).transpose(2, 0, 1, 3)
    by_inner = by_inner.reshape(heads, count, squares, HEAD).transpose(0, 2, 1, 3).reshape(heads, -1, HEAD)
    query = phi(queries.astype(F32)).astype(BF).reshape(count, heads, HEAD).transpose(1, 0, 2)
    marks = jnp.broadcast_to(flags.astype(BF), (MARKS, count))
    out = []
    for k in range(heads):
        to = jnp.bitwise_xor(inner, k)
        parts = [lax.dynamic_index_in_dim(a, to, 0, False) for a in (by_inner, query)]
        out.append(jnp.concatenate(parts + [marks], axis=0))
    return out


def shape(rows, cols, dtype):
    return jax.ShapeDtypeStruct((rows, cols), dtype)


def assemble_kernel(heads, count, split, *refs):
    x_refs = refs[:heads]
    tok, query, first, seg_row, seg_col, marks = refs[heads:]
    inner, outer = inner_outer(heads)
    squares = tok.shape[1] // HEAD
    total = heads * count
    for k, x in enumerate(x_refs):
        place = jnp.bitwise_xor(inner, k)
        rows = aligned(place, count)
        for i in range(squares):
            at = i
            if split:
                core = lax.axis_index("fsdp")
                at = jnp.bitwise_xor(outer, i // 2) * 2 + jnp.bitwise_xor(core, i % 2)
            tok[rows, i * HEAD : (i + 1) * HEAD] = x[aligned(at, count), :]
        query[rows, :] = x[squares * count : (squares + 1) * count, :]
        marks[:, rows] = x[(squares + 1) * count :, :]
    early = lax.broadcasted_iota(jnp.int32, (total, total), 0)
    late = lax.broadcasted_iota(jnp.int32, (total, total), 1)
    upto = jnp.where(early <= late, 1.0, 0.0).astype(BF)
    seg = jnp.dot(marks[...], upto, preferred_element_type=F32)[:1, :]
    seg_row[...] = jnp.broadcast_to(seg, seg_row.shape)
    col = jnp.broadcast_to(seg, (HEAD, total)).T
    seg_col[...] = col
    first[...] = jnp.where(col == 0.0, query[...].astype(F32), 0.0).astype(BF)


def assemble(received, heads, count, depth, split):
    total = heads * count
    return pl.pallas_call(
        functools.partial(assemble_kernel, heads, count, split),
        out_shape=[
            shape(total, depth, BF),
            shape(total, HEAD, BF),
            shape(total, HEAD, BF),
            shape(8, total, F32),
            shape(total, HEAD, F32),
        ],
        scratch_shapes=[pltpu.VMEM((MARKS, total), BF)],
        compiler_params=limit(16),
        cost_estimate=pl.CostEstimate(flops=4 * 10**9, bytes_accessed=0, transcendentals=0),
        name="assemble",
    )(*received)


def product_kernel(heads, places, tok, *refs):
    w_refs, out_refs = refs[:-heads], refs[-heads:]
    inner, _ = inner_outer(heads)
    half = tok.shape[1] // len(places)
    for k in list(range(1, heads)) + [0]:
        cols = aligned(jnp.bitwise_xor(inner, k), HEAD)
        key = jnp.concatenate([w_refs[j][at : at + half, cols] for j, at in places], axis=0)
        value = jnp.concatenate([w_refs[j][at + half : at + 2 * half, cols] for j, at in places], axis=0)
        w = jnp.concatenate([key, value], axis=1)
        out = out_refs[k]
        out[...] = jnp.dot(tok[...], w, preferred_element_type=F32).astype(out.dtype)


def product(tok, ws, heads, places):
    total = tok.shape[0]
    return pl.pallas_call(
        functools.partial(product_kernel, heads, places),
        out_shape=[shape(total, 2 * HEAD, F32)] + [shape(total, 2 * HEAD, BF)] * (heads - 1),
        compiler_params=limit(24),
        name="product",
    )(tok, *ws)


def state_kernel(heads, *refs):
    parts, seg_col = refs[:heads], refs[heads]
    state_ref, key_ref, value_ref = refs[heads + 1 :]
    proj = parts[0][...]
    for part in parts[1:]:
        proj = proj + part[...].astype(F32)
    key = phi(proj[:, :HEAD]).astype(BF)
    value = proj[:, HEAD:].astype(BF)
    last = seg_col[seg_col.shape[0] - 1 :, :]
    tail = jnp.where(seg_col[...] == last, value.astype(F32), 0.0).astype(BF)
    state = lax.dot_general(key, tail, (((0,), (0,)), ((), ())), preferred_element_type=F32)
    state_ref[...] = state.astype(state_ref.dtype)
    key_ref[...] = key
    value_ref[...] = value


def leave(parts, seg_col, heads, kind):
    total = seg_col.shape[0]
    return pl.pallas_call(
        functools.partial(state_kernel, heads),
        out_shape=[shape(HEAD, HEAD, kind), shape(total, HEAD, BF), shape(total, HEAD, BF)],
        compiler_params=limit(16),
        name="state",
    )(*parts, seg_col)


def within_kernel(heads, query, key, value, seg_row, seg_col, out_ref):
    total = query.shape[0]
    count = total // heads
    for i in range(heads):
        rows, width = slice(i * count, (i + 1) * count), (i + 1) * count
        scores = lax.dot_general(
            query[rows, :], key[:width, :], (((1,), (1,)), ((), ())), preferred_element_type=F32
        )
        own = jnp.concatenate([seg_col[rows, :]] * (i + 1), axis=1)
        early = lax.broadcasted_iota(jnp.int32, (count, width), 1)
        late = lax.broadcasted_iota(jnp.int32, (count, width), 0) + i * count
        allowed = (own == seg_row[:1, :width]) & (early <= late)
        scores = jnp.where(allowed, scores, 0.0).astype(BF)
        out_ref[rows, :] = jnp.dot(scores, value[:width, :], preferred_element_type=F32)


def within(query, key, value, seg_row, seg_col, heads):
    return pl.pallas_call(
        functools.partial(within_kernel, heads),
        out_shape=shape(query.shape[0], HEAD, F32),
        compiler_params=limit(16),
        cost_estimate=pl.CostEstimate(flops=2 * 10**9, bytes_accessed=0, transcendentals=0),
        name="within",
    )(query, key, value, seg_row, seg_col)


def finish_kernel(heads, carried, first, inside, gain, *refs):
    out_refs, done = refs[:-1], refs[-1]
    inner, _ = inner_outer(heads)
    count = out_refs[0].shape[0]
    mixed = inside[...] + jnp.dot(first[...], carried[...], preferred_element_type=F32)
    scale = lax.rsqrt(jnp.mean(mixed * mixed, axis=-1, keepdims=True) + 1e-06)
    done[...] = (mixed * scale * gain[:, aligned(inner, HEAD)]).astype(BF)
    for k, out in enumerate(out_refs):
        out[...] = done[aligned(jnp.bitwise_xor(inner, k), count), :]


def finish(carried, first, inside, gain, heads):
    total = first.shape[0]
    return pl.pallas_call(
        functools.partial(finish_kernel, heads),
        out_shape=[shape(total // heads, HEAD, BF)] * heads,
        scratch_shapes=[pltpu.VMEM((total, HEAD), BF)],
        compiler_params=limit(8),
        name="finish",
    )(carried, first, inside, gain)


def join_kernel(heads, *refs):
    inner, _ = inner_outer(heads)
    for k, part in enumerate(refs[:-1]):
        refs[-1][:, aligned(jnp.bitwise_xor(inner, k), HEAD)] = part[...]


def join(parts, heads):
    return pl.pallas_call(
        functools.partial(join_kernel, heads),
        out_shape=shape(parts[0].shape[0], heads * HEAD, BF),
        compiler_params=limit(8),
        name="join",
    )(*parts)


def on_device(n_ctx, fsdp, tokens, queries, flags, w_key, w_value, norm_gain):
    _, count, depth = tokens.shape
    rows, width = w_key.shape
    heads = width // HEAD
    outer = n_ctx // heads

    def swap(a, mask):
        return lax.ppermute(a, "ctx", [(i, i ^ mask) for i in range(n_ctx)])

    split = outer == 4 and fsdp == 2 and rows == HEAD
    if split:
        weights = jnp.concatenate([w_key, w_value], axis=0)
        far = swap(weights, 3 * heads)
        near = swap(weights, heads)
    packed = pack(tokens[0], queries[0], flags, heads, fsdp * rows)
    received = [packed[0]] + [swap(packed[k], k) for k in range(1, heads)]
    tok, query, first, seg_row, seg_col = assemble(received, heads, count, depth // heads, split)
    if split:
        panels = []
        for piece in [weights, near, swap(far, heads), far]:
            panels += [piece, lax.ppermute(piece, "fsdp", [(0, 1), (1, 0)])]
    else:
        groups = [[o * heads + q for o in range(outer)] for q in range(heads)]
        chip = [lax.all_gather(w, "fsdp", axis=0, tiled=True) for w in (w_key, w_value)]
        panels = [lax.all_gather(w, "ctx", axis=0, tiled=True, axis_index_groups=groups) for w in chip]
        panels = [jnp.concatenate(panels, axis=0)]
    partial = product(tok, panels, heads, [(j, 0) for j in range(len(panels))])
    parts = [partial[0]] + [swap(partial[k], k) for k in range(1, heads)]

    doc = DOC_BLOCKS.get(n_ctx, 2 * n_ctx)
    starts = [b for b in range(n_ctx) if b % doc == doc // 2]
    pairs = [
        (b, b + heads)
        for b in range(n_ctx - heads)
        if (b // heads + 1) * heads not in starts
    ]
    rounds = max(1, min(doc // heads, outer) - 1)
    state, key, value = leave(parts, seg_col, heads, BF if rounds == 1 else F32)
    carried = lax.ppermute(state.astype(BF), "ctx", pairs)
    keep = (seg_col[-1:, :] == 0.0).astype(F32)
    for _ in range(rounds - 1):
        carried = lax.ppermute((state + keep * carried.astype(F32)).astype(BF), "ctx", pairs)
    inside = within(query, key, value, seg_row, seg_col, heads)
    done = finish(carried, first, inside, norm_gain.reshape(1, width), heads)
    return join([done[0]] + [swap(done[k], k) for k in range(1, heads)], heads)[None]


def solution(mesh):
    n_ctx, fsdp = mesh.shape["ctx"], mesh.shape["fsdp"]
    in_specs = (
        P("fsdp", "ctx", None),
        P("fsdp", "ctx", None),
        P("fsdp", "ctx"),
        P(("ctx", "fsdp"), None),
        P(("ctx", "fsdp"), None),
        P(),
    )
    return jax.shard_map(
        functools.partial(on_device, n_ctx, fsdp),
        mesh=mesh,
        in_specs=in_specs,
        out_specs=P("fsdp", "ctx", None),
        check_vma=False,
    )
```

time: 67.5 us -> 55.2 us (0.82)
  waiting for transfers between devices: 38.6 us -> 30.9 us
  local copies, waits for them, and re-layouts: 4.6 us -> 1.94 us
  Pallas kernels: 8.61 us -> 7.34 us
  starting transfers between devices: 15.1 us -> 14.1 us
    ppermute x12, waiting for transfers between devices: 34.1 us -> 27.2 us  [swap(): return lax.ppermute(a, 'ctx', [(i, i ^ mask) for i in range(n_ctx)])]
    unnamed x17 -> x7, local copies, waits for them, and re-layouts: 3.59 us -> 1.93 us
    pallas_call x5 -> x7, Pallas kernels: 8.61 us -> 7.34 us  [the longest x1 3.43 us: pack(): pl.pallas_call(functools.partial(pack_kernel, heads), in_specs=[pl.BlockS...]
    ppermute x12, starting transfers between devices: 13.4 us -> 12.3 us  [swap(): return lax.ppermute(a, 'ctx', [(i, i ^ mask) for i in range(n_ctx)])]
    reshape x2 -> x0, local copies, waits for them, and re-layouts: 1.01 us -> none  [on_device(): by_head = [w.reshape(rows, heads, HEAD) for w in (w_key, w_value)]]
    ppermute x1, waiting for transfers between devices: 4.51 us -> 3.73 us  [on_device(): carried = lax.ppermute(state.astype(BF), 'ctx', pairs)]
  transfers between devices with their start and end apart: 17 -> 17, of which waited for: 10 -> 10; matrix products, arithmetic and copies ran while one was open for 0% -> 0% of each run, Pallas kernels for 4% -> 9%
where the time goes in v3:
time: 55.2 us; the launch traced here: 54.4 us
  waiting for transfers between devices  30.9 us (56%)
  starting transfers between devices  14.1 us (26%)
  Pallas kernels  7.34 us (13%)
  local copies, waits for them, and re-layouts  1.94 us (4%)
    ppermute x12, waiting for transfers between devices, swap(): return lax.ppermute(a, 'ctx', [(i, i ^ mask) for i in range(n_ctx)])  27.2 us
    ppermute x12, starting transfers between devices, swap(): return lax.ppermute(a, 'ctx', [(i, i ^ mask) for i in range(n_ctx)])  12.3 us
    ppermute x1, waiting for transfers between devices, on_device(): carried = lax.ppermute(state.astype(BF), 'ctx', pairs)  3.73 us
    pallas_call x1, Pallas kernels, pack(): pl.pallas_call(functools.partial(pack_kernel, heads), in_specs=[pl.BlockS...  3.43 us
    unnamed x7, local copies, waits for them, and re-layouts  1.93 us
    ppermute x1, starting transfers between devices, on_device(): carried = lax.ppermute(state.astype(BF), 'ctx', pairs)  1.29 us
    pallas_call x1, Pallas kernels, product(): pl.pallas_call(functools.partial(product_kernel, heads, places), out_shap...  1.29 us
  transfers between devices with their start and end apart: 17, of which 10 were waited for; matrix products, arithmetic and copies ran while one was open for 0% of the time, Pallas kernels for 9%

profile of v3, /device:TPU:16, one launch (start us, length us, event | category | flops | bytes accessed | tf_op | source)
XLA Modules:
  0.0 54.4 jit_solution(18258746817896112082)
XLA Ops:
  0.0 0.0 copy-start.2
  0.0 0.9 %constant_dynamic-update-slice_fusion.1 = bf16[256,512]{1,0:T(8,128)(2,1)S(1)} fusion(bf16[128,512]{1,0:T(8,128)(2,1)} %param.9), kind=kLoop, calls=%fused_computation.1 | loop fusion | bytes 262144
  1.0 0.0 copy-done.2
  1.0 0.5 collective-permute-start.6
  1.5 3.4 %pack.1 = (bf16[1168,128]{1,0:T(8,128)(2,1)}, bf16[1168,128]{1,0:T(8,128)(2,1)}, bf16[1168,128]{1,0:T(8,128)(2,1)}, bf16[1168,128]{1,0:T(8,128)(2,1)}) custom-call(bf16[128,4096]{1,0:T(8,128)(2,1)} %bitcast.5, bf16[128,512]{1,0:T(8,128)(2,1)} %bitcast.6, s32[1,128]{1,0:T(1,128)} %flag_ref.1), custom_call_target="tpu_custom_call" | custom-call | tf_op jit(solution)/shard_map/pack/pallas_call | solution.py:65
  4.9 1.6 %collective-permute-start = (bf16[1168,128]{1,0:T(8,128)(2,1)}, bf16[1168,128]{1,0:T(8,128)(2,1)S(1)}, u32[]{:S(2)}, u32[]{:S(2)}) collective-permute-start(bf16[1168,128]{1,0:T(8,128)(2,1)} %get-tuple-element.26), channel_id=1, source_target_pairs={{0,2},{2,0},{4,6},{6,4},{8,10},{10,8},{12,14},{14,12},{16,18},{18,... | collective-permute-start | bytes 897032 | tf_op jit(solution)/shard_map/ppermute | solution.py:255
  6.5 1.5 %collective-permute-start.1 = (bf16[1168,128]{1,0:T(8,128)(2,1)}, bf16[1168,128]{1,0:T(8,128)(2,1)S(1)}, u32[]{:S(2)}, u32[]{:S(2)}) collective-permute-start(bf16[1168,128]{1,0:T(8,128)(2,1)} %get-tuple-element.27), channel_id=1, source_target_pairs={{0,4},{2,6},{4,0},{6,2},{8,12},{10,14},{12,8},{14,10},{16,20},{18,... | collective-permute-start | bytes 897032 | tf_op jit(solution)/shard_map/ppermute | solution.py:255
  8.0 0.5 collective-permute-start.2
  8.5 1.1 %collective-permute-start.4 = (bf16[256,512]{1,0:T(8,128)(2,1)S(1)}, bf16[256,512]{1,0:T(8,128)(2,1)S(1)}, u32[]{:S(2)}, u32[]{:S(2)}) collective-permute-start(bf16[256,512]{1,0:T(8,128)(2,1)S(1)} %constant_dynamic-update-slice_fusion.refs_0_), channel_id=1, source_target_pairs={{0,8},{2,10},{4,12},{6,14},{8,0},{10,2},{12,4},{14,6},{16,24},{18,... | collective-permute-start | bytes 786440 | tf_op jit(solution)/shard_map/ppermute | solution.py:255
  9.6 5.1 %collective-permute-done.6.refs_6_ = bf16[256,512]{1,0:T(8,128)(2,1)S(1)} collective-permute-done((bf16[256,512]{1,0:T(8,128)(2,1)S(1)}, bf16[256,512]{1,0:T(8,128)(2,1)S(1)}, u32[]{:S(2)}, u32[]{:S(2)}) %collective-permute-start.6) | collective-permute-done | bytes 262176 | tf_op jit(solution)/shard_map/ppermute | solution.py:255
  14.7 0.0 collective-permute-start.7
  14.7 1.7 %collective-permute-done.4.refs_2_ = bf16[256,512]{1,0:T(8,128)(2,1)S(1)} collective-permute-done((bf16[256,512]{1,0:T(8,128)(2,1)S(1)}, bf16[256,512]{1,0:T(8,128)(2,1)S(1)}, u32[]{:S(2)}, u32[]{:S(2)}) %collective-permute-start.4) | collective-permute-done | bytes 262176 | tf_op jit(solution)/shard_map/ppermute | solution.py:255
  16.4 0.0 collective-permute-start.3
  16.4 0.0 collective-permute-done.refs_1_
  16.4 0.5 collective-permute-start.9
  16.9 4.5 %collective-permute-done.1.refs_2_ = bf16[1168,128]{1,0:T(8,128)(2,1)S(1)} collective-permute-done((bf16[1168,128]{1,0:T(8,128)(2,1)}, bf16[1168,128]{1,0:T(8,128)(2,1)S(1)}, u32[]{:S(2)}, u32[]{:S(2)}) %collective-permute-start.1) | collective-permute-done | bytes 299040 | tf_op jit(solution)/shard_map/ppermute | solution.py:255
  21.4 0.0 collective-permute-start.5
  21.4 0.5 collective-permute-done.7.refs_4_
  21.9 0.0 collective-permute-start.8
  21.9 0.0 collective-permute-done.2.refs_3_
  21.9 0.0 copy-start.1
  21.9 1.0 %copy-done.1 = bf16[1168,128]{1,0:T(8,128)(2,1)S(1)} copy-done((bf16[1168,128]{1,0:T(8,128)(2,1)S(1)}, bf16[1168,128]{1,0:T(8,128)(2,1)}, u32[]{:S(2)}) %copy-start.1) | copy-done | bytes 299032
  22.9 0.5 %assemble.1 = (bf16[512,1024]{1,0:T(8,128)(2,1)S(1)}, bf16[512,128]{1,0:T(8,128)(2,1)S(1)}, bf16[512,128]{1,0:T(8,128)(2,1)S(1)}, f32[8,512]{1,0:T(8,128)S(1)}, f32[512,128]{1,0:T(8,128)S(1)}) custom-call(bf16[1168,128]{1,0:T(8,128)(2,1)S(1)} %copy-done.1, bf16[1168,128]{1,0:T(8,128)(2,1)S(1)} %collective-permute-done.refs_1_, ...), custom_call_target="tpu_custom_call" | custom-call | flops 4000000000 | tf_op jit(solution)/shard_map/assemble/pallas_call | solution.py:120
  23.4 0.0 collective-permute-done.3.refs_1_
  23.4 0.0 collective-permute-done.9.refs_7_
  23.5 0.0 collective-permute-done.5.refs_3_
  23.5 0.0 collective-permute-done.8.refs_5_
  23.5 1.3 %product.1 = (f32[512,256]{1,0:T(8,128)S(1)}, bf16[512,256]{1,0:T(8,128)(2,1)S(1)}, bf16[512,256]{1,0:T(8,128)(2,1)S(1)}, bf16[512,256]{1,0:T(8,128)(2,1)S(1)}) custom-call(bf16[512,1024]{1,0:T(8,128)(2,1)S(1)} %get-tuple-element.29.tok, bf16[256,512]{1,0:T(8,128)(2,1)S(1)} %constant_dynamic-update-slice_fusion.refs_0_, ...), custom_call_target="tpu_custom_call" | custom-call | tf_op jit(solution)/shard_map/product/pallas_call | solution.py:151
  24.8 1.5 %collective-permute-start.10 = (bf16[512,256]{1,0:T(8,128)(2,1)S(1)}, bf16[512,256]{1,0:T(8,128)(2,1)S(1)}, u32[]{:S(2)}, u32[]{:S(2)}) collective-permute-start(bf16[512,256]{1,0:T(8,128)(2,1)S(1)} %get-tuple-element.31), channel_id=1, source_target_pairs={{0,2},{2,0},{4,6},{6,4},{8,10},{10,8},{12,14},{14,12},{16,18},{18,... | collective-permute-start | bytes 786440 | tf_op jit(solution)/shard_map/ppermute | solution.py:255
  26.3 1.5 %collective-permute-start.11 = (bf16[512,256]{1,0:T(8,128)(2,1)S(1)}, bf16[512,256]{1,0:T(8,128)(2,1)S(1)}, u32[]{:S(2)}, u32[]{:S(2)}) collective-permute-start(bf16[512,256]{1,0:T(8,128)(2,1)S(1)} %get-tuple-element.32), channel_id=1, source_target_pairs={{0,4},{2,6},{4,0},{6,2},{8,12},{10,14},{12,8},{14,10},{16,20},{18,... | collective-permute-start | bytes 786440 | tf_op jit(solution)/shard_map/ppermute | solution.py:255
  27.8 0.5 collective-permute-start.12
  28.3 5.6 %collective-permute-done.10.refs_1_ = bf16[512,256]{1,0:T(8,128)(2,1)S(1)} collective-permute-done((bf16[512,256]{1,0:T(8,128)(2,1)S(1)}, bf16[512,256]{1,0:T(8,128)(2,1)S(1)}, u32[]{:S(2)}, u32[]{:S(2)}) %collective-permute-start.10) | collective-permute-done | bytes 262176 | tf_op jit(solution)/shard_map/ppermute | solution.py:255
  33.9 6.4 %collective-permute-done.11.refs_2_ = bf16[512,256]{1,0:T(8,128)(2,1)S(1)} collective-permute-done((bf16[512,256]{1,0:T(8,128)(2,1)S(1)}, bf16[512,256]{1,0:T(8,128)(2,1)S(1)}, u32[]{:S(2)}, u32[]{:S(2)}) %collective-permute-start.11) | collective-permute-done | bytes 262176 | tf_op jit(solution)/shard_map/ppermute | solution.py:255
  40.4 0.0 collective-permute-done.12.refs_3_
  40.4 0.3 state.1
  40.7 1.3 %collective-permute-start.13 = (bf16[128,128]{1,0:T(8,128)(2,1)S(1)}, bf16[128,128]{1,0:T(8,128)(2,1)S(1)}, u32[]{:S(2)}, u32[]{:S(2)}) collective-permute-start(bf16[128,128]{1,0:T(8,128)(2,1)S(1)} %get-tuple-element.35), channel_id=1, source_target_pairs={{8,16},{10,18},{12,20},{14,22},{9,17},{11,19},{13,21},{15,23}} | collective-permute-start | bytes 98312 | tf_op jit(solution)/shard_map/ppermute | solution.py:286
  42.0 0.8 %within.1.inside = f32[512,128]{1,0:T(8,128)S(1)} custom-call(bf16[512,128]{1,0:T(8,128)(2,1)S(1)} %get-tuple-element.37.query, bf16[512,128]{1,0:T(8,128)(2,1)S(1)} %get-tuple-element.38.key, bf16[512,128]{1,0:T(8,128)(2,1)S(1)} %get-tuple-element.39.value, f32[8,512]{1,0:T(8,128)S(1)} %get-tuple-element.40.seg_row, ...), custom_call_target="tpu_custom_call" | custom-call | flops 2000000000 | tf_op jit(solution)/shard_map/within/pallas_call | solution.py:202
  42.8 0.0 copy-start
  42.8 3.7 %collective-permute-done.13.carried = bf16[128,128]{1,0:T(8,128)(2,1)S(1)} collective-permute-done((bf16[128,128]{1,0:T(8,128)(2,1)S(1)}, bf16[128,128]{1,0:T(8,128)(2,1)S(1)}, u32[]{:S(2)}, u32[]{:S(2)}) %collective-permute-start.13) | collective-permute-done | bytes 32800 | tf_op jit(solution)/shard_map/ppermute | solution.py:286
  46.5 0.0 copy-done
  46.5 0.3 finish.1
  46.8 1.3 %collective-permute-start.14 = (bf16[128,128]{1,0:T(8,128)(2,1)S(1)}, bf16[128,128]{1,0:T(8,128)(2,1)S(1)}, u32[]{:S(2)}, u32[]{:S(2)}) collective-permute-start(bf16[128,128]{1,0:T(8,128)(2,1)S(1)} %get-tuple-element.42), channel_id=1, source_target_pairs={{0,2},{2,0},{4,6},{6,4},{8,10},{10,8},{12,14},{14,12},{16,18},{18,... | collective-permute-start | bytes 98312 | tf_op jit(solution)/shard_map/ppermute | solution.py:255
  48.1 0.8 %collective-permute-start.15 = (bf16[128,128]{1,0:T(8,128)(2,1)S(1)}, bf16[128,128]{1,0:T(8,128)(2,1)S(1)}, u32[]{:S(2)}, u32[]{:S(2)}) collective-permute-start(bf16[128,128]{1,0:T(8,128)(2,1)S(1)} %get-tuple-element.43), channel_id=1, source_target_pairs={{0,4},{2,6},{4,0},{6,2},{8,12},{10,14},{12,8},{14,10},{16,20},{18,... | collective-permute-start | bytes 98312 | tf_op jit(solution)/shard_map/ppermute | solution.py:255
  48.9 1.4 %collective-permute-start.16 = (bf16[128,128]{1,0:T(8,128)(2,1)S(1)}, bf16[128,128]{1,0:T(8,128)(2,1)S(1)}, u32[]{:S(2)}, u32[]{:S(2)}) collective-permute-start(bf16[128,128]{1,0:T(8,128)(2,1)S(1)} %get-tuple-element.44), channel_id=1, source_target_pairs={{0,6},{2,4},{4,2},{6,0},{8,14},{10,12},{12,10},{14,8},{16,22},{18,... | collective-permute-start | bytes 98312 | tf_op jit(solution)/shard_map/ppermute | solution.py:255
  50.4 0.5 collective-permute-done.14.refs_1_
  50.9 1.1 %collective-permute-done.15.refs_2_ = bf16[128,128]{1,0:T(8,128)(2,1)S(1)} collective-permute-done((bf16[128,128]{1,0:T(8,128)(2,1)S(1)}, bf16[128,128]{1,0:T(8,128)(2,1)S(1)}, u32[]{:S(2)}, u32[]{:S(2)}) %collective-permute-start.15) | collective-permute-done | bytes 32800 | tf_op jit(solution)/shard_map/ppermute | solution.py:255
  52.0 1.7 %collective-permute-done.16.refs_3_ = bf16[128,128]{1,0:T(8,128)(2,1)S(1)} collective-permute-done((bf16[128,128]{1,0:T(8,128)(2,1)S(1)}, bf16[128,128]{1,0:T(8,128)(2,1)S(1)}, u32[]{:S(2)}, u32[]{:S(2)}) %collective-permute-start.16) | collective-permute-done | bytes 32800 | tf_op jit(solution)/shard_map/ppermute | solution.py:255
  53.8 0.7 %join.1 = bf16[128,512]{1,0:T(8,128)(2,1)} custom-call(bf16[128,128]{1,0:T(8,128)(2,1)S(1)} %get-tuple-element.41.refs_0_, bf16[128,128]{1,0:T(8,128)(2,1)S(1)} %collective-permute-done.14.refs_1_, bf16[128,128]{1,0:T(8,128)(2,1)S(1)} %collective-permute-done.15.refs_2_, bf16[128,128]{1,0:T(8,128)(2,1)S(1)} %collective-permute-done.16.refs_3_), custom_call_target="tpu_custom_call" | custom-call | tf_op jit(solution)/shard_map/join/pallas_call | solution.py:240
  (1 shorter events, 0.0 us)
Async XLA Ops:
  0.0 1.0 %copy-start.2 = (bf16[128,512]{1,0:T(8,128)(2,1)S(1)}, bf16[128,512]{1,0:T(8,128)(2,1)}, u32[]{:S(2)}) copy-start(bf16[128,512]{1,0:T(8,128)(2,1)} %param.10) | copy-start | bytes 393220
  1.0 13.7 %collective-permute-start.6 = (bf16[256,512]{1,0:T(8,128)(2,1)S(1)}, bf16[256,512]{1,0:T(8,128)(2,1)S(1)}, u32[]{:S(2)}, u32[]{:S(2)}) collective-permute-start(bf16[256,512]{1,0:T(8,128)(2,1)S(1)} %constant_dynamic-update-slice_fusion.refs_0_), channel_id=1, source_target_pairs={{0,24},{2,26},{4,28},{6,30},{8,16},{10,18},{12,20},{14,22},{16,8},... | collective-permute-start | bytes 786440 | tf_op jit(solution)/shard_map/ppermute | solution.py:255
  4.9 11.5 %collective-permute-start = (bf16[1168,128]{1,0:T(8,128)(2,1)}, bf16[1168,128]{1,0:T(8,128)(2,1)S(1)}, u32[]{:S(2)}, u32[]{:S(2)}) collective-permute-start(bf16[1168,128]{1,0:T(8,128)(2,1)} %get-tuple-element.26), channel_id=1, source_target_pairs={{0,2},{2,0},{4,6},{6,4},{8,10},{10,8},{12,14},{14,12},{16,18},{18,... | collective-permute-start | bytes 897032 | tf_op jit(solution)/shard_map/ppermute | solution.py:255
  6.5 14.9 %collective-permute-start.1 = (bf16[1168,128]{1,0:T(8,128)(2,1)}, bf16[1168,128]{1,0:T(8,128)(2,1)S(1)}, u32[]{:S(2)}, u32[]{:S(2)}) collective-permute-start(bf16[1168,128]{1,0:T(8,128)(2,1)} %get-tuple-element.27), channel_id=1, source_target_pairs={{0,4},{2,6},{4,0},{6,2},{8,12},{10,14},{12,8},{14,10},{16,20},{18,... | collective-permute-start | bytes 897032 | tf_op jit(solution)/shard_map/ppermute | solution.py:255
  8.0 13.9 %collective-permute-start.2 = (bf16[1168,128]{1,0:T(8,128)(2,1)}, bf16[1168,128]{1,0:T(8,128)(2,1)S(1)}, u32[]{:S(2)}, u32[]{:S(2)}) collective-permute-start(bf16[1168,128]{1,0:T(8,128)(2,1)} %get-tuple-element.28), channel_id=1, source_target_pairs={{0,6},{2,4},{4,2},{6,0},{8,14},{10,12},{12,10},{14,8},{16,22},{18,... | collective-permute-start | bytes 897032 | tf_op jit(solution)/shard_map/ppermute | solution.py:255
  8.5 7.9 %collective-permute-start.4 = (bf16[256,512]{1,0:T(8,128)(2,1)S(1)}, bf16[256,512]{1,0:T(8,128)(2,1)S(1)}, u32[]{:S(2)}, u32[]{:S(2)}) collective-permute-start(bf16[256,512]{1,0:T(8,128)(2,1)S(1)} %constant_dynamic-update-slice_fusion.refs_0_), channel_id=1, source_target_pairs={{0,8},{2,10},{4,12},{6,14},{8,0},{10,2},{12,4},{14,6},{16,24},{18,... | collective-permute-start | bytes 786440 | tf_op jit(solution)/shard_map/ppermute | solution.py:255
  14.7 7.2 %collective-permute-start.7 = (bf16[256,512]{1,0:T(8,128)(2,1)S(1)}, bf16[256,512]{1,0:T(8,128)(2,1)S(1)}, u32[]{:S(2)}, u32[]{:S(2)}) collective-permute-start(bf16[256,512]{1,0:T(8,128)(2,1)S(1)} %collective-permute-done.6.refs_6_), channel_id=1, source_target_pairs={{0,8},{2,10},{4,12},{6,14},{8,0},{10,2},{12,4},{14,6},{16,24},{18,... | collective-permute-start | bytes 786440 | tf_op jit(solution)/shard_map/ppermute | solution.py:255
  16.4 7.0 %collective-permute-start.3 = (bf16[256,512]{1,0:T(8,128)(2,1)S(1)}, bf16[256,512]{1,0:T(8,128)(2,1)S(1)}, u32[]{:S(2)}, u32[]{:S(2)}) collective-permute-start(bf16[256,512]{1,0:T(8,128)(2,1)S(1)} %constant_dynamic-update-slice_fusion.refs_0_), channel_id=1, source_target_pairs={{0,1},{1,0},{2,3},{3,2},{4,5},{5,4},{6,7},{7,6},{8,9},{9,8},{10,11... | collective-permute-start | bytes 786440 | tf_op jit(solution)/shard_map/ppermute | solution.py:268
  16.4 7.0 %collective-permute-start.9 = (bf16[256,512]{1,0:T(8,128)(2,1)S(1)}, bf16[256,512]{1,0:T(8,128)(2,1)S(1)}, u32[]{:S(2)}, u32[]{:S(2)}) collective-permute-start(bf16[256,512]{1,0:T(8,128)(2,1)S(1)} %collective-permute-done.6.refs_6_), channel_id=1, source_target_pairs={{0,1},{1,0},{2,3},{3,2},{4,5},{5,4},{6,7},{7,6},{8,9},{9,8},{10,11... | collective-permute-start | bytes 786440 | tf_op jit(solution)/shard_map/ppermute | solution.py:268
  21.4 2.1 %collective-permute-start.5 = (bf16[256,512]{1,0:T(8,128)(2,1)S(1)}, bf16[256,512]{1,0:T(8,128)(2,1)S(1)}, u32[]{:S(2)}, u32[]{:S(2)}) collective-permute-start(bf16[256,512]{1,0:T(8,128)(2,1)S(1)} %collective-permute-done.4.refs_2_), channel_id=1, source_target_pairs={{0,1},{1,0},{2,3},{3,2},{4,5},{5,4},{6,7},{7,6},{8,9},{9,8},{10,11... | collective-permute-start | bytes 786440 | tf_op jit(solution)/shard_map/ppermute | solution.py:268
  21.9 1.6 %collective-permute-start.8 = (bf16[256,512]{1,0:T(8,128)(2,1)S(1)}, bf16[256,512]{1,0:T(8,128)(2,1)S(1)}, u32[]{:S(2)}, u32[]{:S(2)}) collective-permute-start(bf16[256,512]{1,0:T(8,128)(2,1)S(1)} %collective-permute-done.7.refs_4_), channel_id=1, source_target_pairs={{0,1},{1,0},{2,3},{3,2},{4,5},{5,4},{6,7},{7,6},{8,9},{9,8},{10,11... | collective-permute-start | bytes 786440 | tf_op jit(solution)/shard_map/ppermute | solution.py:268
  21.9 1.0 %copy-start.1 = (bf16[1168,128]{1,0:T(8,128)(2,1)S(1)}, bf16[1168,128]{1,0:T(8,128)(2,1)}, u32[]{:S(2)}) copy-start(bf16[1168,128]{1,0:T(8,128)(2,1)} %get-tuple-element.25.refs_0_) | copy-start | bytes 897028
  24.8 9.2 %collective-permute-start.10 = (bf16[512,256]{1,0:T(8,128)(2,1)S(1)}, bf16[512,256]{1,0:T(8,128)(2,1)S(1)}, u32[]{:S(2)}, u32[]{:S(2)}) collective-permute-start(bf16[512,256]{1,0:T(8,128)(2,1)S(1)} %get-tuple-element.31), channel_id=1, source_target_pairs={{0,2},{2,0},{4,6},{6,4},{8,10},{10,8},{12,14},{14,12},{16,18},{18,... | collective-permute-start | bytes 786440 | tf_op jit(solution)/shard_map/ppermute | solution.py:255
  26.3 14.1 %collective-permute-start.11 = (bf16[512,256]{1,0:T(8,128)(2,1)S(1)}, bf16[512,256]{1,0:T(8,128)(2,1)S(1)}, u32[]{:S(2)}, u32[]{:S(2)}) collective-permute-start(bf16[512,256]{1,0:T(8,128)(2,1)S(1)} %get-tuple-element.32), channel_id=1, source_target_pairs={{0,4},{2,6},{4,0},{6,2},{8,12},{10,14},{12,8},{14,10},{16,20},{18,... | collective-permute-start | bytes 786440 | tf_op jit(solution)/shard_map/ppermute | solution.py:255
  27.8 12.5 %collective-permute-start.12 = (bf16[512,256]{1,0:T(8,128)(2,1)S(1)}, bf16[512,256]{1,0:T(8,128)(2,1)S(1)}, u32[]{:S(2)}, u32[]{:S(2)}) collective-permute-start(bf16[512,256]{1,0:T(8,128)(2,1)S(1)} %get-tuple-element.33), channel_id=1, source_target_pairs={{0,6},{2,4},{4,2},{6,0},{8,14},{10,12},{12,10},{14,8},{16,22},{18,... | collective-permute-start | bytes 786440 | tf_op jit(solution)/shard_map/ppermute | solution.py:255
  40.7 5.8 %collective-permute-start.13 = (bf16[128,128]{1,0:T(8,128)(2,1)S(1)}, bf16[128,128]{1,0:T(8,128)(2,1)S(1)}, u32[]{:S(2)}, u32[]{:S(2)}) collective-permute-start(bf16[128,128]{1,0:T(8,128)(2,1)S(1)} %get-tuple-element.35), channel_id=1, source_target_pairs={{8,16},{10,18},{12,20},{14,22},{9,17},{11,19},{13,21},{15,23}} | collective-permute-start | bytes 98312 | tf_op jit(solution)/shard_map/ppermute | solution.py:286
  42.8 3.7 %copy-start = (f32[512]{0:T(512)S(1)}, f32[512]{0:T(512)}, u32[]{:S(2)}) copy-start(f32[512]{0:T(512)} %param.11) | copy-start | bytes 6148
  46.8 4.1 %collective-permute-start.14 = (bf16[128,128]{1,0:T(8,128)(2,1)S(1)}, bf16[128,128]{1,0:T(8,128)(2,1)S(1)}, u32[]{:S(2)}, u32[]{:S(2)}) collective-permute-start(bf16[128,128]{1,0:T(8,128)(2,1)S(1)} %get-tuple-element.42), channel_id=1, source_target_pairs={{0,2},{2,0},{4,6},{6,4},{8,10},{10,8},{12,14},{14,12},{16,18},{18,... | collective-permute-start | bytes 98312 | tf_op jit(solution)/shard_map/ppermute | solution.py:255
  48.1 3.9 %collective-permute-start.15 = (bf16[128,128]{1,0:T(8,128)(2,1)S(1)}, bf16[128,128]{1,0:T(8,128)(2,1)S(1)}, u32[]{:S(2)}, u32[]{:S(2)}) collective-permute-start(bf16[128,128]{1,0:T(8,128)(2,1)S(1)} %get-tuple-element.43), channel_id=1, source_target_pairs={{0,4},{2,6},{4,0},{6,2},{8,12},{10,14},{12,8},{14,10},{16,20},{18,... | collective-permute-start | bytes 98312 | tf_op jit(solution)/shard_map/ppermute | solution.py:255
  48.9 4.8 %collective-permute-start.16 = (bf16[128,128]{1,0:T(8,128)(2,1)S(1)}, bf16[128,128]{1,0:T(8,128)(2,1)S(1)}, u32[]{:S(2)}, u32[]{:S(2)}) collective-permute-start(bf16[128,128]{1,0:T(8,128)(2,1)S(1)} %get-tuple-element.44), channel_id=1, source_target_pairs={{0,6},{2,4},{4,2},{6,0},{8,14},{10,12},{12,10},{14,8},{16,22},{18,... | collective-permute-start | bytes 98312 | tf_op jit(solution)/shard_map/ppermute | solution.py:255

commit v4 on v3

v4 whole, which is shorter than its diff:
```python
import functools

import jax
import jax.numpy as jnp
from jax import lax
from jax.experimental import pallas as pl
from jax.experimental.pallas import tpu as pltpu
from jax.sharding import PartitionSpec as P

HEAD = 128
BF, F32 = jnp.bfloat16, jnp.float32
DOC_BLOCKS = {16: 8, 64: 16}
MARKS = 16
PARTS = 4


def phi(u):
    return jnp.where(u > 0, u + 1.0, jnp.exp(jnp.minimum(u, 0.0)))


def aligned(index, size):
    return pl.ds(pl.multiple_of(index * size, size), size)


def inner_outer(heads):
    me = lax.axis_index("ctx")
    return lax.rem(me, heads), lax.div(me, heads)


def shape(rows, cols, dtype):
    return jax.ShapeDtypeStruct((rows, cols), dtype)


def limit(mib):
    return pltpu.CompilerParams(vmem_limit_bytes=mib * 2**20)


def stack_kernel(*refs):
    parts, out, sems = refs[:-2], refs[-2], refs[-1]
    copies, at = [], 0
    for i, part in enumerate(parts):
        rows = part.shape[0]
        copies.append(pltpu.make_async_copy(part, out.at[at : at + rows, :], sems.at[i]))
        copies[-1].start()
        at += rows
    for copy in copies:
        copy.wait()


def stack(*parts):
    rows = sum(a.shape[0] for a in parts)
    return pl.pallas_call(
        stack_kernel,
        in_specs=[pl.BlockSpec(memory_space=pl.ANY)] * len(parts),
        out_specs=pl.BlockSpec(memory_space=pltpu.VMEM),
        out_shape=pltpu.VMEM((rows, parts[0].shape[1]), BF),
        scratch_shapes=[pltpu.SemaphoreType.DMA((len(parts),))],
        compiler_params=limit(8),
        name="stack",
    )(*[pltpu.with_memory_space_constraint(a, pltpu.HBM) for a in parts])


def partners(heads):
    return [0] + list(range(heads - 1, 0, -1))


def pack_kernel(heads, tok_ref, query_ref, flag_ref, *refs):
    out_refs = refs[:heads]
    tok, query, flag, sems = refs[heads:]
    inner, _ = inner_outer(heads)
    count, depth = tok_ref.shape
    squares = depth // (heads * HEAD)
    part = count // PARTS
    pairs = [(query_ref, query), (flag_ref, flag)]
    for p in range(PARTS):
        rows = slice(p * part, (p + 1) * part)
        pairs.append((tok_ref.at[rows, :], tok.at[rows, :]))
    copies = [pltpu.make_async_copy(a, b, sems.at[i]) for i, (a, b) in enumerate(pairs)]
    for copy in copies:
        copy.start()
    for copy in copies[:2]:
        copy.wait()
    marks = jnp.broadcast_to(flag[...].astype(F32), (MARKS, count)).astype(BF)
    for k, out in enumerate(out_refs):
        own = query[:, aligned(jnp.bitwise_xor(inner, k), HEAD)].astype(F32)
        out[squares * count : (squares + 1) * count, :] = phi(own).astype(BF)
        out[(squares + 1) * count :, :] = marks
    for p, copy in enumerate(copies[2:]):
        copy.wait()
        for k, out in enumerate(out_refs):
            to = jnp.bitwise_xor(inner, k)
            for i in range(squares):
                at = ((i // 2) * heads + to) * 2 + i % 2
                rows = slice(i * count + p * part, i * count + (p + 1) * part)
                out[rows, :] = tok[p * part : (p + 1) * part, aligned(at, HEAD)]


def pack(tokens, queries, flags, heads, share):
    count, depth = tokens.shape
    squares = depth // (heads * HEAD)
    if share == 2 * HEAD:
        packed = shape((squares + 1) * count + MARKS, HEAD, BF)
        return pl.pallas_call(
            functools.partial(pack_kernel, heads),
            in_specs=[pl.BlockSpec(memory_space=pl.ANY)] * 3,
            out_specs=[pl.BlockSpec(memory_space=pltpu.VMEM)] * heads,
            out_shape=[pltpu.VMEM(packed.shape, BF)] * heads,
            scratch_shapes=[
                pltpu.VMEM((count, depth), BF),
                pltpu.VMEM((count, heads * HEAD), BF),
                pltpu.VMEM((1, count), jnp.int32),
                pltpu.SemaphoreType.DMA((PARTS + 2,)),
            ],
            compiler_params=limit(8),
            name="pack",
        )(*[pltpu.with_memory_space_constraint(a, pltpu.HBM) for a in (tokens, queries, flags)])
    inner, _ = inner_outer(heads)
    by_inner = tokens.reshape(count, -1, heads, share).transpose(2, 0, 1, 3)
    by_inner = by_inner.reshape(heads, count, squares, HEAD).transpose(0, 2, 1, 3).reshape(heads, -1, HEAD)
    query = phi(queries.astype(F32)).astype(BF).reshape(count, heads, HEAD).transpose(1, 0, 2)
    marks = jnp.broadcast_to(flags.astype(BF), (MARKS, count))
    out = []
    for k in range(heads):
        to = jnp.bitwise_xor(inner, k)
        parts = [lax.dynamic_index_in_dim(a, to, 0, False) for a in (by_inner, query)]
        out.append(jnp.concatenate(parts + [marks], axis=0))
    return out


def assemble_kernel(heads, count, split, *refs):
    x_refs = refs[:heads]
    tok, query, first, seg_row, seg_col, marks = refs[heads:]
    inner, outer = inner_outer(heads)
    squares = tok.shape[1] // HEAD
    total = heads * count
    for k, x in zip(partners(heads), x_refs):
        place = jnp.bitwise_xor(inner, k)
        rows = aligned(place, count)
        for i in range(squares):
            at = i
            if split:
                core = lax.axis_index("fsdp")
                at = jnp.bitwise_xor(outer, i // 2) * 2 + jnp.bitwise_xor(core, i % 2)
            tok[rows, i * HEAD : (i + 1) * HEAD] = x[aligned(at, count), :]
        query[rows, :] = x[squares * count : (squares + 1) * count, :]
        marks[:, rows] = x[(squares + 1) * count :, :]
    early = lax.broadcasted_iota(jnp.int32, (total, total), 0)
    late = lax.broadcasted_iota(jnp.int32, (total, total), 1)
    upto = jnp.where(early <= late, 1.0, 0.0).astype(BF)
    seg = jnp.dot(marks[...], upto, preferred_element_type=F32)[:1, :]
    seg_row[...] = jnp.broadcast_to(seg, seg_row.shape)
    col = jnp.broadcast_to(seg, (HEAD, total)).T
    seg_col[...] = col
    first[...] = jnp.where(col == 0.0, query[...].astype(F32), 0.0).astype(BF)


def assemble(received, heads, count, depth, split):
    total = heads * count
    return pl.pallas_call(
        functools.partial(assemble_kernel, heads, count, split),
        out_shape=[
            shape(total, depth, BF),
            shape(total, HEAD, BF),
            shape(total, HEAD, BF),
            shape(8, total, F32),
            shape(total, HEAD, F32),
        ],
        scratch_shapes=[pltpu.VMEM((MARKS, total), BF)],
        compiler_params=limit(16),
        cost_estimate=pl.CostEstimate(flops=4 * 10**9, bytes_accessed=0, transcendentals=0),
        name="assemble",
    )(*received)


def product_kernel(heads, places, tok, *refs):
    w_refs, out_refs = refs[:-heads], refs[-heads:]
    inner, _ = inner_outer(heads)
    rows = tok.shape[1] // len(places)

    def panel(k):
        cols = aligned(jnp.bitwise_xor(inner, k), HEAD)
        return jnp.concatenate([w[at : at + rows, cols] for w, at in zip(w_refs, places)], axis=0)

    order = list(range(1, heads)) + [0]
    for a, b in zip(order[::2], order[1::2]):
        both = jnp.concatenate([panel(a), panel(b)], axis=1)
        both = jnp.dot(tok[...], both, preferred_element_type=F32)
        out_refs[a][...] = both[:, :HEAD].astype(out_refs[a].dtype)
        out_refs[b][...] = both[:, HEAD:].astype(out_refs[b].dtype)


def product(tok, ws, heads, name):
    total = tok.shape[0]
    return pl.pallas_call(
        functools.partial(product_kernel, heads, [at for _, at in ws]),
        out_shape=[shape(total, HEAD, F32)] + [shape(total, HEAD, BF)] * (heads - 1),
        compiler_params=limit(16),
        name=name,
    )(tok, *[w for w, _ in ws])


def gathered(parts):
    proj = parts[0][...]
    for part in parts[1:]:
        proj = proj + part[...].astype(F32)
    return proj


def score_kernel(heads, *refs):
    parts = refs[:heads]
    query, seg_row, seg_col, key_ref, score_ref = refs[heads:]
    total = query.shape[0]
    count = total // heads
    key = phi(gathered(parts)).astype(BF)
    key_ref[...] = key
    for i in range(heads):
        rows, width = slice(i * count, (i + 1) * count), (i + 1) * count
        scores = lax.dot_general(
            query[rows, :], key[:width, :], (((1,), (1,)), ((), ())), preferred_element_type=F32
        )
        own = jnp.concatenate([seg_col[rows, :]] * (i + 1), axis=1)
        early = lax.broadcasted_iota(jnp.int32, (count, width), 1)
        late = lax.broadcasted_iota(jnp.int32, (count, width), 0) + i * count
        allowed = (own == seg_row[:1, :width]) & (early <= late)
        score_ref[rows, :width] = jnp.where(allowed, scores, 0.0).astype(BF)


def score(parts, query, seg_row, seg_col, heads):
    total = query.shape[0]
    return pl.pallas_call(
        functools.partial(score_kernel, heads),
        out_shape=[shape(total, HEAD, BF), shape(total, total, BF)],
        compiler_params=limit(16),
        cost_estimate=pl.CostEstimate(flops=4 * 10**9, bytes_accessed=0, transcendentals=0),
        name="score",
    )(*parts, query, seg_row, seg_col)


def state_kernel(heads, *refs):
    parts = refs[:heads]
    key, seg_col, state_ref, value_ref = refs[heads:]
    value = gathered(parts).astype(BF)
    last = seg_col[seg_col.shape[0] - 1 :, :]
    tail = jnp.where(seg_col[...] == last, value.astype(F32), 0.0).astype(BF)
    state = lax.dot_general(key[...], tail, (((0,), (0,)), ((), ())), preferred_element_type=F32)
    state_ref[...] = state.astype(state_ref.dtype)
    value_ref[...] = value


def leave(parts, key, seg_col, heads, kind):
    total = seg_col.shape[0]
    return pl.pallas_call(
        functools.partial(state_kernel, heads),
        out_shape=[shape(HEAD, HEAD, kind), shape(total, HEAD, BF)],
        compiler_params=limit(16),
        name="state",
    )(*parts, key, seg_col)


def within_kernel(heads, scores, value, out_ref):
    count = value.shape[0] // heads
    for i in range(heads):
        rows, width = slice(i * count, (i + 1) * count), (i + 1) * count
        out_ref[rows, :] = jnp.dot(scores[rows, :width], value[:width, :], preferred_element_type=F32)


def within(scores, value, heads):
    return pl.pallas_call(
        functools.partial(within_kernel, heads),
        out_shape=shape(value.shape[0], HEAD, F32),
        compiler_params=limit(16),
        cost_estimate=pl.CostEstimate(flops=2 * 10**9, bytes_accessed=0, transcendentals=0),
        name="within",
    )(scores, value)


def finish_kernel(heads, carried, first, inside, gain, *refs):
    out_refs, done = refs[:-1], refs[-1]
    inner, _ = inner_outer(heads)
    count = out_refs[0].shape[0]
    mixed = inside[...] + jnp.dot(first[...], carried[...], preferred_element_type=F32)
    scale = lax.rsqrt(jnp.mean(mixed * mixed, axis=-1, keepdims=True) + 1e-06)
    done[...] = (mixed * scale * gain[:, aligned(inner, HEAD)]).astype(BF)
    for k, out in enumerate(out_refs):
        out[...] = done[aligned(jnp.bitwise_xor(inner, k), count), :]


def finish(carried, first, inside, gain, heads):
    total = first.shape[0]
    return pl.pallas_call(
        functools.partial(finish_kernel, heads),
        out_shape=[shape(total // heads, HEAD, BF)] * heads,
        scratch_shapes=[pltpu.VMEM((total, HEAD), BF)],
        compiler_params=limit(8),
        name="finish",
    )(carried, first, inside, gain)


def join_kernel(heads, *refs):
    inner, _ = inner_outer(heads)
    for k, part in zip(partners(heads), refs[:-1]):
        refs[-1][:, aligned(jnp.bitwise_xor(inner, k), HEAD)] = part[...]


def join(parts, heads):
    return pl.pallas_call(
        functools.partial(join_kernel, heads),
        out_shape=shape(parts[0].shape[0], heads * HEAD, BF),
        compiler_params=limit(8),
        name="join",
    )(*parts)


def on_device(n_ctx, fsdp, tokens, queries, flags, w_key, w_value, norm_gain):
    _, count, depth = tokens.shape
    rows, width = w_key.shape
    heads = width // HEAD
    outer = n_ctx // heads

    def swap(a, mask):
        return lax.ppermute(a, "ctx", [(i, i ^ mask) for i in range(n_ctx)])

    def exchange(parts):
        return [parts[0]] + [swap(parts[k], k) for k in partners(heads)[1:]]

    def other(a):
        return lax.ppermute(a, "fsdp", [(0, 1), (1, 0)])

    both = (w_key, w_value)
    split = outer == 4 and fsdp == 2 and rows == HEAD
    if split:
        weights = stack(*both)
        far = swap(weights, 3 * heads)
        near = swap(weights, heads)
    packed = pack(tokens[0], queries[0], flags, heads, fsdp * rows)
    received = exchange(packed)
    tok, query, first, seg_row, seg_col = assemble(received, heads, count, depth // heads, split)
    if split:
        whole = [(w, other(w)) for w in (weights, near, far)]
        panels = []
        for at in (0, rows):
            last = swap(far[at : at + rows], heads)
            own, close, away = [[(w, at) for w in pair] for pair in whole]
            panels.append(own + close + [(last, 0), (other(last), 0)] + away)
    else:
        groups = [[o * heads + q for o in range(outer)] for q in range(heads)]
        chip = [lax.all_gather(w, "fsdp", axis=0, tiled=True) for w in both]
        panels = [
            [(lax.all_gather(w, "ctx", axis=0, tiled=True, axis_index_groups=groups), 0)] for w in chip
        ]
    parts = []
    for panel, name in zip(panels, ("key_product", "value_product")):
        partial = product(tok, panel, heads, name)
        parts.append(exchange(partial))
    key, scores = score(parts[0], query, seg_row, seg_col, heads)

    doc = DOC_BLOCKS.get(n_ctx, 2 * n_ctx)
    starts = [b for b in range(n_ctx) if b % doc == doc // 2]
    pairs = [
        (b, b + heads)
        for b in range(n_ctx - heads)
        if (b // heads + 1) * heads not in starts
    ]
    rounds = max(1, min(doc // heads, outer) - 1)
    state, value = leave(parts[1], key, seg_col, heads, BF if rounds == 1 else F32)
    carried = lax.ppermute(state.astype(BF), "ctx", pairs)
    keep = (seg_col[-1:, :] == 0.0).astype(F32)
    for _ in range(rounds - 1):
        carried = lax.ppermute((state + keep * carried.astype(F32)).astype(BF), "ctx", pairs)
    inside = within(scores, value, heads)
    done = finish(carried, first, inside, norm_gain.reshape(1, width), heads)
    return join(exchange(done), heads)[None]


def solution(mesh):
    n_ctx, fsdp = mesh.shape["ctx"], mesh.shape["fsdp"]
    in_specs = (
        P("fsdp", "ctx", None),
        P("fsdp", "ctx", None),
        P("fsdp", "ctx"),
        P(("ctx", "fsdp"), None),
        P(("ctx", "fsdp"), None),
        P(),
    )
    return jax.shard_map(
        functools.partial(on_device, n_ctx, fsdp),
        mesh=mesh,
        in_specs=in_specs,
        out_specs=P("fsdp", "ctx", None),
        check_vma=False,
    )
```

time: 55.2 us -> 52.8 us (0.957); the launches traced: 54.4 us -> 52.6 us
  starting transfers between devices: 14.1 us -> 20.5 us
  waiting for transfers between devices: 30.9 us -> 25.8 us
  local copies, waits for them, and re-layouts: 1.94 us -> 0.02 us
  Pallas kernels: 7.34 us -> 6.14 us
    ppermute x12 -> x16, starting transfers between devices: 12.3 us -> 18.7 us  [swap(): return lax.ppermute(a, 'ctx', [(i, i ^ mask) for i in range(n_ctx)])]
    ppermute x12 -> x16, waiting for transfers between devices: 27.2 us -> 21.5 us  [swap(): return lax.ppermute(a, 'ctx', [(i, i ^ mask) for i in range(n_ctx)])]
    pallas_call x1, Pallas kernels: 3.43 us -> 1.39 us  [pack(): pl.pallas_call(functools.partial(pack_kernel, heads), in_specs=[pl.BlockS...]
    unnamed x7 -> x2, local copies, waits for them, and re-layouts: 1.93 us -> 0.01 us
    pallas_call x2 -> x5, Pallas kernels: 2.05 us -> 2.98 us  [the longest x2 1.46 us: product(): pl.pallas_call(functools.partial(product_kernel, heads, [at for _, at in...]
  transfers between devices with their start and end apart: 17 -> 22, of which waited for: 10 -> 14; matrix products, arithmetic and copies ran while one was open for 0% -> 0% of each run, Pallas kernels for 9% -> 7%
where the time goes in v4:
time: 52.8 us; the launch traced here: 52.6 us
  waiting for transfers between devices  25.8 us (49%)
  starting transfers between devices  20.5 us (39%)
  Pallas kernels  6.14 us (12%)
    ppermute x16, waiting for transfers between devices, swap(): return lax.ppermute(a, 'ctx', [(i, i ^ mask) for i in range(n_ctx)])  21.5 us
    ppermute x16, starting transfers between devices, swap(): return lax.ppermute(a, 'ctx', [(i, i ^ mask) for i in range(n_ctx)])  18.7 us
    ppermute x1, waiting for transfers between devices, on_device(): carried = lax.ppermute(state.astype(BF), 'ctx', pairs)  4.26 us
    pallas_call x2, Pallas kernels, product(): pl.pallas_call(functools.partial(product_kernel, heads, [at for _, at in...  1.46 us
    pallas_call x1, Pallas kernels, pack(): pl.pallas_call(functools.partial(pack_kernel, heads), in_specs=[pl.BlockS...  1.39 us
    ppermute x1, starting transfers between devices, on_device(): carried = lax.ppermute(state.astype(BF), 'ctx', pairs)  1.29 us
  transfers between devices with their start and end apart: 22, of which 14 were waited for; matrix products, arithmetic and copies ran while one was open for 0% of the time, Pallas kernels for 7%

profile of v4, /device:TPU:16, one launch (start us, length us, event | category | flops | bytes accessed | tf_op | source)
XLA Modules:
  0.0 52.6 jit_solution(3305851044303950659)
XLA Ops:
  0.0 1.0 %stack.1.refs_0_ = bf16[256,512]{1,0:T(8,128)(2,1)S(1)} custom-call(bf16[128,512]{1,0:T(8,128)(2,1)} %refs_0_.1, bf16[128,512]{1,0:T(8,128)(2,1)} %refs_1_.1), custom_call_target="tpu_custom_call" | custom-call | tf_op jit(solution)/shard_map/stack/pallas_call | solution.py:52
  1.0 0.5 collective-permute-start.6
  1.5 1.2 %collective-permute-start.4 = (bf16[256,512]{1,0:T(8,128)(2,1)S(1)}, bf16[256,512]{1,0:T(8,128)(2,1)S(1)}, u32[]{:S(2)}, u32[]{:S(2)}) collective-permute-start(bf16[256,512]{1,0:T(8,128)(2,1)S(1)} %stack.1.refs_0_), channel_id=1, source_target_pairs={{0,8},{2,10},{4,12},{6,14},{8,0},{10,2},{12,4},{14,6},{16,24},{18,... | collective-permute-start | bytes 786440 | tf_op jit(solution)/shard_map/ppermute | solution.py:321
  2.7 1.4 %pack.1 = (bf16[1168,128]{1,0:T(8,128)(2,1)S(1)}, bf16[1168,128]{1,0:T(8,128)(2,1)S(1)}, bf16[1168,128]{1,0:T(8,128)(2,1)S(1)}, bf16[1168,128]{1,0:T(8,128)(2,1)S(1)}) custom-call(bf16[128,4096]{1,0:T(8,128)(2,1)} %bitcast.5, bf16[128,512]{1,0:T(8,128)(2,1)} %bitcast.6, s32[1,128]{1,0:T(1,128)} %flag_ref.1), custom_call_target="tpu_custom_call" | custom-call | tf_op jit(solution)/shard_map/pack/pallas_call | solution.py:103
  4.1 2.7 %collective-permute-start = (bf16[1168,128]{1,0:T(8,128)(2,1)S(1)}, bf16[1168,128]{1,0:T(8,128)(2,1)S(1)}, u32[]{:S(2)}, u32[]{:S(2)}) collective-permute-start(bf16[1168,128]{1,0:T(8,128)(2,1)S(1)} %get-tuple-element.31), channel_id=1, source_target_pairs={{0,6},{2,4},{4,2},{6,0},{8,14},{10,12},{12,10},{14,8},{16,22},{18,... | collective-permute-start | bytes 897032 | tf_op jit(solution)/shard_map/ppermute | solution.py:321
  6.8 0.5 collective-permute-start.1
  7.3 0.4 collective-permute-start.2
  7.7 7.1 %collective-permute-done.6.refs_6_ = bf16[256,512]{1,0:T(8,128)(2,1)S(1)} collective-permute-done((bf16[256,512]{1,0:T(8,128)(2,1)S(1)}, bf16[256,512]{1,0:T(8,128)(2,1)S(1)}, u32[]{:S(2)}, u32[]{:S(2)}) %collective-permute-start.6) | collective-permute-done | bytes 262176 | tf_op jit(solution)/shard_map/ppermute | solution.py:321
  14.7 0.1 collective-permute-start.13
  14.8 0.0 collective-permute-done.4.refs_2_
  14.8 0.1 collective-permute-start.3
  14.9 0.2 collective-permute-done.refs_1_
  15.1 1.8 %collective-permute-start.7 = (bf16[128,512]{1,0:T(8,128)(2,1)S(1)}, bf16[128,512]{1,0:T(8,128)(2,1)S(1)}, u32[]{:S(2)}, u32[]{:S(2)}) collective-permute-start(bf16[128,512]{1,0:T(8,128)(2,1)S(1)} %get-tuple-element.56), channel_id=1, source_target_pairs={{0,8},{2,10},{4,12},{6,14},{8,0},{10,2},{12,4},{14,6},{16,24},{18,... | collective-permute-start | bytes 393224 | tf_op jit(solution)/shard_map/ppermute | solution.py:321
  16.9 3.1 %collective-permute-done.1.refs_2_ = bf16[1168,128]{1,0:T(8,128)(2,1)S(1)} collective-permute-done((bf16[1168,128]{1,0:T(8,128)(2,1)S(1)}, bf16[1168,128]{1,0:T(8,128)(2,1)S(1)}, u32[]{:S(2)}, u32[]{:S(2)}) %collective-permute-start.1) | collective-permute-done | bytes 299040 | tf_op jit(solution)/shard_map/ppermute | solution.py:321
  20.0 0.0 collective-permute-start.9
  20.1 0.1 collective-permute-done.2.refs_3_
  20.1 0.4 collective-permute-start.5
  20.6 0.5 collective-permute-done.13.refs_4_
  21.0 0.0 collective-permute-start.14
  21.0 0.5 %assemble.1 = (bf16[512,1024]{1,0:T(8,128)(2,1)S(1)}, bf16[512,128]{1,0:T(8,128)(2,1)S(1)}, bf16[512,128]{1,0:T(8,128)(2,1)S(1)}, f32[8,512]{1,0:T(8,128)S(1)}, f32[512,128]{1,0:T(8,128)S(1)}) custom-call(bf16[1168,128]{1,0:T(8,128)(2,1)S(1)} %get-tuple-element.30.refs_0_, bf16[1168,128]{1,0:T(8,128)(2,1)S(1)} %collective-permute-done.refs_1_, ...), custom_call_target="tpu_custom_call" | custom-call | flops 4000000000 | tf_op jit(solution)/shard_map/assemble/pallas_call | solution.py:159
  21.6 0.8 %collective-permute-done.7.refs_4_ = bf16[128,512]{1,0:T(8,128)(2,1)S(1)} collective-permute-done((bf16[128,512]{1,0:T(8,128)(2,1)S(1)}, bf16[128,512]{1,0:T(8,128)(2,1)S(1)}, u32[]{:S(2)}, u32[]{:S(2)}) %collective-permute-start.7) | collective-permute-done | bytes 131104 | tf_op jit(solution)/shard_map/ppermute | solution.py:321
  22.4 0.0 collective-permute-start.8
  22.4 0.0 collective-permute-done.3.refs_1_
  22.4 0.0 collective-permute-done.14.refs_5_
  22.4 0.0 collective-permute-done.9.refs_7_
  22.4 0.0 collective-permute-done.5.refs_3_
  22.5 0.7 %key_product.1 = (f32[512,128]{1,0:T(8,128)S(1)}, bf16[512,128]{1,0:T(8,128)(2,1)S(1)}, bf16[512,128]{1,0:T(8,128)(2,1)S(1)}, bf16[512,128]{1,0:T(8,128)(2,1)S(1)}) custom-call(bf16[512,1024]{1,0:T(8,128)(2,1)S(1)} %get-tuple-element.34.tok, bf16[256,512]{1,0:T(8,128)(2,1)S(1)} %stack.1.refs_0_, bf16[256,512]{1,0:T(8,128)(2,1)S(1)} %collective-permute-done.3.refs_1_, ...), custom_call_target="tpu_custom_call" | custom-call | tf_op jit(solution)/shard_map/key_product/pallas_call | solution.py:194
  23.2 2.5 %collective-permute-start.15 = (bf16[512,128]{1,0:T(8,128)(2,1)S(1)}, bf16[512,128]{1,0:T(8,128)(2,1)S(1)}, u32[]{:S(2)}, u32[]{:S(2)}) collective-permute-start(bf16[512,128]{1,0:T(8,128)(2,1)S(1)} %get-tuple-element.40), channel_id=1, source_target_pairs={{0,6},{2,4},{4,2},{6,0},{8,14},{10,12},{12,10},{14,8},{16,22},{18,... | collective-permute-start | bytes 393224 | tf_op jit(solution)/shard_map/ppermute | solution.py:321
  25.7 0.5 collective-permute-start.16
  26.2 0.5 %collective-permute-start.17 = (bf16[512,128]{1,0:T(8,128)(2,1)S(1)}, bf16[512,128]{1,0:T(8,128)(2,1)S(1)}, u32[]{:S(2)}, u32[]{:S(2)}) collective-permute-start(bf16[512,128]{1,0:T(8,128)(2,1)S(1)} %get-tuple-element.42), channel_id=1, source_target_pairs={{0,2},{2,0},{4,6},{6,4},{8,10},{10,8},{12,14},{14,12},{16,18},{18,... | collective-permute-start | bytes 393224 | tf_op jit(solution)/shard_map/ppermute | solution.py:321
  26.8 0.0 collective-permute-done.8.refs_5_
  26.8 0.7 %value_product.1 = (f32[512,128]{1,0:T(8,128)S(1)}, bf16[512,128]{1,0:T(8,128)(2,1)S(1)}, bf16[512,128]{1,0:T(8,128)(2,1)S(1)}, bf16[512,128]{1,0:T(8,128)(2,1)S(1)}) custom-call(bf16[512,1024]{1,0:T(8,128)(2,1)S(1)} %get-tuple-element.34.tok, bf16[256,512]{1,0:T(8,128)(2,1)S(1)} %stack.1.refs_0_, bf16[256,512]{1,0:T(8,128)(2,1)S(1)} %collective-permute-done.3.refs_1_, ...), custom_call_target="tpu_custom_call" | custom-call | tf_op jit(solution)/shard_map/value_product/pallas_call | solution.py:194
  27.5 2.5 %collective-permute-start.10 = (bf16[512,128]{1,0:T(8,128)(2,1)S(1)}, bf16[512,128]{1,0:T(8,128)(2,1)S(1)}, u32[]{:S(2)}, u32[]{:S(2)}) collective-permute-start(bf16[512,128]{1,0:T(8,128)(2,1)S(1)} %get-tuple-element.36), channel_id=1, source_target_pairs={{0,6},{2,4},{4,2},{6,0},{8,14},{10,12},{12,10},{14,8},{16,22},{18,... | collective-permute-start | bytes 393224 | tf_op jit(solution)/shard_map/ppermute | solution.py:321
  30.0 0.5 collective-permute-start.11
  30.5 0.0 collective-permute-done.15.refs_1_
  30.5 1.5 %collective-permute-start.12 = (bf16[512,128]{1,0:T(8,128)(2,1)S(1)}, bf16[512,128]{1,0:T(8,128)(2,1)S(1)}, u32[]{:S(2)}, u32[]{:S(2)}) collective-permute-start(bf16[512,128]{1,0:T(8,128)(2,1)S(1)} %get-tuple-element.38), channel_id=1, source_target_pairs={{0,2},{2,0},{4,6},{6,4},{8,10},{10,8},{12,14},{14,12},{16,18},{18,... | collective-permute-start | bytes 393224 | tf_op jit(solution)/shard_map/ppermute | solution.py:321
  32.0 1.6 %collective-permute-done.16.refs_2_ = bf16[512,128]{1,0:T(8,128)(2,1)S(1)} collective-permute-done((bf16[512,128]{1,0:T(8,128)(2,1)S(1)}, bf16[512,128]{1,0:T(8,128)(2,1)S(1)}, u32[]{:S(2)}, u32[]{:S(2)}) %collective-permute-start.16) | collective-permute-done | bytes 131104 | tf_op jit(solution)/shard_map/ppermute | solution.py:321
  33.6 0.0 collective-permute-done.17.refs_3_
  33.6 0.3 score.1
  33.9 2.5 %collective-permute-done.10.refs_1_ = bf16[512,128]{1,0:T(8,128)(2,1)S(1)} collective-permute-done((bf16[512,128]{1,0:T(8,128)(2,1)S(1)}, bf16[512,128]{1,0:T(8,128)(2,1)S(1)}, u32[]{:S(2)}, u32[]{:S(2)}) %collective-permute-start.10) | collective-permute-done | bytes 131104 | tf_op jit(solution)/shard_map/ppermute | solution.py:321
  36.4 2.1 %collective-permute-done.11.refs_2_ = bf16[512,128]{1,0:T(8,128)(2,1)S(1)} collective-permute-done((bf16[512,128]{1,0:T(8,128)(2,1)S(1)}, bf16[512,128]{1,0:T(8,128)(2,1)S(1)}, u32[]{:S(2)}, u32[]{:S(2)}) %collective-permute-start.11) | collective-permute-done | bytes 131104 | tf_op jit(solution)/shard_map/ppermute | solution.py:321
  38.5 0.1 collective-permute-done.12.refs_3_
  38.6 0.2 state.1
  38.9 1.3 %collective-permute-start.18 = (bf16[128,128]{1,0:T(8,128)(2,1)S(1)}, bf16[128,128]{1,0:T(8,128)(2,1)S(1)}, u32[]{:S(2)}, u32[]{:S(2)}) collective-permute-start(bf16[128,128]{1,0:T(8,128)(2,1)S(1)} %get-tuple-element.47), channel_id=1, source_target_pairs={{8,16},{10,18},{12,20},{14,22},{9,17},{11,19},{13,21},{15,23}} | collective-permute-start | bytes 98312 | tf_op jit(solution)/shard_map/ppermute | solution.py:366
  40.2 0.2 within.1.inside
  40.4 0.0 copy-start
  40.4 4.3 %collective-permute-done.18.carried = bf16[128,128]{1,0:T(8,128)(2,1)S(1)} collective-permute-done((bf16[128,128]{1,0:T(8,128)(2,1)S(1)}, bf16[128,128]{1,0:T(8,128)(2,1)S(1)}, u32[]{:S(2)}, u32[]{:S(2)}) %collective-permute-start.18) | collective-permute-done | bytes 32800 | tf_op jit(solution)/shard_map/ppermute | solution.py:366
  44.7 0.0 copy-done
  44.7 0.3 finish.1
  45.0 1.7 %collective-permute-start.19 = (bf16[128,128]{1,0:T(8,128)(2,1)S(1)}, bf16[128,128]{1,0:T(8,128)(2,1)S(1)}, u32[]{:S(2)}, u32[]{:S(2)}) collective-permute-start(bf16[128,128]{1,0:T(8,128)(2,1)S(1)} %get-tuple-element.52), channel_id=1, source_target_pairs={{0,6},{2,4},{4,2},{6,0},{8,14},{10,12},{12,10},{14,8},{16,22},{18,... | collective-permute-start | bytes 98312 | tf_op jit(solution)/shard_map/ppermute | solution.py:321
  46.7 1.3 %collective-permute-start.20 = (bf16[128,128]{1,0:T(8,128)(2,1)S(1)}, bf16[128,128]{1,0:T(8,128)(2,1)S(1)}, u32[]{:S(2)}, u32[]{:S(2)}) collective-permute-start(bf16[128,128]{1,0:T(8,128)(2,1)S(1)} %get-tuple-element.53), channel_id=1, source_target_pairs={{0,4},{2,6},{4,0},{6,2},{8,12},{10,14},{12,8},{14,10},{16,20},{18,... | collective-permute-start | bytes 98312 | tf_op jit(solution)/shard_map/ppermute | solution.py:321
  48.0 0.5 %collective-permute-start.21 = (bf16[128,128]{1,0:T(8,128)(2,1)S(1)}, bf16[128,128]{1,0:T(8,128)(2,1)S(1)}, u32[]{:S(2)}, u32[]{:S(2)}) collective-permute-start(bf16[128,128]{1,0:T(8,128)(2,1)S(1)} %get-tuple-element.54), channel_id=1, source_target_pairs={{0,2},{2,0},{4,6},{6,4},{8,10},{10,8},{12,14},{14,12},{16,18},{18,... | collective-permute-start | bytes 98312 | tf_op jit(solution)/shard_map/ppermute | solution.py:321
  48.6 1.3 %collective-permute-done.19.refs_1_ = bf16[128,128]{1,0:T(8,128)(2,1)S(1)} collective-permute-done((bf16[128,128]{1,0:T(8,128)(2,1)S(1)}, bf16[128,128]{1,0:T(8,128)(2,1)S(1)}, u32[]{:S(2)}, u32[]{:S(2)}) %collective-permute-start.19) | collective-permute-done | bytes 32800 | tf_op jit(solution)/shard_map/ppermute | solution.py:321
  49.9 0.7 %collective-permute-done.20.refs_2_ = bf16[128,128]{1,0:T(8,128)(2,1)S(1)} collective-permute-done((bf16[128,128]{1,0:T(8,128)(2,1)S(1)}, bf16[128,128]{1,0:T(8,128)(2,1)S(1)}, u32[]{:S(2)}, u32[]{:S(2)}) %collective-permute-start.20) | collective-permute-done | bytes 32800 | tf_op jit(solution)/shard_map/ppermute | solution.py:321
  50.6 1.3 %collective-permute-done.21.refs_3_ = bf16[128,128]{1,0:T(8,128)(2,1)S(1)} collective-permute-done((bf16[128,128]{1,0:T(8,128)(2,1)S(1)}, bf16[128,128]{1,0:T(8,128)(2,1)S(1)}, u32[]{:S(2)}, u32[]{:S(2)}) %collective-permute-start.21) | collective-permute-done | bytes 32800 | tf_op jit(solution)/shard_map/ppermute | solution.py:321
  51.9 0.7 %join.1 = bf16[128,512]{1,0:T(8,128)(2,1)} custom-call(bf16[128,128]{1,0:T(8,128)(2,1)S(1)} %get-tuple-element.51.refs_0_, bf16[128,128]{1,0:T(8,128)(2,1)S(1)} %collective-permute-done.19.refs_1_, bf16[128,128]{1,0:T(8,128)(2,1)S(1)} %collective-permute-done.20.refs_2_, bf16[128,128]{1,0:T(8,128)(2,1)S(1)} %collective-permute-done.21.refs_3_), custom_call_target="tpu_custom_call" | custom-call | tf_op jit(solution)/shard_map/join/pallas_call | solution.py:306
  (1 shorter events, 0.0 us)
Async XLA Ops:
  1.0 13.7 %collective-permute-start.6 = (bf16[256,512]{1,0:T(8,128)(2,1)S(1)}, bf16[256,512]{1,0:T(8,128)(2,1)S(1)}, u32[]{:S(2)}, u32[]{:S(2)}) collective-permute-start(bf16[256,512]{1,0:T(8,128)(2,1)S(1)} %stack.1.refs_0_), channel_id=1, source_target_pairs={{0,24},{2,26},{4,28},{6,30},{8,16},{10,18},{12,20},{14,22},{16,8},... | collective-permute-start | bytes 786440 | tf_op jit(solution)/shard_map/ppermute | solution.py:321
  1.5 13.3 %collective-permute-start.4 = (bf16[256,512]{1,0:T(8,128)(2,1)S(1)}, bf16[256,512]{1,0:T(8,128)(2,1)S(1)}, u32[]{:S(2)}, u32[]{:S(2)}) collective-permute-start(bf16[256,512]{1,0:T(8,128)(2,1)S(1)} %stack.1.refs_0_), channel_id=1, source_target_pairs={{0,8},{2,10},{4,12},{6,14},{8,0},{10,2},{12,4},{14,6},{16,24},{18,... | collective-permute-start | bytes 786440 | tf_op jit(solution)/shard_map/ppermute | solution.py:321
  4.1 11.0 %collective-permute-start = (bf16[1168,128]{1,0:T(8,128)(2,1)S(1)}, bf16[1168,128]{1,0:T(8,128)(2,1)S(1)}, u32[]{:S(2)}, u32[]{:S(2)}) collective-permute-start(bf16[1168,128]{1,0:T(8,128)(2,1)S(1)} %get-tuple-element.31), channel_id=1, source_target_pairs={{0,6},{2,4},{4,2},{6,0},{8,14},{10,12},{12,10},{14,8},{16,22},{18,... | collective-permute-start | bytes 897032 | tf_op jit(solution)/shard_map/ppermute | solution.py:321
  6.8 13.3 %collective-permute-start.1 = (bf16[1168,128]{1,0:T(8,128)(2,1)S(1)}, bf16[1168,128]{1,0:T(8,128)(2,1)S(1)}, u32[]{:S(2)}, u32[]{:S(2)}) collective-permute-start(bf16[1168,128]{1,0:T(8,128)(2,1)S(1)} %get-tuple-element.32), channel_id=1, source_target_pairs={{0,4},{2,6},{4,0},{6,2},{8,12},{10,14},{12,8},{14,10},{16,20},{18,... | collective-permute-start | bytes 897032 | tf_op jit(solution)/shard_map/ppermute | solution.py:321
  7.3 12.9 %collective-permute-start.2 = (bf16[1168,128]{1,0:T(8,128)(2,1)S(1)}, bf16[1168,128]{1,0:T(8,128)(2,1)S(1)}, u32[]{:S(2)}, u32[]{:S(2)}) collective-permute-start(bf16[1168,128]{1,0:T(8,128)(2,1)S(1)} %get-tuple-element.33), channel_id=1, source_target_pairs={{0,2},{2,0},{4,6},{6,4},{8,10},{10,8},{12,14},{14,12},{16,18},{18,... | collective-permute-start | bytes 897032 | tf_op jit(solution)/shard_map/ppermute | solution.py:321
  14.7 6.3 %collective-permute-start.13 = (bf16[128,512]{1,0:T(8,128)(2,1)S(1)}, bf16[128,512]{1,0:T(8,128)(2,1)S(1)}, u32[]{:S(2)}, u32[]{:S(2)}) collective-permute-start(bf16[128,512]{1,0:T(8,128)(2,1)S(1)} %get-tuple-element.55), channel_id=1, source_target_pairs={{0,8},{2,10},{4,12},{6,14},{8,0},{10,2},{12,4},{14,6},{16,24},{18,... | collective-permute-start | bytes 393224 | tf_op jit(solution)/shard_map/ppermute | solution.py:321
  14.8 7.6 %collective-permute-start.3 = (bf16[256,512]{1,0:T(8,128)(2,1)S(1)}, bf16[256,512]{1,0:T(8,128)(2,1)S(1)}, u32[]{:S(2)}, u32[]{:S(2)}) collective-permute-start(bf16[256,512]{1,0:T(8,128)(2,1)S(1)} %stack.1.refs_0_), channel_id=1, source_target_pairs={{0,1},{1,0},{2,3},{3,2},{4,5},{5,4},{6,7},{7,6},{8,9},{9,8},{10,11... | collective-permute-start | bytes 786440 | tf_op jit(solution)/shard_map/ppermute | solution.py:327
  15.1 7.3 %collective-permute-start.7 = (bf16[128,512]{1,0:T(8,128)(2,1)S(1)}, bf16[128,512]{1,0:T(8,128)(2,1)S(1)}, u32[]{:S(2)}, u32[]{:S(2)}) collective-permute-start(bf16[128,512]{1,0:T(8,128)(2,1)S(1)} %get-tuple-element.56), channel_id=1, source_target_pairs={{0,8},{2,10},{4,12},{6,14},{8,0},{10,2},{12,4},{14,6},{16,24},{18,... | collective-permute-start | bytes 393224 | tf_op jit(solution)/shard_map/ppermute | solution.py:321
  20.0 2.4 %collective-permute-start.9 = (bf16[256,512]{1,0:T(8,128)(2,1)S(1)}, bf16[256,512]{1,0:T(8,128)(2,1)S(1)}, u32[]{:S(2)}, u32[]{:S(2)}) collective-permute-start(bf16[256,512]{1,0:T(8,128)(2,1)S(1)} %collective-permute-done.6.refs_6_), channel_id=1, source_target_pairs={{0,1},{1,0},{2,3},{3,2},{4,5},{5,4},{6,7},{7,6},{8,9},{9,8},{10,11... | collective-permute-start | bytes 786440 | tf_op jit(solution)/shard_map/ppermute | solution.py:327
  20.1 2.3 %collective-permute-start.5 = (bf16[256,512]{1,0:T(8,128)(2,1)S(1)}, bf16[256,512]{1,0:T(8,128)(2,1)S(1)}, u32[]{:S(2)}, u32[]{:S(2)}) collective-permute-start(bf16[256,512]{1,0:T(8,128)(2,1)S(1)} %collective-permute-done.4.refs_2_), channel_id=1, source_target_pairs={{0,1},{1,0},{2,3},{3,2},{4,5},{5,4},{6,7},{7,6},{8,9},{9,8},{10,11... | collective-permute-start | bytes 786440 | tf_op jit(solution)/shard_map/ppermute | solution.py:327
  21.0 1.4 %collective-permute-start.14 = (bf16[128,512]{1,0:T(8,128)(2,1)S(1)}, bf16[128,512]{1,0:T(8,128)(2,1)S(1)}, u32[]{:S(2)}, u32[]{:S(2)}) collective-permute-start(bf16[128,512]{1,0:T(8,128)(2,1)S(1)} %collective-permute-done.13.refs_4_), channel_id=1, source_target_pairs={{0,1},{1,0},{2,3},{3,2},{4,5},{5,4},{6,7},{7,6},{8,9},{9,8},{10,11... | collective-permute-start | bytes 393224 | tf_op jit(solution)/shard_map/ppermute | solution.py:327
  22.4 4.3 %collective-permute-start.8 = (bf16[128,512]{1,0:T(8,128)(2,1)S(1)}, bf16[128,512]{1,0:T(8,128)(2,1)S(1)}, u32[]{:S(2)}, u32[]{:S(2)}) collective-permute-start(bf16[128,512]{1,0:T(8,128)(2,1)S(1)} %collective-permute-done.7.refs_4_), channel_id=1, source_target_pairs={{0,1},{1,0},{2,3},{3,2},{4,5},{5,4},{6,7},{7,6},{8,9},{9,8},{10,11... | collective-permute-start | bytes 393224 | tf_op jit(solution)/shard_map/ppermute | solution.py:327
  23.2 7.3 %collective-permute-start.15 = (bf16[512,128]{1,0:T(8,128)(2,1)S(1)}, bf16[512,128]{1,0:T(8,128)(2,1)S(1)}, u32[]{:S(2)}, u32[]{:S(2)}) collective-permute-start(bf16[512,128]{1,0:T(8,128)(2,1)S(1)} %get-tuple-element.40), channel_id=1, source_target_pairs={{0,6},{2,4},{4,2},{6,0},{8,14},{10,12},{12,10},{14,8},{16,22},{18,... | collective-permute-start | bytes 393224 | tf_op jit(solution)/shard_map/ppermute | solution.py:321
  25.7 7.9 %collective-permute-start.16 = (bf16[512,128]{1,0:T(8,128)(2,1)S(1)}, bf16[512,128]{1,0:T(8,128)(2,1)S(1)}, u32[]{:S(2)}, u32[]{:S(2)}) collective-permute-start(bf16[512,128]{1,0:T(8,128)(2,1)S(1)} %get-tuple-element.41), channel_id=1, source_target_pairs={{0,4},{2,6},{4,0},{6,2},{8,12},{10,14},{12,8},{14,10},{16,20},{18,... | collective-permute-start | bytes 393224 | tf_op jit(solution)/shard_map/ppermute | solution.py:321
  26.2 7.4 %collective-permute-start.17 = (bf16[512,128]{1,0:T(8,128)(2,1)S(1)}, bf16[512,128]{1,0:T(8,128)(2,1)S(1)}, u32[]{:S(2)}, u32[]{:S(2)}) collective-permute-start(bf16[512,128]{1,0:T(8,128)(2,1)S(1)} %get-tuple-element.42), channel_id=1, source_target_pairs={{0,2},{2,0},{4,6},{6,4},{8,10},{10,8},{12,14},{14,12},{16,18},{18,... | collective-permute-start | bytes 393224 | tf_op jit(solution)/shard_map/ppermute | solution.py:321
  27.5 8.9 %collective-permute-start.10 = (bf16[512,128]{1,0:T(8,128)(2,1)S(1)}, bf16[512,128]{1,0:T(8,128)(2,1)S(1)}, u32[]{:S(2)}, u32[]{:S(2)}) collective-permute-start(bf16[512,128]{1,0:T(8,128)(2,1)S(1)} %get-tuple-element.36), channel_id=1, source_target_pairs={{0,6},{2,4},{4,2},{6,0},{8,14},{10,12},{12,10},{14,8},{16,22},{18,... | collective-permute-start | bytes 393224 | tf_op jit(solution)/shard_map/ppermute | solution.py:321
  30.0 8.5 %collective-permute-start.11 = (bf16[512,128]{1,0:T(8,128)(2,1)S(1)}, bf16[512,128]{1,0:T(8,128)(2,1)S(1)}, u32[]{:S(2)}, u32[]{:S(2)}) collective-permute-start(bf16[512,128]{1,0:T(8,128)(2,1)S(1)} %get-tuple-element.37), channel_id=1, source_target_pairs={{0,4},{2,6},{4,0},{6,2},{8,12},{10,14},{12,8},{14,10},{16,20},{18,... | collective-permute-start | bytes 393224 | tf_op jit(solution)/shard_map/ppermute | solution.py:321
  30.5 8.1 %collective-permute-start.12 = (bf16[512,128]{1,0:T(8,128)(2,1)S(1)}, bf16[512,128]{1,0:T(8,128)(2,1)S(1)}, u32[]{:S(2)}, u32[]{:S(2)}) collective-permute-start(bf16[512,128]{1,0:T(8,128)(2,1)S(1)} %get-tuple-element.38), channel_id=1, source_target_pairs={{0,2},{2,0},{4,6},{6,4},{8,10},{10,8},{12,14},{14,12},{16,18},{18,... | collective-permute-start | bytes 393224 | tf_op jit(solution)/shard_map/ppermute | solution.py:321
  38.9 5.8 %collective-permute-start.18 = (bf16[128,128]{1,0:T(8,128)(2,1)S(1)}, bf16[128,128]{1,0:T(8,128)(2,1)S(1)}, u32[]{:S(2)}, u32[]{:S(2)}) collective-permute-start(bf16[128,128]{1,0:T(8,128)(2,1)S(1)} %get-tuple-element.47), channel_id=1, source_target_pairs={{8,16},{10,18},{12,20},{14,22},{9,17},{11,19},{13,21},{15,23}} | collective-permute-start | bytes 98312 | tf_op jit(solution)/shard_map/ppermute | solution.py:366
  40.4 4.3 %copy-start = (f32[512]{0:T(512)S(1)}, f32[512]{0:T(512)}, u32[]{:S(2)}) copy-start(f32[512]{0:T(512)} %param.11) | copy-start | bytes 6148
  45.0 4.9 %collective-permute-start.19 = (bf16[128,128]{1,0:T(8,128)(2,1)S(1)}, bf16[128,128]{1,0:T(8,128)(2,1)S(1)}, u32[]{:S(2)}, u32[]{:S(2)}) collective-permute-start(bf16[128,128]{1,0:T(8,128)(2,1)S(1)} %get-tuple-element.52), channel_id=1, source_target_pairs={{0,6},{2,4},{4,2},{6,0},{8,14},{10,12},{12,10},{14,8},{16,22},{18,... | collective-permute-start | bytes 98312 | tf_op jit(solution)/shard_map/ppermute | solution.py:321
  46.7 3.9 %collective-permute-start.20 = (bf16[128,128]{1,0:T(8,128)(2,1)S(1)}, bf16[128,128]{1,0:T(8,128)(2,1)S(1)}, u32[]{:S(2)}, u32[]{:S(2)}) collective-permute-start(bf16[128,128]{1,0:T(8,128)(2,1)S(1)} %get-tuple-element.53), channel_id=1, source_target_pairs={{0,4},{2,6},{4,0},{6,2},{8,12},{10,14},{12,8},{14,10},{16,20},{18,... | collective-permute-start | bytes 98312 | tf_op jit(solution)/shard_map/ppermute | solution.py:321
  48.0 3.9 %collective-permute-start.21 = (bf16[128,128]{1,0:T(8,128)(2,1)S(1)}, bf16[128,128]{1,0:T(8,128)(2,1)S(1)}, u32[]{:S(2)}, u32[]{:S(2)}) collective-permute-start(bf16[128,128]{1,0:T(8,128)(2,1)S(1)} %get-tuple-element.54), channel_id=1, source_target_pairs={{0,2},{2,0},{4,6},{6,4},{8,10},{10,8},{12,14},{14,12},{16,18},{18,... | collective-permute-start | bytes 98312 | tf_op jit(solution)/shard_map/ppermute | solution.py:321

commit v5 on v4

--- a/solution.py
+++ b/solution.py
@@ -328,28 +328,36 @@
 
     both = (w_key, w_value)
     split = outer == 4 and fsdp == 2 and rows == HEAD
+    share = fsdp * rows
     if split:
         weights = stack(*both)
         far = swap(weights, 3 * heads)
-        near = swap(weights, heads)
-    packed = pack(tokens[0], queries[0], flags, heads, fsdp * rows)
-    received = exchange(packed)
-    tok, query, first, seg_row, seg_col = assemble(received, heads, count, depth // heads, split)
-    if split:
+        packed = pack(tokens[0], queries[0], flags, heads, share)
+        weights2, *packed = lax.optimization_barrier((weights, *packed))
+        near = swap(weights2, heads)
+        received = list(exchange(packed))
         whole = [(w, other(w)) for w in (weights, near, far)]
-        panels = []
-        for at in (0, rows):
-            last = swap(far[at : at + rows], heads)
-            own, close, away = [[(w, at) for w in pair] for pair in whole]
-            panels.append(own + close + [(last, 0), (other(last), 0)] + away)
+        away = [far[:rows], far[rows:]]
+        last = [swap(away[0], heads)]
+        last.append(swap(away[1], heads))
+        across = other(last[0])
     else:
+        packed = pack(tokens[0], queries[0], flags, heads, share)
+        received = exchange(packed)
         groups = [[o * heads + q for o in range(outer)] for q in range(heads)]
         chip = [lax.all_gather(w, "fsdp", axis=0, tiled=True) for w in both]
-        panels = [
-            [(lax.all_gather(w, "ctx", axis=0, tiled=True, axis_index_groups=groups), 0)] for w in chip
-        ]
+        full = [lax.all_gather(w, "ctx", axis=0, tiled=True, axis_index_groups=groups) for w in chip]
+    tok, query, first, seg_row, seg_col = assemble(received, heads, count, depth // heads, split)
     parts = []
-    for panel, name in zip(panels, ("key_product", "value_product")):
+    for i, name in enumerate(("key_product", "value_product")):
+        if split:
+            if i == 1:
+                last[1], parts[0][0] = lax.optimization_barrier((last[1], parts[0][0]))
+                across = other(last[1])
+            own, close, distant = [[(w, i * rows) for w in pair] for pair in whole]
+            panel = own + close + [(last[i], 0), (across, 0)] + distant
+        else:
+            panel = [(full[i], 0)]
         partial = product(tok, panel, heads, name)
         parts.append(exchange(partial))
     key, scores = score(parts[0], query, seg_row, seg_col, heads)

time: 52.8 us -> 52.1 us (0.987)
  waiting for transfers between devices: 25.8 us -> 24.6 us
  starting transfers between devices: 20.5 us -> 21.1 us
    ppermute x16, waiting for transfers between devices: 21.5 us -> 19.6 us  [swap(): return lax.ppermute(a, 'ctx', [(i, i ^ mask) for i in range(n_ctx)])]
    ppermute x5, waiting for transfers between devices: 0.01 us -> 0.79 us  [other(): return lax.ppermute(a, 'fsdp', [(0, 1), (1, 0)])]
    ppermute x16, starting transfers between devices: 18.7 us -> 19.3 us  [swap(): return lax.ppermute(a, 'ctx', [(i, i ^ mask) for i in range(n_ctx)])]
  transfers between devices with their start and end apart: 22 -> 22, of which waited for: 14 -> 16; matrix products, arithmetic and copies ran while one was open for 0% -> 0% of each run, Pallas kernels for 7% -> 8%
where the time goes in v5:
time: 52.1 us; the launch traced here: 51.9 us
  waiting for transfers between devices  24.6 us (47%)
  starting transfers between devices  21.1 us (40%)
  Pallas kernels  6.12 us (12%)
    ppermute x16, waiting for transfers between devices, swap(): return lax.ppermute(a, 'ctx', [(i, i ^ mask) for i in range(n_ctx)])  19.6 us
    ppermute x16, starting transfers between devices, swap(): return lax.ppermute(a, 'ctx', [(i, i ^ mask) for i in range(n_ctx)])  19.3 us
    ppermute x1, waiting for transfers between devices, on_device(): carried = lax.ppermute(state.astype(BF), 'ctx', pairs)  4.26 us
    pallas_call x2, Pallas kernels, product(): pl.pallas_call(functools.partial(product_kernel, heads, [at for _, at in...  1.45 us
    pallas_call x1, Pallas kernels, pack(): pl.pallas_call(functools.partial(pack_kernel, heads), in_specs=[pl.BlockS...  1.39 us
    ppermute x1, starting transfers between devices, on_device(): carried = lax.ppermute(state.astype(BF), 'ctx', pairs)  1.29 us
  transfers between devices with their start and end apart: 22, of which 16 were waited for; matrix products, arithmetic and copies ran while one was open for 0% of the time, Pallas kernels for 8%

profile of v5, /device:TPU:16, one launch (start us, length us, event | category | flops | bytes accessed | tf_op | source)
XLA Modules:
  0.0 51.9 jit_solution(1232302550078208660)
XLA Ops:
  0.0 1.0 %stack.1.refs_0_ = bf16[256,512]{1,0:T(8,128)(2,1)S(1)} custom-call(bf16[128,512]{1,0:T(8,128)(2,1)} %refs_0_.1, bf16[128,512]{1,0:T(8,128)(2,1)} %refs_1_.1), custom_call_target="tpu_custom_call" | custom-call | tf_op jit(solution)/shard_map/stack/pallas_call | solution.py:52
  1.0 0.5 collective-permute-start.6
  1.5 1.4 %pack.1 = (bf16[1168,128]{1,0:T(8,128)(2,1)S(1)}, bf16[1168,128]{1,0:T(8,128)(2,1)S(1)}, bf16[1168,128]{1,0:T(8,128)(2,1)S(1)}, bf16[1168,128]{1,0:T(8,128)(2,1)S(1)}) custom-call(bf16[128,4096]{1,0:T(8,128)(2,1)} %bitcast.5, bf16[128,512]{1,0:T(8,128)(2,1)} %bitcast.6, s32[1,128]{1,0:T(1,128)} %flag_ref.1), custom_call_target="tpu_custom_call" | custom-call | tf_op jit(solution)/shard_map/pack/pallas_call | solution.py:103
  2.9 2.5 %collective-permute-start = (bf16[1168,128]{1,0:T(8,128)(2,1)S(1)}, bf16[1168,128]{1,0:T(8,128)(2,1)S(1)}, u32[]{:S(2)}, u32[]{:S(2)}) collective-permute-start(bf16[1168,128]{1,0:T(8,128)(2,1)S(1)} %get-tuple-element.42), channel_id=1, source_target_pairs={{0,6},{2,4},{4,2},{6,0},{8,14},{10,12},{12,10},{14,8},{16,22},{18,... | collective-permute-start | bytes 897032 | tf_op jit(solution)/shard_map/ppermute | solution.py:321
  5.4 0.5 collective-permute-start.1
  5.9 0.5 %collective-permute-start.2 = (bf16[1168,128]{1,0:T(8,128)(2,1)S(1)}, bf16[1168,128]{1,0:T(8,128)(2,1)S(1)}, u32[]{:S(2)}, u32[]{:S(2)}) collective-permute-start(bf16[1168,128]{1,0:T(8,128)(2,1)S(1)} %get-tuple-element.44), channel_id=1, source_target_pairs={{0,2},{2,0},{4,6},{6,4},{8,10},{10,8},{12,14},{14,12},{16,18},{18,... | collective-permute-start | bytes 897032 | tf_op jit(solution)/shard_map/ppermute | solution.py:321
  6.5 1.1 %collective-permute-start.4 = (bf16[256,512]{1,0:T(8,128)(2,1)S(1)}, bf16[256,512]{1,0:T(8,128)(2,1)S(1)}, u32[]{:S(2)}, u32[]{:S(2)}) collective-permute-start(bf16[256,512]{1,0:T(8,128)(2,1)S(1)} %stack.1.refs_0_), channel_id=1, source_target_pairs={{0,8},{2,10},{4,12},{6,14},{8,0},{10,2},{12,4},{14,6},{16,24},{18,... | collective-permute-start | bytes 786440 | tf_op jit(solution)/shard_map/ppermute | solution.py:321
  7.6 7.1 %collective-permute-done.6.refs_6_ = bf16[256,512]{1,0:T(8,128)(2,1)S(1)} collective-permute-done((bf16[256,512]{1,0:T(8,128)(2,1)S(1)}, bf16[256,512]{1,0:T(8,128)(2,1)S(1)}, u32[]{:S(2)}, u32[]{:S(2)}) %collective-permute-start.6) | collective-permute-done | bytes 262176 | tf_op jit(solution)/shard_map/ppermute | solution.py:321
  14.7 0.1 collective-permute-start.8
  14.8 1.0 %collective-permute-done.4.refs_2_ = bf16[256,512]{1,0:T(8,128)(2,1)S(1)} collective-permute-done((bf16[256,512]{1,0:T(8,128)(2,1)S(1)}, bf16[256,512]{1,0:T(8,128)(2,1)S(1)}, u32[]{:S(2)}, u32[]{:S(2)}) %collective-permute-start.4) | collective-permute-done | bytes 262176 | tf_op jit(solution)/shard_map/ppermute | solution.py:321
  15.8 0.0 collective-permute-start.3
  15.8 0.0 collective-permute-done.refs_1_
  15.8 2.5 %collective-permute-start.7 = (bf16[128,512]{1,0:T(8,128)(2,1)S(1)}, bf16[128,512]{1,0:T(8,128)(2,1)S(1)}, u32[]{:S(2)}, u32[]{:S(2)}) collective-permute-start(bf16[128,512]{1,0:T(8,128)(2,1)S(1)} %get-tuple-element.70), channel_id=1, source_target_pairs={{0,8},{2,10},{4,12},{6,14},{8,0},{10,2},{12,4},{14,6},{16,24},{18,... | collective-permute-start | bytes 393224 | tf_op jit(solution)/shard_map/ppermute | solution.py:321
  18.3 0.5 %collective-permute-done.1.refs_2_ = bf16[1168,128]{1,0:T(8,128)(2,1)S(1)} collective-permute-done((bf16[1168,128]{1,0:T(8,128)(2,1)S(1)}, bf16[1168,128]{1,0:T(8,128)(2,1)S(1)}, u32[]{:S(2)}, u32[]{:S(2)}) %collective-permute-start.1) | collective-permute-done | bytes 299040 | tf_op jit(solution)/shard_map/ppermute | solution.py:321
  18.8 0.0 collective-permute-start.10
  18.9 0.1 collective-permute-done.2.refs_3_
  18.9 0.4 collective-permute-start.5
  19.3 0.5 collective-permute-done.8.refs_4_
  19.9 0.0 collective-permute-start.9
  19.9 0.5 %assemble.1 = (bf16[512,1024]{1,0:T(8,128)(2,1)S(1)}, bf16[512,128]{1,0:T(8,128)(2,1)S(1)}, bf16[512,128]{1,0:T(8,128)(2,1)S(1)}, f32[8,512]{1,0:T(8,128)S(1)}, f32[512,128]{1,0:T(8,128)S(1)}) custom-call(bf16[1168,128]{1,0:T(8,128)(2,1)S(1)} %get-tuple-element.41.refs_0_, bf16[1168,128]{1,0:T(8,128)(2,1)S(1)} %collective-permute-done.refs_1_, ...), custom_call_target="tpu_custom_call" | custom-call | flops 4000000000 | tf_op jit(solution)/shard_map/assemble/pallas_call | solution.py:159
  20.4 0.0 collective-permute-done.3.refs_1_
  20.4 0.3 collective-permute-done.5.refs_3_
  20.7 0.5 collective-permute-done.9.refs_5_
  21.2 0.0 collective-permute-done.10.refs_7_
  21.2 0.7 %key_product.1 = (f32[512,128]{1,0:T(8,128)S(1)}, bf16[512,128]{1,0:T(8,128)(2,1)S(1)}, bf16[512,128]{1,0:T(8,128)(2,1)S(1)}, bf16[512,128]{1,0:T(8,128)(2,1)S(1)}) custom-call(bf16[512,1024]{1,0:T(8,128)(2,1)S(1)} %get-tuple-element.45.tok, bf16[256,512]{1,0:T(8,128)(2,1)S(1)} %stack.1.refs_0_, bf16[256,512]{1,0:T(8,128)(2,1)S(1)} %collective-permute-done.3.refs_1_, ...), custom_call_target="tpu_custom_call" | custom-call | tf_op jit(solution)/shard_map/key_product/pallas_call | solution.py:194
  21.9 0.6 %collective-permute-done.7.refs_4_ = bf16[128,512]{1,0:T(8,128)(2,1)S(1)} collective-permute-done((bf16[128,512]{1,0:T(8,128)(2,1)S(1)}, bf16[128,512]{1,0:T(8,128)(2,1)S(1)}, u32[]{:S(2)}, u32[]{:S(2)}) %collective-permute-start.7) | collective-permute-done | bytes 131104 | tf_op jit(solution)/shard_map/ppermute | solution.py:321
  22.6 0.0 collective-permute-start.11
  22.6 2.4 %collective-permute-start.15 = (bf16[512,128]{1,0:T(8,128)(2,1)S(1)}, bf16[512,128]{1,0:T(8,128)(2,1)S(1)}, u32[]{:S(2)}, u32[]{:S(2)}) collective-permute-start(bf16[512,128]{1,0:T(8,128)(2,1)S(1)} %get-tuple-element.54), channel_id=1, source_target_pairs={{0,6},{2,4},{4,2},{6,0},{8,14},{10,12},{12,10},{14,8},{16,22},{18,... | collective-permute-start | bytes 393224 | tf_op jit(solution)/shard_map/ppermute | solution.py:321
  25.1 0.5 collective-permute-start.16
  25.6 0.5 %collective-permute-start.17 = (bf16[512,128]{1,0:T(8,128)(2,1)S(1)}, bf16[512,128]{1,0:T(8,128)(2,1)S(1)}, u32[]{:S(2)}, u32[]{:S(2)}) collective-permute-start(bf16[512,128]{1,0:T(8,128)(2,1)S(1)} %get-tuple-element.56), channel_id=1, source_target_pairs={{0,2},{2,0},{4,6},{6,4},{8,10},{10,8},{12,14},{14,12},{16,18},{18,... | collective-permute-start | bytes 393224 | tf_op jit(solution)/shard_map/ppermute | solution.py:321
  26.1 0.0 collective-permute-done.11.refs_5_
  26.1 0.7 %value_product.1 = (f32[512,128]{1,0:T(8,128)S(1)}, bf16[512,128]{1,0:T(8,128)(2,1)S(1)}, bf16[512,128]{1,0:T(8,128)(2,1)S(1)}, bf16[512,128]{1,0:T(8,128)(2,1)S(1)}) custom-call(bf16[512,1024]{1,0:T(8,128)(2,1)S(1)} %get-tuple-element.45.tok, bf16[256,512]{1,0:T(8,128)(2,1)S(1)} %stack.1.refs_0_, bf16[256,512]{1,0:T(8,128)(2,1)S(1)} %collective-permute-done.3.refs_1_, ...), custom_call_target="tpu_custom_call" | custom-call | tf_op jit(solution)/shard_map/value_product/pallas_call | solution.py:194
  26.8 2.5 %collective-permute-start.12 = (bf16[512,128]{1,0:T(8,128)(2,1)S(1)}, bf16[512,128]{1,0:T(8,128)(2,1)S(1)}, u32[]{:S(2)}, u32[]{:S(2)}) collective-permute-start(bf16[512,128]{1,0:T(8,128)(2,1)S(1)} %get-tuple-element.50), channel_id=1, source_target_pairs={{0,6},{2,4},{4,2},{6,0},{8,14},{10,12},{12,10},{14,8},{16,22},{18,... | collective-permute-start | bytes 393224 | tf_op jit(solution)/shard_map/ppermute | solution.py:321
  29.3 0.5 collective-permute-start.13
  29.9 0.0 collective-permute-done.15.refs_1_
  29.9 1.5 %collective-permute-start.14 = (bf16[512,128]{1,0:T(8,128)(2,1)S(1)}, bf16[512,128]{1,0:T(8,128)(2,1)S(1)}, u32[]{:S(2)}, u32[]{:S(2)}) collective-permute-start(bf16[512,128]{1,0:T(8,128)(2,1)S(1)} %get-tuple-element.52), channel_id=1, source_target_pairs={{0,2},{2,0},{4,6},{6,4},{8,10},{10,8},{12,14},{14,12},{16,18},{18,... | collective-permute-start | bytes 393224 | tf_op jit(solution)/shard_map/ppermute | solution.py:321
  31.3 1.6 %collective-permute-done.16.refs_2_ = bf16[512,128]{1,0:T(8,128)(2,1)S(1)} collective-permute-done((bf16[512,128]{1,0:T(8,128)(2,1)S(1)}, bf16[512,128]{1,0:T(8,128)(2,1)S(1)}, u32[]{:S(2)}, u32[]{:S(2)}) %collective-permute-start.16) | collective-permute-done | bytes 131104 | tf_op jit(solution)/shard_map/ppermute | solution.py:321
  33.0 0.0 collective-permute-done.17.refs_3_
  33.0 0.3 score.1
  33.3 2.5 %collective-permute-done.12.refs_1_ = bf16[512,128]{1,0:T(8,128)(2,1)S(1)} collective-permute-done((bf16[512,128]{1,0:T(8,128)(2,1)S(1)}, bf16[512,128]{1,0:T(8,128)(2,1)S(1)}, u32[]{:S(2)}, u32[]{:S(2)}) %collective-permute-start.12) | collective-permute-done | bytes 131104 | tf_op jit(solution)/shard_map/ppermute | solution.py:321
  35.8 2.1 %collective-permute-done.13.refs_2_ = bf16[512,128]{1,0:T(8,128)(2,1)S(1)} collective-permute-done((bf16[512,128]{1,0:T(8,128)(2,1)S(1)}, bf16[512,128]{1,0:T(8,128)(2,1)S(1)}, u32[]{:S(2)}, u32[]{:S(2)}) %collective-permute-start.13) | collective-permute-done | bytes 131104 | tf_op jit(solution)/shard_map/ppermute | solution.py:321
  37.8 0.1 collective-permute-done.14.refs_3_
  38.0 0.2 state.1
  38.2 1.3 %collective-permute-start.18 = (bf16[128,128]{1,0:T(8,128)(2,1)S(1)}, bf16[128,128]{1,0:T(8,128)(2,1)S(1)}, u32[]{:S(2)}, u32[]{:S(2)}) collective-permute-start(bf16[128,128]{1,0:T(8,128)(2,1)S(1)} %get-tuple-element.61), channel_id=1, source_target_pairs={{8,16},{10,18},{12,20},{14,22},{9,17},{11,19},{13,21},{15,23}} | collective-permute-start | bytes 98312 | tf_op jit(solution)/shard_map/ppermute | solution.py:374
  39.5 0.2 within.1.inside
  39.7 0.0 copy-start
  39.8 4.3 %collective-permute-done.18.carried = bf16[128,128]{1,0:T(8,128)(2,1)S(1)} collective-permute-done((bf16[128,128]{1,0:T(8,128)(2,1)S(1)}, bf16[128,128]{1,0:T(8,128)(2,1)S(1)}, u32[]{:S(2)}, u32[]{:S(2)}) %collective-permute-start.18) | collective-permute-done | bytes 32800 | tf_op jit(solution)/shard_map/ppermute | solution.py:374
  44.0 0.0 copy-done
  44.0 0.3 finish.1
  44.3 1.7 %collective-permute-start.19 = (bf16[128,128]{1,0:T(8,128)(2,1)S(1)}, bf16[128,128]{1,0:T(8,128)(2,1)S(1)}, u32[]{:S(2)}, u32[]{:S(2)}) collective-permute-start(bf16[128,128]{1,0:T(8,128)(2,1)S(1)} %get-tuple-element.66), channel_id=1, source_target_pairs={{0,6},{2,4},{4,2},{6,0},{8,14},{10,12},{12,10},{14,8},{16,22},{18,... | collective-permute-start | bytes 98312 | tf_op jit(solution)/shard_map/ppermute | solution.py:321
  46.0 1.3 %collective-permute-start.20 = (bf16[128,128]{1,0:T(8,128)(2,1)S(1)}, bf16[128,128]{1,0:T(8,128)(2,1)S(1)}, u32[]{:S(2)}, u32[]{:S(2)}) collective-permute-start(bf16[128,128]{1,0:T(8,128)(2,1)S(1)} %get-tuple-element.67), channel_id=1, source_target_pairs={{0,4},{2,6},{4,0},{6,2},{8,12},{10,14},{12,8},{14,10},{16,20},{18,... | collective-permute-start | bytes 98312 | tf_op jit(solution)/shard_map/ppermute | solution.py:321
  47.4 0.5 %collective-permute-start.21 = (bf16[128,128]{1,0:T(8,128)(2,1)S(1)}, bf16[128,128]{1,0:T(8,128)(2,1)S(1)}, u32[]{:S(2)}, u32[]{:S(2)}) collective-permute-start(bf16[128,128]{1,0:T(8,128)(2,1)S(1)} %get-tuple-element.68), channel_id=1, source_target_pairs={{0,2},{2,0},{4,6},{6,4},{8,10},{10,8},{12,14},{14,12},{16,18},{18,... | collective-permute-start | bytes 98312 | tf_op jit(solution)/shard_map/ppermute | solution.py:321
  47.9 1.3 %collective-permute-done.19.refs_1_ = bf16[128,128]{1,0:T(8,128)(2,1)S(1)} collective-permute-done((bf16[128,128]{1,0:T(8,128)(2,1)S(1)}, bf16[128,128]{1,0:T(8,128)(2,1)S(1)}, u32[]{:S(2)}, u32[]{:S(2)}) %collective-permute-start.19) | collective-permute-done | bytes 32800 | tf_op jit(solution)/shard_map/ppermute | solution.py:321
  49.2 0.7 %collective-permute-done.20.refs_2_ = bf16[128,128]{1,0:T(8,128)(2,1)S(1)} collective-permute-done((bf16[128,128]{1,0:T(8,128)(2,1)S(1)}, bf16[128,128]{1,0:T(8,128)(2,1)S(1)}, u32[]{:S(2)}, u32[]{:S(2)}) %collective-permute-start.20) | collective-permute-done | bytes 32800 | tf_op jit(solution)/shard_map/ppermute | solution.py:321
  49.9 1.3 %collective-permute-done.21.refs_3_ = bf16[128,128]{1,0:T(8,128)(2,1)S(1)} collective-permute-done((bf16[128,128]{1,0:T(8,128)(2,1)S(1)}, bf16[128,128]{1,0:T(8,128)(2,1)S(1)}, u32[]{:S(2)}, u32[]{:S(2)}) %collective-permute-start.21) | collective-permute-done | bytes 32800 | tf_op jit(solution)/shard_map/ppermute | solution.py:321
  51.3 0.7 %join.1 = bf16[128,512]{1,0:T(8,128)(2,1)} custom-call(bf16[128,128]{1,0:T(8,128)(2,1)S(1)} %get-tuple-element.65.refs_0_, bf16[128,128]{1,0:T(8,128)(2,1)S(1)} %collective-permute-done.19.refs_1_, bf16[128,128]{1,0:T(8,128)(2,1)S(1)} %collective-permute-done.20.refs_2_, bf16[128,128]{1,0:T(8,128)(2,1)S(1)} %collective-permute-done.21.refs_3_), custom_call_target="tpu_custom_call" | custom-call | tf_op jit(solution)/shard_map/join/pallas_call | solution.py:306
  (1 shorter events, 0.0 us)
Async XLA Ops:
  1.0 13.7 %collective-permute-start.6 = (bf16[256,512]{1,0:T(8,128)(2,1)S(1)}, bf16[256,512]{1,0:T(8,128)(2,1)S(1)}, u32[]{:S(2)}, u32[]{:S(2)}) collective-permute-start(bf16[256,512]{1,0:T(8,128)(2,1)S(1)} %stack.1.refs_0_), channel_id=1, source_target_pairs={{0,24},{2,26},{4,28},{6,30},{8,16},{10,18},{12,20},{14,22},{16,8},... | collective-permute-start | bytes 786440 | tf_op jit(solution)/shard_map/ppermute | solution.py:321
  2.9 12.9 %collective-permute-start = (bf16[1168,128]{1,0:T(8,128)(2,1)S(1)}, bf16[1168,128]{1,0:T(8,128)(2,1)S(1)}, u32[]{:S(2)}, u32[]{:S(2)}) collective-permute-start(bf16[1168,128]{1,0:T(8,128)(2,1)S(1)} %get-tuple-element.42), channel_id=1, source_target_pairs={{0,6},{2,4},{4,2},{6,0},{8,14},{10,12},{12,10},{14,8},{16,22},{18,... | collective-permute-start | bytes 897032 | tf_op jit(solution)/shard_map/ppermute | solution.py:321
  5.4 13.4 %collective-permute-start.1 = (bf16[1168,128]{1,0:T(8,128)(2,1)S(1)}, bf16[1168,128]{1,0:T(8,128)(2,1)S(1)}, u32[]{:S(2)}, u32[]{:S(2)}) collective-permute-start(bf16[1168,128]{1,0:T(8,128)(2,1)S(1)} %get-tuple-element.43), channel_id=1, source_target_pairs={{0,4},{2,6},{4,0},{6,2},{8,12},{10,14},{12,8},{14,10},{16,20},{18,... | collective-permute-start | bytes 897032 | tf_op jit(solution)/shard_map/ppermute | solution.py:321
  5.9 13.0 %collective-permute-start.2 = (bf16[1168,128]{1,0:T(8,128)(2,1)S(1)}, bf16[1168,128]{1,0:T(8,128)(2,1)S(1)}, u32[]{:S(2)}, u32[]{:S(2)}) collective-permute-start(bf16[1168,128]{1,0:T(8,128)(2,1)S(1)} %get-tuple-element.44), channel_id=1, source_target_pairs={{0,2},{2,0},{4,6},{6,4},{8,10},{10,8},{12,14},{14,12},{16,18},{18,... | collective-permute-start | bytes 897032 | tf_op jit(solution)/shard_map/ppermute | solution.py:321
  6.5 9.3 %collective-permute-start.4 = (bf16[256,512]{1,0:T(8,128)(2,1)S(1)}, bf16[256,512]{1,0:T(8,128)(2,1)S(1)}, u32[]{:S(2)}, u32[]{:S(2)}) collective-permute-start(bf16[256,512]{1,0:T(8,128)(2,1)S(1)} %stack.1.refs_0_), channel_id=1, source_target_pairs={{0,8},{2,10},{4,12},{6,14},{8,0},{10,2},{12,4},{14,6},{16,24},{18,... | collective-permute-start | bytes 786440 | tf_op jit(solution)/shard_map/ppermute | solution.py:321
  14.7 5.1 %collective-permute-start.8 = (bf16[128,512]{1,0:T(8,128)(2,1)S(1)}, bf16[128,512]{1,0:T(8,128)(2,1)S(1)}, u32[]{:S(2)}, u32[]{:S(2)}) collective-permute-start(bf16[128,512]{1,0:T(8,128)(2,1)S(1)} %get-tuple-element.69), channel_id=1, source_target_pairs={{0,8},{2,10},{4,12},{6,14},{8,0},{10,2},{12,4},{14,6},{16,24},{18,... | collective-permute-start | bytes 393224 | tf_op jit(solution)/shard_map/ppermute | solution.py:321
  15.8 4.6 %collective-permute-start.3 = (bf16[256,512]{1,0:T(8,128)(2,1)S(1)}, bf16[256,512]{1,0:T(8,128)(2,1)S(1)}, u32[]{:S(2)}, u32[]{:S(2)}) collective-permute-start(bf16[256,512]{1,0:T(8,128)(2,1)S(1)} %stack.1.refs_0_), channel_id=1, source_target_pairs={{0,1},{1,0},{2,3},{3,2},{4,5},{5,4},{6,7},{7,6},{8,9},{9,8},{10,11... | collective-permute-start | bytes 786440 | tf_op jit(solution)/shard_map/ppermute | solution.py:327
  15.8 6.8 %collective-permute-start.7 = (bf16[128,512]{1,0:T(8,128)(2,1)S(1)}, bf16[128,512]{1,0:T(8,128)(2,1)S(1)}, u32[]{:S(2)}, u32[]{:S(2)}) collective-permute-start(bf16[128,512]{1,0:T(8,128)(2,1)S(1)} %get-tuple-element.70), channel_id=1, source_target_pairs={{0,8},{2,10},{4,12},{6,14},{8,0},{10,2},{12,4},{14,6},{16,24},{18,... | collective-permute-start | bytes 393224 | tf_op jit(solution)/shard_map/ppermute | solution.py:321
  18.8 2.4 %collective-permute-start.10 = (bf16[256,512]{1,0:T(8,128)(2,1)S(1)}, bf16[256,512]{1,0:T(8,128)(2,1)S(1)}, u32[]{:S(2)}, u32[]{:S(2)}) collective-permute-start(bf16[256,512]{1,0:T(8,128)(2,1)S(1)} %collective-permute-done.6.refs_6_), channel_id=1, source_target_pairs={{0,1},{1,0},{2,3},{3,2},{4,5},{5,4},{6,7},{7,6},{8,9},{9,8},{10,11... | collective-permute-start | bytes 786440 | tf_op jit(solution)/shard_map/ppermute | solution.py:327
  18.9 1.8 %collective-permute-start.5 = (bf16[256,512]{1,0:T(8,128)(2,1)S(1)}, bf16[256,512]{1,0:T(8,128)(2,1)S(1)}, u32[]{:S(2)}, u32[]{:S(2)}) collective-permute-start(bf16[256,512]{1,0:T(8,128)(2,1)S(1)} %collective-permute-done.4.refs_2_), channel_id=1, source_target_pairs={{0,1},{1,0},{2,3},{3,2},{4,5},{5,4},{6,7},{7,6},{8,9},{9,8},{10,11... | collective-permute-start | bytes 786440 | tf_op jit(solution)/shard_map/ppermute | solution.py:327
  19.9 1.3 %collective-permute-start.9 = (bf16[128,512]{1,0:T(8,128)(2,1)S(1)}, bf16[128,512]{1,0:T(8,128)(2,1)S(1)}, u32[]{:S(2)}, u32[]{:S(2)}) collective-permute-start(bf16[128,512]{1,0:T(8,128)(2,1)S(1)} %collective-permute-done.8.refs_4_), channel_id=1, source_target_pairs={{0,1},{1,0},{2,3},{3,2},{4,5},{5,4},{6,7},{7,6},{8,9},{9,8},{10,11... | collective-permute-start | bytes 393224 | tf_op jit(solution)/shard_map/ppermute | solution.py:327
  22.6 3.5 %collective-permute-start.11 = (bf16[128,512]{1,0:T(8,128)(2,1)S(1)}, bf16[128,512]{1,0:T(8,128)(2,1)S(1)}, u32[]{:S(2)}, u32[]{:S(2)}) collective-permute-start(bf16[128,512]{1,0:T(8,128)(2,1)S(1)} %collective-permute-done.7.refs_4_), channel_id=1, source_target_pairs={{0,1},{1,0},{2,3},{3,2},{4,5},{5,4},{6,7},{7,6},{8,9},{9,8},{10,11... | collective-permute-start | bytes 393224 | tf_op jit(solution)/shard_map/ppermute | solution.py:327
  22.6 7.2 %collective-permute-start.15 = (bf16[512,128]{1,0:T(8,128)(2,1)S(1)}, bf16[512,128]{1,0:T(8,128)(2,1)S(1)}, u32[]{:S(2)}, u32[]{:S(2)}) collective-permute-start(bf16[512,128]{1,0:T(8,128)(2,1)S(1)} %get-tuple-element.54), channel_id=1, source_target_pairs={{0,6},{2,4},{4,2},{6,0},{8,14},{10,12},{12,10},{14,8},{16,22},{18,... | collective-permute-start | bytes 393224 | tf_op jit(solution)/shard_map/ppermute | solution.py:321
  25.1 7.9 %collective-permute-start.16 = (bf16[512,128]{1,0:T(8,128)(2,1)S(1)}, bf16[512,128]{1,0:T(8,128)(2,1)S(1)}, u32[]{:S(2)}, u32[]{:S(2)}) collective-permute-start(bf16[512,128]{1,0:T(8,128)(2,1)S(1)} %get-tuple-element.55), channel_id=1, source_target_pairs={{0,4},{2,6},{4,0},{6,2},{8,12},{10,14},{12,8},{14,10},{16,20},{18,... | collective-permute-start | bytes 393224 | tf_op jit(solution)/shard_map/ppermute | solution.py:321
  25.6 7.4 %collective-permute-start.17 = (bf16[512,128]{1,0:T(8,128)(2,1)S(1)}, bf16[512,128]{1,0:T(8,128)(2,1)S(1)}, u32[]{:S(2)}, u32[]{:S(2)}) collective-permute-start(bf16[512,128]{1,0:T(8,128)(2,1)S(1)} %get-tuple-element.56), channel_id=1, source_target_pairs={{0,2},{2,0},{4,6},{6,4},{8,10},{10,8},{12,14},{14,12},{16,18},{18,... | collective-permute-start | bytes 393224 | tf_op jit(solution)/shard_map/ppermute | solution.py:321
  26.8 8.9 %collective-permute-start.12 = (bf16[512,128]{1,0:T(8,128)(2,1)S(1)}, bf16[512,128]{1,0:T(8,128)(2,1)S(1)}, u32[]{:S(2)}, u32[]{:S(2)}) collective-permute-start(bf16[512,128]{1,0:T(8,128)(2,1)S(1)} %get-tuple-element.50), channel_id=1, source_target_pairs={{0,6},{2,4},{4,2},{6,0},{8,14},{10,12},{12,10},{14,8},{16,22},{18,... | collective-permute-start | bytes 393224 | tf_op jit(solution)/shard_map/ppermute | solution.py:321
  29.3 8.5 %collective-permute-start.13 = (bf16[512,128]{1,0:T(8,128)(2,1)S(1)}, bf16[512,128]{1,0:T(8,128)(2,1)S(1)}, u32[]{:S(2)}, u32[]{:S(2)}) collective-permute-start(bf16[512,128]{1,0:T(8,128)(2,1)S(1)} %get-tuple-element.51), channel_id=1, source_target_pairs={{0,4},{2,6},{4,0},{6,2},{8,12},{10,14},{12,8},{14,10},{16,20},{18,... | collective-permute-start | bytes 393224 | tf_op jit(solution)/shard_map/ppermute | solution.py:321
  29.9 8.1 %collective-permute-start.14 = (bf16[512,128]{1,0:T(8,128)(2,1)S(1)}, bf16[512,128]{1,0:T(8,128)(2,1)S(1)}, u32[]{:S(2)}, u32[]{:S(2)}) collective-permute-start(bf16[512,128]{1,0:T(8,128)(2,1)S(1)} %get-tuple-element.52), channel_id=1, source_target_pairs={{0,2},{2,0},{4,6},{6,4},{8,10},{10,8},{12,14},{14,12},{16,18},{18,... | collective-permute-start | bytes 393224 | tf_op jit(solution)/shard_map/ppermute | solution.py:321
  38.2 5.8 %collective-permute-start.18 = (bf16[128,128]{1,0:T(8,128)(2,1)S(1)}, bf16[128,128]{1,0:T(8,128)(2,1)S(1)}, u32[]{:S(2)}, u32[]{:S(2)}) collective-permute-start(bf16[128,128]{1,0:T(8,128)(2,1)S(1)} %get-tuple-element.61), channel_id=1, source_target_pairs={{8,16},{10,18},{12,20},{14,22},{9,17},{11,19},{13,21},{15,23}} | collective-permute-start | bytes 98312 | tf_op jit(solution)/shard_map/ppermute | solution.py:374
  39.7 4.3 %copy-start = (f32[512]{0:T(512)S(1)}, f32[512]{0:T(512)}, u32[]{:S(2)}) copy-start(f32[512]{0:T(512)} %param.11) | copy-start | bytes 6148
  44.3 4.9 %collective-permute-start.19 = (bf16[128,128]{1,0:T(8,128)(2,1)S(1)}, bf16[128,128]{1,0:T(8,128)(2,1)S(1)}, u32[]{:S(2)}, u32[]{:S(2)}) collective-permute-start(bf16[128,128]{1,0:T(8,128)(2,1)S(1)} %get-tuple-element.66), channel_id=1, source_target_pairs={{0,6},{2,4},{4,2},{6,0},{8,14},{10,12},{12,10},{14,8},{16,22},{18,... | collective-permute-start | bytes 98312 | tf_op jit(solution)/shard_map/ppermute | solution.py:321
  46.0 3.9 %collective-permute-start.20 = (bf16[128,128]{1,0:T(8,128)(2,1)S(1)}, bf16[128,128]{1,0:T(8,128)(2,1)S(1)}, u32[]{:S(2)}, u32[]{:S(2)}) collective-permute-start(bf16[128,128]{1,0:T(8,128)(2,1)S(1)} %get-tuple-element.67), channel_id=1, source_target_pairs={{0,4},{2,6},{4,0},{6,2},{8,12},{10,14},{12,8},{14,10},{16,20},{18,... | collective-permute-start | bytes 98312 | tf_op jit(solution)/shard_map/ppermute | solution.py:321
  47.4 3.9 %collective-permute-start.21 = (bf16[128,128]{1,0:T(8,128)(2,1)S(1)}, bf16[128,128]{1,0:T(8,128)(2,1)S(1)}, u32[]{:S(2)}, u32[]{:S(2)}) collective-permute-start(bf16[128,128]{1,0:T(8,128)(2,1)S(1)} %get-tuple-element.68), channel_id=1, source_target_pairs={{0,2},{2,0},{4,6},{6,4},{8,10},{10,8},{12,14},{14,12},{16,18},{18,... | collective-permute-start | bytes 98312 | tf_op jit(solution)/shard_map/ppermute | solution.py:321

commit v6 on v5

--- a/solution.py
+++ b/solution.py
@@ -61,7 +61,7 @@
 
 
 def partners(heads):
-    return [0] + list(range(heads - 1, 0, -1))
+    return [0, heads - 1] + list(range(1, heads - 1))
 
 
 def pack_kernel(heads, tok_ref, query_ref, flag_ref, *refs):
@@ -177,9 +177,14 @@
     inner, _ = inner_outer(heads)
     rows = tok.shape[1] // len(places)
 
+    def rows_at(at):
+        if at is None:
+            return aligned(1 - lax.axis_index("fsdp"), rows)
+        return slice(at, at + rows)
+
     def panel(k):
         cols = aligned(jnp.bitwise_xor(inner, k), HEAD)
-        return jnp.concatenate([w[at : at + rows, cols] for w, at in zip(w_refs, places)], axis=0)
+        return jnp.concatenate([w[rows_at(at), cols] for w, at in zip(w_refs, places)], axis=0)
 
     order = list(range(1, heads)) + [0]
     for a, b in zip(order[::2], order[1::2]):
@@ -333,8 +338,8 @@
         weights = stack(*both)
         far = swap(weights, 3 * heads)
         packed = pack(tokens[0], queries[0], flags, heads, share)
-        weights2, *packed = lax.optimization_barrier((weights, *packed))
-        near = swap(weights2, heads)
+        held, *packed = lax.optimization_barrier((weights, *packed))
+        near = swap(held, heads)
         received = list(exchange(packed))
         whole = [(w, other(w)) for w in (weights, near, far)]
         away = [far[:rows], far[rows:]]
@@ -353,9 +358,9 @@
         if split:
             if i == 1:
                 last[1], parts[0][0] = lax.optimization_barrier((last[1], parts[0][0]))
-                across = other(last[1])
+                across = lax.all_gather(last[1], "fsdp", axis=0, tiled=True)
             own, close, distant = [[(w, i * rows) for w in pair] for pair in whole]
-            panel = own + close + [(last[i], 0), (across, 0)] + distant
+            panel = own + close + [(last[i], 0), (across, None if i else 0)] + distant
         else:
             panel = [(full[i], 0)]
         partial = product(tok, panel, heads, name)

time: 52.1 us -> 51.7 us (level)
  blocking collectives: 0 us -> 1.98 us
  waiting for transfers between devices: 24.6 us -> 23.1 us
  starting transfers between devices: 21.1 us -> 20.2 us
    all_gather x0 -> x1, blocking collectives: none -> 1.98 us  [on_device(): across = lax.all_gather(last[1], 'fsdp', axis=0, tiled=True)]
    ppermute x16, waiting for transfers between devices: 19.6 us -> 18 us  [swap(): return lax.ppermute(a, 'ctx', [(i, i ^ mask) for i in range(n_ctx)])]
    ppermute x16, starting transfers between devices: 19.3 us -> 18.4 us  [swap(): return lax.ppermute(a, 'ctx', [(i, i ^ mask) for i in range(n_ctx)])]
  transfers between devices with their start and end apart: 22 -> 21, of which waited for: 16 -> 12; matrix products, arithmetic and copies ran while one was open for 0% -> 0% of each run, Pallas kernels for 8% -> 8%
where the time goes in v6:
time: 51.7 us; the launch traced here: 51.5 us
  waiting for transfers between devices  23.1 us (45%)
  starting transfers between devices  20.2 us (39%)
  Pallas kernels  6.13 us (12%)
  blocking collectives  1.98 us (4%)
    ppermute x16, starting transfers between devices, swap(): return lax.ppermute(a, 'ctx', [(i, i ^ mask) for i in range(n_ctx)])  18.4 us
    ppermute x16, waiting for transfers between devices, swap(): return lax.ppermute(a, 'ctx', [(i, i ^ mask) for i in range(n_ctx)])  18 us
    ppermute x1, waiting for transfers between devices, on_device(): carried = lax.ppermute(state.astype(BF), 'ctx', pairs)  4.26 us
    all_gather x1, blocking collectives, on_device(): across = lax.all_gather(last[1], 'fsdp', axis=0, tiled=True)  1.98 us
    pallas_call x2, Pallas kernels, product(): pl.pallas_call(functools.partial(product_kernel, heads, [at for _, at in...  1.45 us
    pallas_call x1, Pallas kernels, pack(): pl.pallas_call(functools.partial(pack_kernel, heads), in_specs=[pl.BlockS...  1.39 us
    ppermute x1, starting transfers between devices, on_device(): carried = lax.ppermute(state.astype(BF), 'ctx', pairs)  1.29 us
  transfers between devices with their start and end apart: 21, of which 12 were waited for; matrix products, arithmetic and copies ran while one was open for 0% of the time, Pallas kernels for 8%

profile of v6, /device:TPU:16, one launch (start us, length us, event | category | flops | bytes accessed | tf_op | source)
XLA Modules:
  0.0 51.5 jit_solution(7687438887598233273)
XLA Ops:
  0.0 1.0 %stack.1.refs_0_ = bf16[256,512]{1,0:T(8,128)(2,1)S(1)} custom-call(bf16[128,512]{1,0:T(8,128)(2,1)} %refs_0_.1, bf16[128,512]{1,0:T(8,128)(2,1)} %refs_1_.1), custom_call_target="tpu_custom_call" | custom-call | tf_op jit(solution)/shard_map/stack/pallas_call | solution.py:52
  1.0 0.5 collective-permute-start.6
  1.5 1.4 %pack.1 = (bf16[1168,128]{1,0:T(8,128)(2,1)S(1)}, bf16[1168,128]{1,0:T(8,128)(2,1)S(1)}, bf16[1168,128]{1,0:T(8,128)(2,1)S(1)}, bf16[1168,128]{1,0:T(8,128)(2,1)S(1)}) custom-call(bf16[128,4096]{1,0:T(8,128)(2,1)} %bitcast.5, bf16[128,512]{1,0:T(8,128)(2,1)} %bitcast.6, s32[1,128]{1,0:T(1,128)} %flag_ref.1), custom_call_target="tpu_custom_call" | custom-call | tf_op jit(solution)/shard_map/pack/pallas_call | solution.py:103
  2.9 2.5 %collective-permute-start = (bf16[1168,128]{1,0:T(8,128)(2,1)S(1)}, bf16[1168,128]{1,0:T(8,128)(2,1)S(1)}, u32[]{:S(2)}, u32[]{:S(2)}) collective-permute-start(bf16[1168,128]{1,0:T(8,128)(2,1)S(1)} %get-tuple-element.42), channel_id=1, source_target_pairs={{0,6},{2,4},{4,2},{6,0},{8,14},{10,12},{12,10},{14,8},{16,22},{18,... | collective-permute-start | bytes 897032 | tf_op jit(solution)/shard_map/ppermute | solution.py:326
  5.4 0.5 %collective-permute-start.1 = (bf16[1168,128]{1,0:T(8,128)(2,1)S(1)}, bf16[1168,128]{1,0:T(8,128)(2,1)S(1)}, u32[]{:S(2)}, u32[]{:S(2)}) collective-permute-start(bf16[1168,128]{1,0:T(8,128)(2,1)S(1)} %get-tuple-element.43), channel_id=1, source_target_pairs={{0,2},{2,0},{4,6},{6,4},{8,10},{10,8},{12,14},{14,12},{16,18},{18,... | collective-permute-start | bytes 897032 | tf_op jit(solution)/shard_map/ppermute | solution.py:326
  6.0 0.5 collective-permute-start.2
  6.5 1.1 %collective-permute-start.4 = (bf16[256,512]{1,0:T(8,128)(2,1)S(1)}, bf16[256,512]{1,0:T(8,128)(2,1)S(1)}, u32[]{:S(2)}, u32[]{:S(2)}) collective-permute-start(bf16[256,512]{1,0:T(8,128)(2,1)S(1)} %stack.1.refs_0_), channel_id=1, source_target_pairs={{0,8},{2,10},{4,12},{6,14},{8,0},{10,2},{12,4},{14,6},{16,24},{18,... | collective-permute-start | bytes 786440 | tf_op jit(solution)/shard_map/ppermute | solution.py:326
  7.6 7.1 %collective-permute-done.6.refs_6_ = bf16[256,512]{1,0:T(8,128)(2,1)S(1)} collective-permute-done((bf16[256,512]{1,0:T(8,128)(2,1)S(1)}, bf16[256,512]{1,0:T(8,128)(2,1)S(1)}, u32[]{:S(2)}, u32[]{:S(2)}) %collective-permute-start.6) | collective-permute-done | bytes 262176 | tf_op jit(solution)/shard_map/ppermute | solution.py:326
  14.7 0.1 collective-permute-start.8
  14.8 1.0 %collective-permute-done.4.refs_2_ = bf16[256,512]{1,0:T(8,128)(2,1)S(1)} collective-permute-done((bf16[256,512]{1,0:T(8,128)(2,1)S(1)}, bf16[256,512]{1,0:T(8,128)(2,1)S(1)}, u32[]{:S(2)}, u32[]{:S(2)}) %collective-permute-start.4) | collective-permute-done | bytes 262176 | tf_op jit(solution)/shard_map/ppermute | solution.py:326
  15.8 0.0 collective-permute-start.3
  15.8 0.0 collective-permute-done.refs_1_
  15.8 2.5 %collective-permute-start.7 = (bf16[128,512]{1,0:T(8,128)(2,1)S(1)}, bf16[128,512]{1,0:T(8,128)(2,1)S(1)}, u32[]{:S(2)}, u32[]{:S(2)}) collective-permute-start(bf16[128,512]{1,0:T(8,128)(2,1)S(1)} %get-tuple-element.70), channel_id=1, source_target_pairs={{0,8},{2,10},{4,12},{6,14},{8,0},{10,2},{12,4},{14,6},{16,24},{18,... | collective-permute-start | bytes 393224 | tf_op jit(solution)/shard_map/ppermute | solution.py:326
  18.3 0.6 %collective-permute-done.1.refs_2_ = bf16[1168,128]{1,0:T(8,128)(2,1)S(1)} collective-permute-done((bf16[1168,128]{1,0:T(8,128)(2,1)S(1)}, bf16[1168,128]{1,0:T(8,128)(2,1)S(1)}, u32[]{:S(2)}, u32[]{:S(2)}) %collective-permute-start.1) | collective-permute-done | bytes 299040 | tf_op jit(solution)/shard_map/ppermute | solution.py:326
  18.9 0.0 collective-permute-start.10
  18.9 0.0 collective-permute-done.2.refs_3_
  18.9 0.5 collective-permute-start.5
  19.4 0.4 collective-permute-done.8.refs_4_
  19.9 0.0 collective-permute-start.9
  19.9 0.5 %assemble.1 = (bf16[512,1024]{1,0:T(8,128)(2,1)S(1)}, bf16[512,128]{1,0:T(8,128)(2,1)S(1)}, bf16[512,128]{1,0:T(8,128)(2,1)S(1)}, f32[8,512]{1,0:T(8,128)S(1)}, f32[512,128]{1,0:T(8,128)S(1)}) custom-call(bf16[1168,128]{1,0:T(8,128)(2,1)S(1)} %get-tuple-element.41.refs_0_, bf16[1168,128]{1,0:T(8,128)(2,1)S(1)} %collective-permute-done.refs_1_, ...), custom_call_target="tpu_custom_call" | custom-call | flops 4000000000 | tf_op jit(solution)/shard_map/assemble/pallas_call | solution.py:159
  20.4 0.0 collective-permute-done.3.refs_1_
  20.4 0.4 collective-permute-done.5.refs_3_
  20.8 0.4 collective-permute-done.9.refs_5_
  21.2 0.0 collective-permute-done.10.refs_7_
  21.2 0.7 %key_product.1 = (f32[512,128]{1,0:T(8,128)S(1)}, bf16[512,128]{1,0:T(8,128)(2,1)S(1)}, bf16[512,128]{1,0:T(8,128)(2,1)S(1)}, bf16[512,128]{1,0:T(8,128)(2,1)S(1)}) custom-call(bf16[512,1024]{1,0:T(8,128)(2,1)S(1)} %get-tuple-element.45.tok, bf16[256,512]{1,0:T(8,128)(2,1)S(1)} %stack.1.refs_0_, bf16[256,512]{1,0:T(8,128)(2,1)S(1)} %collective-permute-done.3.refs_1_, ...), custom_call_target="tpu_custom_call" | custom-call | tf_op jit(solution)/shard_map/key_product/pallas_call | solution.py:199
  21.9 2.5 %collective-permute-start.14 = (bf16[512,128]{1,0:T(8,128)(2,1)S(1)}, bf16[512,128]{1,0:T(8,128)(2,1)S(1)}, u32[]{:S(2)}, u32[]{:S(2)}) collective-permute-start(bf16[512,128]{1,0:T(8,128)(2,1)S(1)} %get-tuple-element.54), channel_id=1, source_target_pairs={{0,6},{2,4},{4,2},{6,0},{8,14},{10,12},{12,10},{14,8},{16,22},{18,... | collective-permute-start | bytes 393224 | tf_op jit(solution)/shard_map/ppermute | solution.py:326
  24.5 0.5 %collective-permute-start.15 = (bf16[512,128]{1,0:T(8,128)(2,1)S(1)}, bf16[512,128]{1,0:T(8,128)(2,1)S(1)}, u32[]{:S(2)}, u32[]{:S(2)}) collective-permute-start(bf16[512,128]{1,0:T(8,128)(2,1)S(1)} %get-tuple-element.55), channel_id=1, source_target_pairs={{0,2},{2,0},{4,6},{6,4},{8,10},{10,8},{12,14},{14,12},{16,18},{18,... | collective-permute-start | bytes 393224 | tf_op jit(solution)/shard_map/ppermute | solution.py:326
  25.0 0.5 collective-permute-start.16
  25.5 0.0 collective-permute-done.7.refs_4_
  25.5 2.0 %all_gather.3.refs_5_ = bf16[256,512]{1,0:T(8,128)(2,1)S(1)} all-gather(bf16[128,512]{1,0:T(8,128)(2,1)S(1)} %collective-permute-done.7.refs_4_), channel_id=1, replica_groups=mesh['ctx'=16,'fsdp'=2] {'fsdp'}, dimensions={0}, use_global_device_ids=true | all-gather | bytes 393216 | tf_op jit(solution)/shard_map/all_gather | solution.py:361
  27.5 0.7 %value_product.1 = (f32[512,128]{1,0:T(8,128)S(1)}, bf16[512,128]{1,0:T(8,128)(2,1)S(1)}, bf16[512,128]{1,0:T(8,128)(2,1)S(1)}, bf16[512,128]{1,0:T(8,128)(2,1)S(1)}) custom-call(bf16[512,1024]{1,0:T(8,128)(2,1)S(1)} %get-tuple-element.45.tok, bf16[256,512]{1,0:T(8,128)(2,1)S(1)} %stack.1.refs_0_, bf16[256,512]{1,0:T(8,128)(2,1)S(1)} %collective-permute-done.3.refs_1_, ...), custom_call_target="tpu_custom_call" | custom-call | tf_op jit(solution)/shard_map/value_product/pallas_call | solution.py:199
  28.2 2.5 %collective-permute-start.11 = (bf16[512,128]{1,0:T(8,128)(2,1)S(1)}, bf16[512,128]{1,0:T(8,128)(2,1)S(1)}, u32[]{:S(2)}, u32[]{:S(2)}) collective-permute-start(bf16[512,128]{1,0:T(8,128)(2,1)S(1)} %get-tuple-element.50), channel_id=1, source_target_pairs={{0,6},{2,4},{4,2},{6,0},{8,14},{10,12},{12,10},{14,8},{16,22},{18,... | collective-permute-start | bytes 393224 | tf_op jit(solution)/shard_map/ppermute | solution.py:326
  30.7 0.5 %collective-permute-start.12 = (bf16[512,128]{1,0:T(8,128)(2,1)S(1)}, bf16[512,128]{1,0:T(8,128)(2,1)S(1)}, u32[]{:S(2)}, u32[]{:S(2)}) collective-permute-start(bf16[512,128]{1,0:T(8,128)(2,1)S(1)} %get-tuple-element.51), channel_id=1, source_target_pairs={{0,2},{2,0},{4,6},{6,4},{8,10},{10,8},{12,14},{14,12},{16,18},{18,... | collective-permute-start | bytes 393224 | tf_op jit(solution)/shard_map/ppermute | solution.py:326
  31.3 0.0 collective-permute-done.14.refs_1_
  31.3 0.5 collective-permute-start.13
  31.8 0.0 collective-permute-done.15.refs_2_
  31.8 0.0 collective-permute-done.16.refs_3_
  31.8 0.3 score.1
  32.1 3.4 %collective-permute-done.11.refs_1_ = bf16[512,128]{1,0:T(8,128)(2,1)S(1)} collective-permute-done((bf16[512,128]{1,0:T(8,128)(2,1)S(1)}, bf16[512,128]{1,0:T(8,128)(2,1)S(1)}, u32[]{:S(2)}, u32[]{:S(2)}) %collective-permute-start.11) | collective-permute-done | bytes 131104 | tf_op jit(solution)/shard_map/ppermute | solution.py:326
  35.5 2.1 %collective-permute-done.12.refs_2_ = bf16[512,128]{1,0:T(8,128)(2,1)S(1)} collective-permute-done((bf16[512,128]{1,0:T(8,128)(2,1)S(1)}, bf16[512,128]{1,0:T(8,128)(2,1)S(1)}, u32[]{:S(2)}, u32[]{:S(2)}) %collective-permute-start.12) | collective-permute-done | bytes 131104 | tf_op jit(solution)/shard_map/ppermute | solution.py:326
  37.6 0.0 collective-permute-done.13.refs_3_
  37.6 0.2 state.1
  37.8 1.3 %collective-permute-start.17 = (bf16[128,128]{1,0:T(8,128)(2,1)S(1)}, bf16[128,128]{1,0:T(8,128)(2,1)S(1)}, u32[]{:S(2)}, u32[]{:S(2)}) collective-permute-start(bf16[128,128]{1,0:T(8,128)(2,1)S(1)} %get-tuple-element.61), channel_id=1, source_target_pairs={{8,16},{10,18},{12,20},{14,22},{9,17},{11,19},{13,21},{15,23}} | collective-permute-start | bytes 98312 | tf_op jit(solution)/shard_map/ppermute | solution.py:379
  39.1 0.2 within.1.inside
  39.4 0.0 copy-start
  39.4 4.3 %collective-permute-done.17.carried = bf16[128,128]{1,0:T(8,128)(2,1)S(1)} collective-permute-done((bf16[128,128]{1,0:T(8,128)(2,1)S(1)}, bf16[128,128]{1,0:T(8,128)(2,1)S(1)}, u32[]{:S(2)}, u32[]{:S(2)}) %collective-permute-start.17) | collective-permute-done | bytes 32800 | tf_op jit(solution)/shard_map/ppermute | solution.py:379
  43.7 0.0 copy-done
  43.7 0.3 finish.1
  44.0 2.4 %collective-permute-start.18 = (bf16[128,128]{1,0:T(8,128)(2,1)S(1)}, bf16[128,128]{1,0:T(8,128)(2,1)S(1)}, u32[]{:S(2)}, u32[]{:S(2)}) collective-permute-start(bf16[128,128]{1,0:T(8,128)(2,1)S(1)} %get-tuple-element.66), channel_id=1, source_target_pairs={{0,6},{2,4},{4,2},{6,0},{8,14},{10,12},{12,10},{14,8},{16,22},{18,... | collective-permute-start | bytes 98312 | tf_op jit(solution)/shard_map/ppermute | solution.py:326
  46.4 0.5 %collective-permute-start.19 = (bf16[128,128]{1,0:T(8,128)(2,1)S(1)}, bf16[128,128]{1,0:T(8,128)(2,1)S(1)}, u32[]{:S(2)}, u32[]{:S(2)}) collective-permute-start(bf16[128,128]{1,0:T(8,128)(2,1)S(1)} %get-tuple-element.67), channel_id=1, source_target_pairs={{0,2},{2,0},{4,6},{6,4},{8,10},{10,8},{12,14},{14,12},{16,18},{18,... | collective-permute-start | bytes 98312 | tf_op jit(solution)/shard_map/ppermute | solution.py:326
  47.0 0.6 %collective-permute-start.20 = (bf16[128,128]{1,0:T(8,128)(2,1)S(1)}, bf16[128,128]{1,0:T(8,128)(2,1)S(1)}, u32[]{:S(2)}, u32[]{:S(2)}) collective-permute-start(bf16[128,128]{1,0:T(8,128)(2,1)S(1)} %get-tuple-element.68), channel_id=1, source_target_pairs={{0,4},{2,6},{4,0},{6,2},{8,12},{10,14},{12,8},{14,10},{16,20},{18,... | collective-permute-start | bytes 98312 | tf_op jit(solution)/shard_map/ppermute | solution.py:326
  47.5 1.3 %collective-permute-done.18.refs_1_ = bf16[128,128]{1,0:T(8,128)(2,1)S(1)} collective-permute-done((bf16[128,128]{1,0:T(8,128)(2,1)S(1)}, bf16[128,128]{1,0:T(8,128)(2,1)S(1)}, u32[]{:S(2)}, u32[]{:S(2)}) %collective-permute-start.18) | collective-permute-done | bytes 32800 | tf_op jit(solution)/shard_map/ppermute | solution.py:326
  48.8 1.5 %collective-permute-done.19.refs_2_ = bf16[128,128]{1,0:T(8,128)(2,1)S(1)} collective-permute-done((bf16[128,128]{1,0:T(8,128)(2,1)S(1)}, bf16[128,128]{1,0:T(8,128)(2,1)S(1)}, u32[]{:S(2)}, u32[]{:S(2)}) %collective-permute-start.19) | collective-permute-done | bytes 32800 | tf_op jit(solution)/shard_map/ppermute | solution.py:326
  50.3 0.5 %collective-permute-done.20.refs_3_ = bf16[128,128]{1,0:T(8,128)(2,1)S(1)} collective-permute-done((bf16[128,128]{1,0:T(8,128)(2,1)S(1)}, bf16[128,128]{1,0:T(8,128)(2,1)S(1)}, u32[]{:S(2)}, u32[]{:S(2)}) %collective-permute-start.20) | collective-permute-done | bytes 32800 | tf_op jit(solution)/shard_map/ppermute | solution.py:326
  50.9 0.7 %join.1 = bf16[128,512]{1,0:T(8,128)(2,1)} custom-call(bf16[128,128]{1,0:T(8,128)(2,1)S(1)} %get-tuple-element.65.refs_0_, bf16[128,128]{1,0:T(8,128)(2,1)S(1)} %collective-permute-done.18.refs_1_, bf16[128,128]{1,0:T(8,128)(2,1)S(1)} %collective-permute-done.19.refs_2_, bf16[128,128]{1,0:T(8,128)(2,1)S(1)} %collective-permute-done.20.refs_3_), custom_call_target="tpu_custom_call" | custom-call | tf_op jit(solution)/shard_map/join/pallas_call | solution.py:311
  (1 shorter events, 0.0 us)
Async XLA Ops:
  1.0 13.7 %collective-permute-start.6 = (bf16[256,512]{1,0:T(8,128)(2,1)S(1)}, bf16[256,512]{1,0:T(8,128)(2,1)S(1)}, u32[]{:S(2)}, u32[]{:S(2)}) collective-permute-start(bf16[256,512]{1,0:T(8,128)(2,1)S(1)} %stack.1.refs_0_), channel_id=1, source_target_pairs={{0,24},{2,26},{4,28},{6,30},{8,16},{10,18},{12,20},{14,22},{16,8},... | collective-permute-start | bytes 786440 | tf_op jit(solution)/shard_map/ppermute | solution.py:326
  2.9 12.9 %collective-permute-start = (bf16[1168,128]{1,0:T(8,128)(2,1)S(1)}, bf16[1168,128]{1,0:T(8,128)(2,1)S(1)}, u32[]{:S(2)}, u32[]{:S(2)}) collective-permute-start(bf16[1168,128]{1,0:T(8,128)(2,1)S(1)} %get-tuple-element.42), channel_id=1, source_target_pairs={{0,6},{2,4},{4,2},{6,0},{8,14},{10,12},{12,10},{14,8},{16,22},{18,... | collective-permute-start | bytes 897032 | tf_op jit(solution)/shard_map/ppermute | solution.py:326
  5.4 13.5 %collective-permute-start.1 = (bf16[1168,128]{1,0:T(8,128)(2,1)S(1)}, bf16[1168,128]{1,0:T(8,128)(2,1)S(1)}, u32[]{:S(2)}, u32[]{:S(2)}) collective-permute-start(bf16[1168,128]{1,0:T(8,128)(2,1)S(1)} %get-tuple-element.43), channel_id=1, source_target_pairs={{0,2},{2,0},{4,6},{6,4},{8,10},{10,8},{12,14},{14,12},{16,18},{18,... | collective-permute-start | bytes 897032 | tf_op jit(solution)/shard_map/ppermute | solution.py:326
  6.0 13.0 %collective-permute-start.2 = (bf16[1168,128]{1,0:T(8,128)(2,1)S(1)}, bf16[1168,128]{1,0:T(8,128)(2,1)S(1)}, u32[]{:S(2)}, u32[]{:S(2)}) collective-permute-start(bf16[1168,128]{1,0:T(8,128)(2,1)S(1)} %get-tuple-element.44), channel_id=1, source_target_pairs={{0,4},{2,6},{4,0},{6,2},{8,12},{10,14},{12,8},{14,10},{16,20},{18,... | collective-permute-start | bytes 897032 | tf_op jit(solution)/shard_map/ppermute | solution.py:326
  6.5 9.3 %collective-permute-start.4 = (bf16[256,512]{1,0:T(8,128)(2,1)S(1)}, bf16[256,512]{1,0:T(8,128)(2,1)S(1)}, u32[]{:S(2)}, u32[]{:S(2)}) collective-permute-start(bf16[256,512]{1,0:T(8,128)(2,1)S(1)} %stack.1.refs_0_), channel_id=1, source_target_pairs={{0,8},{2,10},{4,12},{6,14},{8,0},{10,2},{12,4},{14,6},{16,24},{18,... | collective-permute-start | bytes 786440 | tf_op jit(solution)/shard_map/ppermute | solution.py:326
  14.7 5.1 %collective-permute-start.8 = (bf16[128,512]{1,0:T(8,128)(2,1)S(1)}, bf16[128,512]{1,0:T(8,128)(2,1)S(1)}, u32[]{:S(2)}, u32[]{:S(2)}) collective-permute-start(bf16[128,512]{1,0:T(8,128)(2,1)S(1)} %get-tuple-element.69), channel_id=1, source_target_pairs={{0,8},{2,10},{4,12},{6,14},{8,0},{10,2},{12,4},{14,6},{16,24},{18,... | collective-permute-start | bytes 393224 | tf_op jit(solution)/shard_map/ppermute | solution.py:326
  15.8 4.6 %collective-permute-start.3 = (bf16[256,512]{1,0:T(8,128)(2,1)S(1)}, bf16[256,512]{1,0:T(8,128)(2,1)S(1)}, u32[]{:S(2)}, u32[]{:S(2)}) collective-permute-start(bf16[256,512]{1,0:T(8,128)(2,1)S(1)} %stack.1.refs_0_), channel_id=1, source_target_pairs={{0,1},{1,0},{2,3},{3,2},{4,5},{5,4},{6,7},{7,6},{8,9},{9,8},{10,11... | collective-permute-start | bytes 786440 | tf_op jit(solution)/shard_map/ppermute | solution.py:332
  15.8 9.7 %collective-permute-start.7 = (bf16[128,512]{1,0:T(8,128)(2,1)S(1)}, bf16[128,512]{1,0:T(8,128)(2,1)S(1)}, u32[]{:S(2)}, u32[]{:S(2)}) collective-permute-start(bf16[128,512]{1,0:T(8,128)(2,1)S(1)} %get-tuple-element.70), channel_id=1, source_target_pairs={{0,8},{2,10},{4,12},{6,14},{8,0},{10,2},{12,4},{14,6},{16,24},{18,... | collective-permute-start | bytes 393224 | tf_op jit(solution)/shard_map/ppermute | solution.py:326
  18.9 2.3 %collective-permute-start.10 = (bf16[256,512]{1,0:T(8,128)(2,1)S(1)}, bf16[256,512]{1,0:T(8,128)(2,1)S(1)}, u32[]{:S(2)}, u32[]{:S(2)}) collective-permute-start(bf16[256,512]{1,0:T(8,128)(2,1)S(1)} %collective-permute-done.6.refs_6_), channel_id=1, source_target_pairs={{0,1},{1,0},{2,3},{3,2},{4,5},{5,4},{6,7},{7,6},{8,9},{9,8},{10,11... | collective-permute-start | bytes 786440 | tf_op jit(solution)/shard_map/ppermute | solution.py:332
  18.9 1.9 %collective-permute-start.5 = (bf16[256,512]{1,0:T(8,128)(2,1)S(1)}, bf16[256,512]{1,0:T(8,128)(2,1)S(1)}, u32[]{:S(2)}, u32[]{:S(2)}) collective-permute-start(bf16[256,512]{1,0:T(8,128)(2,1)S(1)} %collective-permute-done.4.refs_2_), channel_id=1, source_target_pairs={{0,1},{1,0},{2,3},{3,2},{4,5},{5,4},{6,7},{7,6},{8,9},{9,8},{10,11... | collective-permute-start | bytes 786440 | tf_op jit(solution)/shard_map/ppermute | solution.py:332
  19.9 1.3 %collective-permute-start.9 = (bf16[128,512]{1,0:T(8,128)(2,1)S(1)}, bf16[128,512]{1,0:T(8,128)(2,1)S(1)}, u32[]{:S(2)}, u32[]{:S(2)}) collective-permute-start(bf16[128,512]{1,0:T(8,128)(2,1)S(1)} %collective-permute-done.8.refs_4_), channel_id=1, source_target_pairs={{0,1},{1,0},{2,3},{3,2},{4,5},{5,4},{6,7},{7,6},{8,9},{9,8},{10,11... | collective-permute-start | bytes 393224 | tf_op jit(solution)/shard_map/ppermute | solution.py:332
  21.9 9.3 %collective-permute-start.14 = (bf16[512,128]{1,0:T(8,128)(2,1)S(1)}, bf16[512,128]{1,0:T(8,128)(2,1)S(1)}, u32[]{:S(2)}, u32[]{:S(2)}) collective-permute-start(bf16[512,128]{1,0:T(8,128)(2,1)S(1)} %get-tuple-element.54), channel_id=1, source_target_pairs={{0,6},{2,4},{4,2},{6,0},{8,14},{10,12},{12,10},{14,8},{16,22},{18,... | collective-permute-start | bytes 393224 | tf_op jit(solution)/shard_map/ppermute | solution.py:326
  24.5 7.3 %collective-permute-start.15 = (bf16[512,128]{1,0:T(8,128)(2,1)S(1)}, bf16[512,128]{1,0:T(8,128)(2,1)S(1)}, u32[]{:S(2)}, u32[]{:S(2)}) collective-permute-start(bf16[512,128]{1,0:T(8,128)(2,1)S(1)} %get-tuple-element.55), channel_id=1, source_target_pairs={{0,2},{2,0},{4,6},{6,4},{8,10},{10,8},{12,14},{14,12},{16,18},{18,... | collective-permute-start | bytes 393224 | tf_op jit(solution)/shard_map/ppermute | solution.py:326
  25.0 6.8 %collective-permute-start.16 = (bf16[512,128]{1,0:T(8,128)(2,1)S(1)}, bf16[512,128]{1,0:T(8,128)(2,1)S(1)}, u32[]{:S(2)}, u32[]{:S(2)}) collective-permute-start(bf16[512,128]{1,0:T(8,128)(2,1)S(1)} %get-tuple-element.56), channel_id=1, source_target_pairs={{0,4},{2,6},{4,0},{6,2},{8,12},{10,14},{12,8},{14,10},{16,20},{18,... | collective-permute-start | bytes 393224 | tf_op jit(solution)/shard_map/ppermute | solution.py:326
  28.2 7.3 %collective-permute-start.11 = (bf16[512,128]{1,0:T(8,128)(2,1)S(1)}, bf16[512,128]{1,0:T(8,128)(2,1)S(1)}, u32[]{:S(2)}, u32[]{:S(2)}) collective-permute-start(bf16[512,128]{1,0:T(8,128)(2,1)S(1)} %get-tuple-element.50), channel_id=1, source_target_pairs={{0,6},{2,4},{4,2},{6,0},{8,14},{10,12},{12,10},{14,8},{16,22},{18,... | collective-permute-start | bytes 393224 | tf_op jit(solution)/shard_map/ppermute | solution.py:326
  30.7 6.9 %collective-permute-start.12 = (bf16[512,128]{1,0:T(8,128)(2,1)S(1)}, bf16[512,128]{1,0:T(8,128)(2,1)S(1)}, u32[]{:S(2)}, u32[]{:S(2)}) collective-permute-start(bf16[512,128]{1,0:T(8,128)(2,1)S(1)} %get-tuple-element.51), channel_id=1, source_target_pairs={{0,2},{2,0},{4,6},{6,4},{8,10},{10,8},{12,14},{14,12},{16,18},{18,... | collective-permute-start | bytes 393224 | tf_op jit(solution)/shard_map/ppermute | solution.py:326
  31.3 6.3 %collective-permute-start.13 = (bf16[512,128]{1,0:T(8,128)(2,1)S(1)}, bf16[512,128]{1,0:T(8,128)(2,1)S(1)}, u32[]{:S(2)}, u32[]{:S(2)}) collective-permute-start(bf16[512,128]{1,0:T(8,128)(2,1)S(1)} %get-tuple-element.52), channel_id=1, source_target_pairs={{0,4},{2,6},{4,0},{6,2},{8,12},{10,14},{12,8},{14,10},{16,20},{18,... | collective-permute-start | bytes 393224 | tf_op jit(solution)/shard_map/ppermute | solution.py:326
  37.8 5.8 %collective-permute-start.17 = (bf16[128,128]{1,0:T(8,128)(2,1)S(1)}, bf16[128,128]{1,0:T(8,128)(2,1)S(1)}, u32[]{:S(2)}, u32[]{:S(2)}) collective-permute-start(bf16[128,128]{1,0:T(8,128)(2,1)S(1)} %get-tuple-element.61), channel_id=1, source_target_pairs={{8,16},{10,18},{12,20},{14,22},{9,17},{11,19},{13,21},{15,23}} | collective-permute-start | bytes 98312 | tf_op jit(solution)/shard_map/ppermute | solution.py:379
  39.4 4.3 %copy-start = (f32[512]{0:T(512)S(1)}, f32[512]{0:T(512)}, u32[]{:S(2)}) copy-start(f32[512]{0:T(512)} %param.11) | copy-start | bytes 6148
  44.0 4.9 %collective-permute-start.18 = (bf16[128,128]{1,0:T(8,128)(2,1)S(1)}, bf16[128,128]{1,0:T(8,128)(2,1)S(1)}, u32[]{:S(2)}, u32[]{:S(2)}) collective-permute-start(bf16[128,128]{1,0:T(8,128)(2,1)S(1)} %get-tuple-element.66), channel_id=1, source_target_pairs={{0,6},{2,4},{4,2},{6,0},{8,14},{10,12},{12,10},{14,8},{16,22},{18,... | collective-permute-start | bytes 98312 | tf_op jit(solution)/shard_map/ppermute | solution.py:326
  46.4 3.9 %collective-permute-start.19 = (bf16[128,128]{1,0:T(8,128)(2,1)S(1)}, bf16[128,128]{1,0:T(8,128)(2,1)S(1)}, u32[]{:S(2)}, u32[]{:S(2)}) collective-permute-start(bf16[128,128]{1,0:T(8,128)(2,1)S(1)} %get-tuple-element.67), channel_id=1, source_target_pairs={{0,2},{2,0},{4,6},{6,4},{8,10},{10,8},{12,14},{14,12},{16,18},{18,... | collective-permute-start | bytes 98312 | tf_op jit(solution)/shard_map/ppermute | solution.py:326
  47.0 3.9 %collective-permute-start.20 = (bf16[128,128]{1,0:T(8,128)(2,1)S(1)}, bf16[128,128]{1,0:T(8,128)(2,1)S(1)}, u32[]{:S(2)}, u32[]{:S(2)}) collective-permute-start(bf16[128,128]{1,0:T(8,128)(2,1)S(1)} %get-tuple-element.68), channel_id=1, source_target_pairs={{0,4},{2,6},{4,0},{6,2},{8,12},{10,14},{12,8},{14,10},{16,20},{18,... | collective-permute-start | bytes 98312 | tf_op jit(solution)/shard_map/ppermute | solution.py:326

commit v7 on v6

--- a/solution.py
+++ b/solution.py
@@ -62,6 +62,10 @@
 
 def partners(heads):
     return [0, heads - 1] + list(range(1, heads - 1))
+
+
+def token_partners(heads):
+    return partners(heads)
 
 
 def pack_kernel(heads, tok_ref, query_ref, flag_ref, *refs):
@@ -133,7 +137,7 @@
     inner, outer = inner_outer(heads)
     squares = tok.shape[1] // HEAD
     total = heads * count
-    for k, x in zip(partners(heads), x_refs):
+    for k, x in zip(token_partners(heads), x_refs):
         place = jnp.bitwise_xor(inner, k)
         rows = aligned(place, count)
         for i in range(squares):
@@ -178,8 +182,9 @@
     rows = tok.shape[1] // len(places)
 
     def rows_at(at):
-        if at is None:
-            return aligned(1 - lax.axis_index("fsdp"), rows)
+        if isinstance(at, tuple):
+            other = 1 - lax.axis_index("fsdp")
+            return pl.ds(pl.multiple_of(other * at[0] + at[1], rows), rows)
         return slice(at, at + rows)
 
     def panel(k):
@@ -325,8 +330,8 @@
     def swap(a, mask):
         return lax.ppermute(a, "ctx", [(i, i ^ mask) for i in range(n_ctx)])
 
-    def exchange(parts):
-        return [parts[0]] + [swap(parts[k], k) for k in partners(heads)[1:]]
+    def exchange(parts, order=partners):
+        return [parts[0]] + [swap(parts[k], k) for k in order(heads)[1:]]
 
     def other(a):
         return lax.ppermute(a, "fsdp", [(0, 1), (1, 0)])
@@ -340,15 +345,17 @@
         packed = pack(tokens[0], queries[0], flags, heads, share)
         held, *packed = lax.optimization_barrier((weights, *packed))
         near = swap(held, heads)
-        received = list(exchange(packed))
-        whole = [(w, other(w)) for w in (weights, near, far)]
+        received = exchange(packed, token_partners)
+        mine = lax.all_gather(weights, "fsdp", axis=0, tiled=True)
+        mine, far = lax.optimization_barrier((mine, far))
+        whole = [(w, other(w)) for w in (near, far)]
         away = [far[:rows], far[rows:]]
         last = [swap(away[0], heads)]
         last.append(swap(away[1], heads))
         across = other(last[0])
     else:
         packed = pack(tokens[0], queries[0], flags, heads, share)
-        received = exchange(packed)
+        received = exchange(packed, token_partners)
         groups = [[o * heads + q for o in range(outer)] for q in range(heads)]
         chip = [lax.all_gather(w, "fsdp", axis=0, tiled=True) for w in both]
         full = [lax.all_gather(w, "ctx", axis=0, tiled=True, axis_index_groups=groups) for w in chip]
@@ -359,8 +366,9 @@
             if i == 1:
                 last[1], parts[0][0] = lax.optimization_barrier((last[1], parts[0][0]))
                 across = lax.all_gather(last[1], "fsdp", axis=0, tiled=True)
-            own, close, distant = [[(w, i * rows) for w in pair] for pair in whole]
-            panel = own + close + [(last[i], 0), (across, None if i else 0)] + distant
+            close, distant = [[(w, i * rows) for w in pair] for pair in whole]
+            own = [(weights, i * rows), (mine, (2 * rows, i * rows))]
+            panel = own + close + [(last[i], 0), (across, (rows, 0) if i else 0)] + distant
         else:
             panel = [(full[i], 0)]
         partial = product(tok, panel, heads, name)

time: 51.7 us -> 51.7 us (level)
  blocking collectives: 1.98 us -> 4.15 us
  waiting for transfers between devices: 23.1 us -> 21.4 us
    all_gather x0 -> x1, blocking collectives: none -> 2.17 us  [on_device(): mine = lax.all_gather(weights, 'fsdp', axis=0, tiled=True)]
    ppermute x16, waiting for transfers between devices: 18 us -> 16.4 us  [swap(): return lax.ppermute(a, 'ctx', [(i, i ^ mask) for i in range(n_ctx)])]
  transfers between devices with their start and end apart: 21 -> 20, of which waited for: 12 -> 11; matrix products, arithmetic and copies ran while one was open for 0% -> 0% of each run, Pallas kernels for 8% -> 8%
where the time goes in v7:
time: 51.7 us; the launch traced here: 51.5 us
  waiting for transfers between devices  21.4 us (41%)
  starting transfers between devices  19.7 us (38%)
  Pallas kernels  6.13 us (12%)
  blocking collectives  4.15 us (8%)
    ppermute x16, starting transfers between devices, swap(): return lax.ppermute(a, 'ctx', [(i, i ^ mask) for i in range(n_ctx)])  18.4 us
    ppermute x16, waiting for transfers between devices, swap(): return lax.ppermute(a, 'ctx', [(i, i ^ mask) for i in range(n_ctx)])  16.4 us
    ppermute x1, waiting for transfers between devices, on_device(): carried = lax.ppermute(state.astype(BF), 'ctx', pairs)  4.26 us
    all_gather x1, blocking collectives, on_device(): mine = lax.all_gather(weights, 'fsdp', axis=0, tiled=True)  2.17 us
    all_gather x1, blocking collectives, on_device(): across = lax.all_gather(last[1], 'fsdp', axis=0, tiled=True)  1.98 us
    pallas_call x2, Pallas kernels, product(): pl.pallas_call(functools.partial(product_kernel, heads, [at for _, at in...  1.45 us
    pallas_call x1, Pallas kernels, pack(): pl.pallas_call(functools.partial(pack_kernel, heads), in_specs=[pl.BlockS...  1.39 us
    ppermute x1, starting transfers between devices, on_device(): carried = lax.ppermute(state.astype(BF), 'ctx', pairs)  1.29 us
  transfers between devices with their start and end apart: 20, of which 11 were waited for; matrix products, arithmetic and copies ran while one was open for 0% of the time, Pallas kernels for 8%

profile of v7, /device:TPU:16, one launch (start us, length us, event | category | flops | bytes accessed | tf_op | source)
XLA Modules:
  0.0 51.5 jit_solution(14754665006893685094)
XLA Ops:
  0.0 1.0 %stack.1.refs_0_ = bf16[256,512]{1,0:T(8,128)(2,1)S(1)} custom-call(bf16[128,512]{1,0:T(8,128)(2,1)} %refs_0_.1, bf16[128,512]{1,0:T(8,128)(2,1)} %refs_1_.1), custom_call_target="tpu_custom_call" | custom-call | tf_op jit(solution)/shard_map/stack/pallas_call | solution.py:52
  1.0 0.5 collective-permute-start.3
  1.5 1.4 %pack.1 = (bf16[1168,128]{1,0:T(8,128)(2,1)S(1)}, bf16[1168,128]{1,0:T(8,128)(2,1)S(1)}, bf16[1168,128]{1,0:T(8,128)(2,1)S(1)}, bf16[1168,128]{1,0:T(8,128)(2,1)S(1)}) custom-call(bf16[128,4096]{1,0:T(8,128)(2,1)} %bitcast.5, bf16[128,512]{1,0:T(8,128)(2,1)} %bitcast.6, s32[1,128]{1,0:T(1,128)} %flag_ref.1), custom_call_target="tpu_custom_call" | custom-call | tf_op jit(solution)/shard_map/pack/pallas_call | solution.py:107
  2.9 2.5 %collective-permute-start = (bf16[1168,128]{1,0:T(8,128)(2,1)S(1)}, bf16[1168,128]{1,0:T(8,128)(2,1)S(1)}, u32[]{:S(2)}, u32[]{:S(2)}) collective-permute-start(bf16[1168,128]{1,0:T(8,128)(2,1)S(1)} %get-tuple-element.44), channel_id=1, source_target_pairs={{0,6},{2,4},{4,2},{6,0},{8,14},{10,12},{12,10},{14,8},{16,22},{18,... | collective-permute-start | bytes 897032 | tf_op jit(solution)/shard_map/ppermute | solution.py:331
  5.4 0.5 %collective-permute-start.1 = (bf16[1168,128]{1,0:T(8,128)(2,1)S(1)}, bf16[1168,128]{1,0:T(8,128)(2,1)S(1)}, u32[]{:S(2)}, u32[]{:S(2)}) collective-permute-start(bf16[1168,128]{1,0:T(8,128)(2,1)S(1)} %get-tuple-element.45), channel_id=1, source_target_pairs={{0,2},{2,0},{4,6},{6,4},{8,10},{10,8},{12,14},{14,12},{16,18},{18,... | collective-permute-start | bytes 897032 | tf_op jit(solution)/shard_map/ppermute | solution.py:331
  6.0 0.5 collective-permute-start.2
  6.5 1.1 %collective-permute-start.4 = (bf16[256,512]{1,0:T(8,128)(2,1)S(1)}, bf16[256,512]{1,0:T(8,128)(2,1)S(1)}, u32[]{:S(2)}, u32[]{:S(2)}) collective-permute-start(bf16[256,512]{1,0:T(8,128)(2,1)S(1)} %stack.1.refs_0_), channel_id=1, source_target_pairs={{0,8},{2,10},{4,12},{6,14},{8,0},{10,2},{12,4},{14,6},{16,24},{18,... | collective-permute-start | bytes 786440 | tf_op jit(solution)/shard_map/ppermute | solution.py:331
  7.6 2.2 %all_gather.6.refs_1_ = bf16[512,512]{1,0:T(8,128)(2,1)S(1)} all-gather(bf16[256,512]{1,0:T(8,128)(2,1)S(1)} %stack.1.refs_0_), channel_id=1, replica_groups=mesh['ctx'=16,'fsdp'=2] {'fsdp'}, dimensions={0}, use_global_device_ids=true | all-gather | bytes 786432 | tf_op jit(solution)/shard_map/all_gather | solution.py:349
  9.8 4.9 %collective-permute-done.3.refs_6_ = bf16[256,512]{1,0:T(8,128)(2,1)S(1)} collective-permute-done((bf16[256,512]{1,0:T(8,128)(2,1)S(1)}, bf16[256,512]{1,0:T(8,128)(2,1)S(1)}, u32[]{:S(2)}, u32[]{:S(2)}) %collective-permute-start.3) | collective-permute-done | bytes 262176 | tf_op jit(solution)/shard_map/ppermute | solution.py:331
  14.7 0.1 collective-permute-start.7
  14.8 1.0 %collective-permute-done.4.refs_2_ = bf16[256,512]{1,0:T(8,128)(2,1)S(1)} collective-permute-done((bf16[256,512]{1,0:T(8,128)(2,1)S(1)}, bf16[256,512]{1,0:T(8,128)(2,1)S(1)}, u32[]{:S(2)}, u32[]{:S(2)}) %collective-permute-start.4) | collective-permute-done | bytes 262176 | tf_op jit(solution)/shard_map/ppermute | solution.py:331
  15.8 0.0 collective-permute-start.9
  15.8 0.0 collective-permute-done.refs_1_
  15.8 2.5 %collective-permute-start.6 = (bf16[128,512]{1,0:T(8,128)(2,1)S(1)}, bf16[128,512]{1,0:T(8,128)(2,1)S(1)}, u32[]{:S(2)}, u32[]{:S(2)}) collective-permute-start(bf16[128,512]{1,0:T(8,128)(2,1)S(1)} %get-tuple-element.74), channel_id=1, source_target_pairs={{0,8},{2,10},{4,12},{6,14},{8,0},{10,2},{12,4},{14,6},{16,24},{18,... | collective-permute-start | bytes 393224 | tf_op jit(solution)/shard_map/ppermute | solution.py:331
  18.3 0.6 %collective-permute-done.1.refs_2_ = bf16[1168,128]{1,0:T(8,128)(2,1)S(1)} collective-permute-done((bf16[1168,128]{1,0:T(8,128)(2,1)S(1)}, bf16[1168,128]{1,0:T(8,128)(2,1)S(1)}, u32[]{:S(2)}, u32[]{:S(2)}) %collective-permute-start.1) | collective-permute-done | bytes 299040 | tf_op jit(solution)/shard_map/ppermute | solution.py:331
  18.9 0.0 collective-permute-start.5
  18.9 0.9 %collective-permute-done.7.refs_4_ = bf16[128,512]{1,0:T(8,128)(2,1)S(1)} collective-permute-done((bf16[128,512]{1,0:T(8,128)(2,1)S(1)}, bf16[128,512]{1,0:T(8,128)(2,1)S(1)}, u32[]{:S(2)}, u32[]{:S(2)}) %collective-permute-start.7) | collective-permute-done | bytes 131104 | tf_op jit(solution)/shard_map/ppermute | solution.py:331
  19.9 0.0 collective-permute-start.8
  19.9 0.0 collective-permute-done.2.refs_3_
  19.9 0.5 %assemble.1 = (bf16[512,1024]{1,0:T(8,128)(2,1)S(1)}, bf16[512,128]{1,0:T(8,128)(2,1)S(1)}, bf16[512,128]{1,0:T(8,128)(2,1)S(1)}, f32[8,512]{1,0:T(8,128)S(1)}, f32[512,128]{1,0:T(8,128)S(1)}) custom-call(bf16[1168,128]{1,0:T(8,128)(2,1)S(1)} %get-tuple-element.43.refs_0_, bf16[1168,128]{1,0:T(8,128)(2,1)S(1)} %collective-permute-done.refs_1_, ...), custom_call_target="tpu_custom_call" | custom-call | flops 4000000000 | tf_op jit(solution)/shard_map/assemble/pallas_call | solution.py:163
  20.4 0.0 collective-permute-done.5.refs_3_
  20.5 0.7 %collective-permute-done.8.refs_5_ = bf16[128,512]{1,0:T(8,128)(2,1)S(1)} collective-permute-done((bf16[128,512]{1,0:T(8,128)(2,1)S(1)}, bf16[128,512]{1,0:T(8,128)(2,1)S(1)}, u32[]{:S(2)}, u32[]{:S(2)}) %collective-permute-start.8) | collective-permute-done | bytes 131104 | tf_op jit(solution)/shard_map/ppermute | solution.py:337
  21.2 0.0 collective-permute-done.9.refs_7_
  21.2 0.7 %key_product.1 = (f32[512,128]{1,0:T(8,128)S(1)}, bf16[512,128]{1,0:T(8,128)(2,1)S(1)}, bf16[512,128]{1,0:T(8,128)(2,1)S(1)}, bf16[512,128]{1,0:T(8,128)(2,1)S(1)}) custom-call(bf16[512,1024]{1,0:T(8,128)(2,1)S(1)} %get-tuple-element.47.tok, bf16[256,512]{1,0:T(8,128)(2,1)S(1)} %stack.1.refs_0_, bf16[512,512]{1,0:T(8,128)(2,1)S(1)} %all_gather.6.refs_1_, ...), custom_call_target="tpu_custom_call" | custom-call | tf_op jit(solution)/shard_map/key_product/pallas_call | solution.py:204
  21.9 2.5 %collective-permute-start.13 = (bf16[512,128]{1,0:T(8,128)(2,1)S(1)}, bf16[512,128]{1,0:T(8,128)(2,1)S(1)}, u32[]{:S(2)}, u32[]{:S(2)}) collective-permute-start(bf16[512,128]{1,0:T(8,128)(2,1)S(1)} %get-tuple-element.58), channel_id=1, source_target_pairs={{0,6},{2,4},{4,2},{6,0},{8,14},{10,12},{12,10},{14,8},{16,22},{18,... | collective-permute-start | bytes 393224 | tf_op jit(solution)/shard_map/ppermute | solution.py:331
  24.4 0.5 %collective-permute-start.14 = (bf16[512,128]{1,0:T(8,128)(2,1)S(1)}, bf16[512,128]{1,0:T(8,128)(2,1)S(1)}, u32[]{:S(2)}, u32[]{:S(2)}) collective-permute-start(bf16[512,128]{1,0:T(8,128)(2,1)S(1)} %get-tuple-element.59), channel_id=1, source_target_pairs={{0,2},{2,0},{4,6},{6,4},{8,10},{10,8},{12,14},{14,12},{16,18},{18,... | collective-permute-start | bytes 393224 | tf_op jit(solution)/shard_map/ppermute | solution.py:331
  25.0 0.5 collective-permute-start.15
  25.5 0.0 collective-permute-done.6.refs_4_
  25.5 2.0 %all_gather.7.refs_5_ = bf16[256,512]{1,0:T(8,128)(2,1)S(1)} all-gather(bf16[128,512]{1,0:T(8,128)(2,1)S(1)} %collective-permute-done.6.refs_4_), channel_id=1, replica_groups=mesh['ctx'=16,'fsdp'=2] {'fsdp'}, dimensions={0}, use_global_device_ids=true | all-gather | bytes 393216 | tf_op jit(solution)/shard_map/all_gather | solution.py:368
  27.5 0.7 %value_product.1 = (f32[512,128]{1,0:T(8,128)S(1)}, bf16[512,128]{1,0:T(8,128)(2,1)S(1)}, bf16[512,128]{1,0:T(8,128)(2,1)S(1)}, bf16[512,128]{1,0:T(8,128)(2,1)S(1)}) custom-call(bf16[512,1024]{1,0:T(8,128)(2,1)S(1)} %get-tuple-element.47.tok, bf16[256,512]{1,0:T(8,128)(2,1)S(1)} %stack.1.refs_0_, bf16[512,512]{1,0:T(8,128)(2,1)S(1)} %all_gather.6.refs_1_, ...), custom_call_target="tpu_custom_call" | custom-call | tf_op jit(solution)/shard_map/value_product/pallas_call | solution.py:204
  28.2 2.5 %collective-permute-start.10 = (bf16[512,128]{1,0:T(8,128)(2,1)S(1)}, bf16[512,128]{1,0:T(8,128)(2,1)S(1)}, u32[]{:S(2)}, u32[]{:S(2)}) collective-permute-start(bf16[512,128]{1,0:T(8,128)(2,1)S(1)} %get-tuple-element.54), channel_id=1, source_target_pairs={{0,6},{2,4},{4,2},{6,0},{8,14},{10,12},{12,10},{14,8},{16,22},{18,... | collective-permute-start | bytes 393224 | tf_op jit(solution)/shard_map/ppermute | solution.py:331
  30.7 0.5 %collective-permute-start.11 = (bf16[512,128]{1,0:T(8,128)(2,1)S(1)}, bf16[512,128]{1,0:T(8,128)(2,1)S(1)}, u32[]{:S(2)}, u32[]{:S(2)}) collective-permute-start(bf16[512,128]{1,0:T(8,128)(2,1)S(1)} %get-tuple-element.55), channel_id=1, source_target_pairs={{0,2},{2,0},{4,6},{6,4},{8,10},{10,8},{12,14},{14,12},{16,18},{18,... | collective-permute-start | bytes 393224 | tf_op jit(solution)/shard_map/ppermute | solution.py:331
  31.3 0.0 collective-permute-done.13.refs_1_
  31.3 0.5 collective-permute-start.12
  31.8 0.0 collective-permute-done.14.refs_2_
  31.8 0.0 collective-permute-done.15.refs_3_
  31.8 0.3 score.1
  32.1 3.4 %collective-permute-done.10.refs_1_ = bf16[512,128]{1,0:T(8,128)(2,1)S(1)} collective-permute-done((bf16[512,128]{1,0:T(8,128)(2,1)S(1)}, bf16[512,128]{1,0:T(8,128)(2,1)S(1)}, u32[]{:S(2)}, u32[]{:S(2)}) %collective-permute-start.10) | collective-permute-done | bytes 131104 | tf_op jit(solution)/shard_map/ppermute | solution.py:331
  35.5 2.1 %collective-permute-done.11.refs_2_ = bf16[512,128]{1,0:T(8,128)(2,1)S(1)} collective-permute-done((bf16[512,128]{1,0:T(8,128)(2,1)S(1)}, bf16[512,128]{1,0:T(8,128)(2,1)S(1)}, u32[]{:S(2)}, u32[]{:S(2)}) %collective-permute-start.11) | collective-permute-done | bytes 131104 | tf_op jit(solution)/shard_map/ppermute | solution.py:331
  37.6 0.0 collective-permute-done.12.refs_3_
  37.6 0.2 state.1
  37.8 1.3 %collective-permute-start.16 = (bf16[128,128]{1,0:T(8,128)(2,1)S(1)}, bf16[128,128]{1,0:T(8,128)(2,1)S(1)}, u32[]{:S(2)}, u32[]{:S(2)}) collective-permute-start(bf16[128,128]{1,0:T(8,128)(2,1)S(1)} %get-tuple-element.65), channel_id=1, source_target_pairs={{8,16},{10,18},{12,20},{14,22},{9,17},{11,19},{13,21},{15,23}} | collective-permute-start | bytes 98312 | tf_op jit(solution)/shard_map/ppermute | solution.py:387
  39.1 0.2 within.1.inside
  39.4 0.0 copy-start
  39.4 4.3 %collective-permute-done.16.carried = bf16[128,128]{1,0:T(8,128)(2,1)S(1)} collective-permute-done((bf16[128,128]{1,0:T(8,128)(2,1)S(1)}, bf16[128,128]{1,0:T(8,128)(2,1)S(1)}, u32[]{:S(2)}, u32[]{:S(2)}) %collective-permute-start.16) | collective-permute-done | bytes 32800 | tf_op jit(solution)/shard_map/ppermute | solution.py:387
  43.6 0.0 copy-done
  43.7 0.3 finish.1
  44.0 2.4 %collective-permute-start.17 = (bf16[128,128]{1,0:T(8,128)(2,1)S(1)}, bf16[128,128]{1,0:T(8,128)(2,1)S(1)}, u32[]{:S(2)}, u32[]{:S(2)}) collective-permute-start(bf16[128,128]{1,0:T(8,128)(2,1)S(1)} %get-tuple-element.70), channel_id=1, source_target_pairs={{0,6},{2,4},{4,2},{6,0},{8,14},{10,12},{12,10},{14,8},{16,22},{18,... | collective-permute-start | bytes 98312 | tf_op jit(solution)/shard_map/ppermute | solution.py:331
  46.4 0.5 %collective-permute-start.18 = (bf16[128,128]{1,0:T(8,128)(2,1)S(1)}, bf16[128,128]{1,0:T(8,128)(2,1)S(1)}, u32[]{:S(2)}, u32[]{:S(2)}) collective-permute-start(bf16[128,128]{1,0:T(8,128)(2,1)S(1)} %get-tuple-element.71), channel_id=1, source_target_pairs={{0,2},{2,0},{4,6},{6,4},{8,10},{10,8},{12,14},{14,12},{16,18},{18,... | collective-permute-start | bytes 98312 | tf_op jit(solution)/shard_map/ppermute | solution.py:331
  46.9 0.6 %collective-permute-start.19 = (bf16[128,128]{1,0:T(8,128)(2,1)S(1)}, bf16[128,128]{1,0:T(8,128)(2,1)S(1)}, u32[]{:S(2)}, u32[]{:S(2)}) collective-permute-start(bf16[128,128]{1,0:T(8,128)(2,1)S(1)} %get-tuple-element.72), channel_id=1, source_target_pairs={{0,4},{2,6},{4,0},{6,2},{8,12},{10,14},{12,8},{14,10},{16,20},{18,... | collective-permute-start | bytes 98312 | tf_op jit(solution)/shard_map/ppermute | solution.py:331
  47.5 1.3 %collective-permute-done.17.refs_1_ = bf16[128,128]{1,0:T(8,128)(2,1)S(1)} collective-permute-done((bf16[128,128]{1,0:T(8,128)(2,1)S(1)}, bf16[128,128]{1,0:T(8,128)(2,1)S(1)}, u32[]{:S(2)}, u32[]{:S(2)}) %collective-permute-start.17) | collective-permute-done | bytes 32800 | tf_op jit(solution)/shard_map/ppermute | solution.py:331
  48.8 1.5 %collective-permute-done.18.refs_2_ = bf16[128,128]{1,0:T(8,128)(2,1)S(1)} collective-permute-done((bf16[128,128]{1,0:T(8,128)(2,1)S(1)}, bf16[128,128]{1,0:T(8,128)(2,1)S(1)}, u32[]{:S(2)}, u32[]{:S(2)}) %collective-permute-start.18) | collective-permute-done | bytes 32800 | tf_op jit(solution)/shard_map/ppermute | solution.py:331
  50.3 0.5 %collective-permute-done.19.refs_3_ = bf16[128,128]{1,0:T(8,128)(2,1)S(1)} collective-permute-done((bf16[128,128]{1,0:T(8,128)(2,1)S(1)}, bf16[128,128]{1,0:T(8,128)(2,1)S(1)}, u32[]{:S(2)}, u32[]{:S(2)}) %collective-permute-start.19) | collective-permute-done | bytes 32800 | tf_op jit(solution)/shard_map/ppermute | solution.py:331
  50.9 0.7 %join.1 = bf16[128,512]{1,0:T(8,128)(2,1)} custom-call(bf16[128,128]{1,0:T(8,128)(2,1)S(1)} %get-tuple-element.69.refs_0_, bf16[128,128]{1,0:T(8,128)(2,1)S(1)} %collective-permute-done.17.refs_1_, bf16[128,128]{1,0:T(8,128)(2,1)S(1)} %collective-permute-done.18.refs_2_, bf16[128,128]{1,0:T(8,128)(2,1)S(1)} %collective-permute-done.19.refs_3_), custom_call_target="tpu_custom_call" | custom-call | tf_op jit(solution)/shard_map/join/pallas_call | solution.py:316
  (1 shorter events, 0.0 us)
Async XLA Ops:
  1.0 13.7 %collective-permute-start.3 = (bf16[256,512]{1,0:T(8,128)(2,1)S(1)}, bf16[256,512]{1,0:T(8,128)(2,1)S(1)}, u32[]{:S(2)}, u32[]{:S(2)}) collective-permute-start(bf16[256,512]{1,0:T(8,128)(2,1)S(1)} %stack.1.refs_0_), channel_id=1, source_target_pairs={{0,24},{2,26},{4,28},{6,30},{8,16},{10,18},{12,20},{14,22},{16,8},... | collective-permute-start | bytes 786440 | tf_op jit(solution)/shard_map/ppermute | solution.py:331
  2.9 12.9 %collective-permute-start = (bf16[1168,128]{1,0:T(8,128)(2,1)S(1)}, bf16[1168,128]{1,0:T(8,128)(2,1)S(1)}, u32[]{:S(2)}, u32[]{:S(2)}) collective-permute-start(bf16[1168,128]{1,0:T(8,128)(2,1)S(1)} %get-tuple-element.44), channel_id=1, source_target_pairs={{0,6},{2,4},{4,2},{6,0},{8,14},{10,12},{12,10},{14,8},{16,22},{18,... | collective-permute-start | bytes 897032 | tf_op jit(solution)/shard_map/ppermute | solution.py:331
  5.4 13.5 %collective-permute-start.1 = (bf16[1168,128]{1,0:T(8,128)(2,1)S(1)}, bf16[1168,128]{1,0:T(8,128)(2,1)S(1)}, u32[]{:S(2)}, u32[]{:S(2)}) collective-permute-start(bf16[1168,128]{1,0:T(8,128)(2,1)S(1)} %get-tuple-element.45), channel_id=1, source_target_pairs={{0,2},{2,0},{4,6},{6,4},{8,10},{10,8},{12,14},{14,12},{16,18},{18,... | collective-permute-start | bytes 897032 | tf_op jit(solution)/shard_map/ppermute | solution.py:331
  6.0 13.9 %collective-permute-start.2 = (bf16[1168,128]{1,0:T(8,128)(2,1)S(1)}, bf16[1168,128]{1,0:T(8,128)(2,1)S(1)}, u32[]{:S(2)}, u32[]{:S(2)}) collective-permute-start(bf16[1168,128]{1,0:T(8,128)(2,1)S(1)} %get-tuple-element.46), channel_id=1, source_target_pairs={{0,4},{2,6},{4,0},{6,2},{8,12},{10,14},{12,8},{14,10},{16,20},{18,... | collective-permute-start | bytes 897032 | tf_op jit(solution)/shard_map/ppermute | solution.py:331
  6.5 9.3 %collective-permute-start.4 = (bf16[256,512]{1,0:T(8,128)(2,1)S(1)}, bf16[256,512]{1,0:T(8,128)(2,1)S(1)}, u32[]{:S(2)}, u32[]{:S(2)}) collective-permute-start(bf16[256,512]{1,0:T(8,128)(2,1)S(1)} %stack.1.refs_0_), channel_id=1, source_target_pairs={{0,8},{2,10},{4,12},{6,14},{8,0},{10,2},{12,4},{14,6},{16,24},{18,... | collective-permute-start | bytes 786440 | tf_op jit(solution)/shard_map/ppermute | solution.py:331
  14.7 5.1 %collective-permute-start.7 = (bf16[128,512]{1,0:T(8,128)(2,1)S(1)}, bf16[128,512]{1,0:T(8,128)(2,1)S(1)}, u32[]{:S(2)}, u32[]{:S(2)}) collective-permute-start(bf16[128,512]{1,0:T(8,128)(2,1)S(1)} %get-tuple-element.73), channel_id=1, source_target_pairs={{0,8},{2,10},{4,12},{6,14},{8,0},{10,2},{12,4},{14,6},{16,24},{18,... | collective-permute-start | bytes 393224 | tf_op jit(solution)/shard_map/ppermute | solution.py:331
  15.8 5.4 %collective-permute-start.9 = (bf16[256,512]{1,0:T(8,128)(2,1)S(1)}, bf16[256,512]{1,0:T(8,128)(2,1)S(1)}, u32[]{:S(2)}, u32[]{:S(2)}) collective-permute-start(bf16[256,512]{1,0:T(8,128)(2,1)S(1)} %collective-permute-done.3.refs_6_), channel_id=1, source_target_pairs={{0,1},{1,0},{2,3},{3,2},{4,5},{5,4},{6,7},{7,6},{8,9},{9,8},{10,11... | collective-permute-start | bytes 786440 | tf_op jit(solution)/shard_map/ppermute | solution.py:337
  15.8 9.7 %collective-permute-start.6 = (bf16[128,512]{1,0:T(8,128)(2,1)S(1)}, bf16[128,512]{1,0:T(8,128)(2,1)S(1)}, u32[]{:S(2)}, u32[]{:S(2)}) collective-permute-start(bf16[128,512]{1,0:T(8,128)(2,1)S(1)} %get-tuple-element.74), channel_id=1, source_target_pairs={{0,8},{2,10},{4,12},{6,14},{8,0},{10,2},{12,4},{14,6},{16,24},{18,... | collective-permute-start | bytes 393224 | tf_op jit(solution)/shard_map/ppermute | solution.py:331
  18.9 1.5 %collective-permute-start.5 = (bf16[256,512]{1,0:T(8,128)(2,1)S(1)}, bf16[256,512]{1,0:T(8,128)(2,1)S(1)}, u32[]{:S(2)}, u32[]{:S(2)}) collective-permute-start(bf16[256,512]{1,0:T(8,128)(2,1)S(1)} %collective-permute-done.4.refs_2_), channel_id=1, source_target_pairs={{0,1},{1,0},{2,3},{3,2},{4,5},{5,4},{6,7},{7,6},{8,9},{9,8},{10,11... | collective-permute-start | bytes 786440 | tf_op jit(solution)/shard_map/ppermute | solution.py:337
  19.9 1.3 %collective-permute-start.8 = (bf16[128,512]{1,0:T(8,128)(2,1)S(1)}, bf16[128,512]{1,0:T(8,128)(2,1)S(1)}, u32[]{:S(2)}, u32[]{:S(2)}) collective-permute-start(bf16[128,512]{1,0:T(8,128)(2,1)S(1)} %collective-permute-done.7.refs_4_), channel_id=1, source_target_pairs={{0,1},{1,0},{2,3},{3,2},{4,5},{5,4},{6,7},{7,6},{8,9},{9,8},{10,11... | collective-permute-start | bytes 393224 | tf_op jit(solution)/shard_map/ppermute | solution.py:337
  21.9 9.3 %collective-permute-start.13 = (bf16[512,128]{1,0:T(8,128)(2,1)S(1)}, bf16[512,128]{1,0:T(8,128)(2,1)S(1)}, u32[]{:S(2)}, u32[]{:S(2)}) collective-permute-start(bf16[512,128]{1,0:T(8,128)(2,1)S(1)} %get-tuple-element.58), channel_id=1, source_target_pairs={{0,6},{2,4},{4,2},{6,0},{8,14},{10,12},{12,10},{14,8},{16,22},{18,... | collective-permute-start | bytes 393224 | tf_op jit(solution)/shard_map/ppermute | solution.py:331
  24.4 7.3 %collective-permute-start.14 = (bf16[512,128]{1,0:T(8,128)(2,1)S(1)}, bf16[512,128]{1,0:T(8,128)(2,1)S(1)}, u32[]{:S(2)}, u32[]{:S(2)}) collective-permute-start(bf16[512,128]{1,0:T(8,128)(2,1)S(1)} %get-tuple-element.59), channel_id=1, source_target_pairs={{0,2},{2,0},{4,6},{6,4},{8,10},{10,8},{12,14},{14,12},{16,18},{18,... | collective-permute-start | bytes 393224 | tf_op jit(solution)/shard_map/ppermute | solution.py:331
  25.0 6.8 %collective-permute-start.15 = (bf16[512,128]{1,0:T(8,128)(2,1)S(1)}, bf16[512,128]{1,0:T(8,128)(2,1)S(1)}, u32[]{:S(2)}, u32[]{:S(2)}) collective-permute-start(bf16[512,128]{1,0:T(8,128)(2,1)S(1)} %get-tuple-element.60), channel_id=1, source_target_pairs={{0,4},{2,6},{4,0},{6,2},{8,12},{10,14},{12,8},{14,10},{16,20},{18,... | collective-permute-start | bytes 393224 | tf_op jit(solution)/shard_map/ppermute | solution.py:331
  28.2 7.3 %collective-permute-start.10 = (bf16[512,128]{1,0:T(8,128)(2,1)S(1)}, bf16[512,128]{1,0:T(8,128)(2,1)S(1)}, u32[]{:S(2)}, u32[]{:S(2)}) collective-permute-start(bf16[512,128]{1,0:T(8,128)(2,1)S(1)} %get-tuple-element.54), channel_id=1, source_target_pairs={{0,6},{2,4},{4,2},{6,0},{8,14},{10,12},{12,10},{14,8},{16,22},{18,... | collective-permute-start | bytes 393224 | tf_op jit(solution)/shard_map/ppermute | solution.py:331
  30.7 6.9 %collective-permute-start.11 = (bf16[512,128]{1,0:T(8,128)(2,1)S(1)}, bf16[512,128]{1,0:T(8,128)(2,1)S(1)}, u32[]{:S(2)}, u32[]{:S(2)}) collective-permute-start(bf16[512,128]{1,0:T(8,128)(2,1)S(1)} %get-tuple-element.55), channel_id=1, source_target_pairs={{0,2},{2,0},{4,6},{6,4},{8,10},{10,8},{12,14},{14,12},{16,18},{18,... | collective-permute-start | bytes 393224 | tf_op jit(solution)/shard_map/ppermute | solution.py:331
  31.3 6.3 %collective-permute-start.12 = (bf16[512,128]{1,0:T(8,128)(2,1)S(1)}, bf16[512,128]{1,0:T(8,128)(2,1)S(1)}, u32[]{:S(2)}, u32[]{:S(2)}) collective-permute-start(bf16[512,128]{1,0:T(8,128)(2,1)S(1)} %get-tuple-element.56), channel_id=1, source_target_pairs={{0,4},{2,6},{4,0},{6,2},{8,12},{10,14},{12,8},{14,10},{16,20},{18,... | collective-permute-start | bytes 393224 | tf_op jit(solution)/shard_map/ppermute | solution.py:331
  37.8 5.8 %collective-permute-start.16 = (bf16[128,128]{1,0:T(8,128)(2,1)S(1)}, bf16[128,128]{1,0:T(8,128)(2,1)S(1)}, u32[]{:S(2)}, u32[]{:S(2)}) collective-permute-start(bf16[128,128]{1,0:T(8,128)(2,1)S(1)} %get-tuple-element.65), channel_id=1, source_target_pairs={{8,16},{10,18},{12,20},{14,22},{9,17},{11,19},{13,21},{15,23}} | collective-permute-start | bytes 98312 | tf_op jit(solution)/shard_map/ppermute | solution.py:387
  39.4 4.3 %copy-start = (f32[512]{0:T(512)S(1)}, f32[512]{0:T(512)}, u32[]{:S(2)}) copy-start(f32[512]{0:T(512)} %param.11) | copy-start | bytes 6148
  44.0 4.9 %collective-permute-start.17 = (bf16[128,128]{1,0:T(8,128)(2,1)S(1)}, bf16[128,128]{1,0:T(8,128)(2,1)S(1)}, u32[]{:S(2)}, u32[]{:S(2)}) collective-permute-start(bf16[128,128]{1,0:T(8,128)(2,1)S(1)} %get-tuple-element.70), channel_id=1, source_target_pairs={{0,6},{2,4},{4,2},{6,0},{8,14},{10,12},{12,10},{14,8},{16,22},{18,... | collective-permute-start | bytes 98312 | tf_op jit(solution)/shard_map/ppermute | solution.py:331
  46.4 3.9 %collective-permute-start.18 = (bf16[128,128]{1,0:T(8,128)(2,1)S(1)}, bf16[128,128]{1,0:T(8,128)(2,1)S(1)}, u32[]{:S(2)}, u32[]{:S(2)}) collective-permute-start(bf16[128,128]{1,0:T(8,128)(2,1)S(1)} %get-tuple-element.71), channel_id=1, source_target_pairs={{0,2},{2,0},{4,6},{6,4},{8,10},{10,8},{12,14},{14,12},{16,18},{18,... | collective-permute-start | bytes 98312 | tf_op jit(solution)/shard_map/ppermute | solution.py:331
  46.9 3.9 %collective-permute-start.19 = (bf16[128,128]{1,0:T(8,128)(2,1)S(1)}, bf16[128,128]{1,0:T(8,128)(2,1)S(1)}, u32[]{:S(2)}, u32[]{:S(2)}) collective-permute-start(bf16[128,128]{1,0:T(8,128)(2,1)S(1)} %get-tuple-element.72), channel_id=1, source_target_pairs={{0,4},{2,6},{4,0},{6,2},{8,12},{10,14},{12,8},{14,10},{16,20},{18,... | collective-permute-start | bytes 98312 | tf_op jit(solution)/shard_map/ppermute | solution.py:331
